TPU v7x, 128 devices: a whole 4x4x4 slice. The times are simulated.
128 devices in a mesh: gx: 8 (over z, y_hi), gy: 16 (over x, y_lo, core).
Axes of the slice: x: 4, y: 4 (y_hi: 2, y_lo: 2; y = y_hi * 2 + y_lo), z: 4, core: 2. Of those that a mesh axis runs over, the one named last changes fastest.
Arguments:
- les_wind: float32 [2, 8, 256, 1024], P(None, None, ('gx', 'gy')), may hold values from -0.4 to 0.4
- les_temp: float32 [8, 256, 1024], P(None, ('gx', 'gy')), may hold values from 0.8 to 1.25
- acoustic_start: float32 [3, 8, 512, 2048], P(None, None, 'gx', 'gy'), may hold values from -6 to 6
Outputs:
- acoustic_end: float32 [3, 8, 512, 2048], P(None, None, 'gx', 'gy')
All inputs are finite; a program needn't handle non-finite values.
Results may differ from a plain program's by a relative error of at most 0.00013.
Values sent between devices are 32-bit elements; how exact they have to be, the bound alone decides.
No kernel may reach another device: no remote copies, remote signals or barrier semaphores. Data moves between devices by JAX's collectives and lax.ppermute only.
A program may use at most 128 MiB of HBM per device.

v0:
```python
import functools

import jax
import jax.numpy as jnp
import ml_dtypes
import numpy as np
from jax import lax
from jax.experimental import pallas as pl
from jax.experimental.pallas import tpu as pltpu
from jax.sharding import PartitionSpec as P

STEPS = 3
STAGES = 3 * STEPS
REACH = 2 * STAGES
LEVELS = 8
ROWS = 64
COLS = 128
EXT = ROWS + 2 * REACH
MARGIN = REACH // 2 + 1
CROWS = ROWS // 2
WINDOW = COLS // 2 + 2 * MARGIN
HALF = WINDOW // 2
RIGHT = 3 * REACH
RIM = 6 * REACH
EDGE = REACH // 3
MIDDLE = (ROWS - 2 * REACH) // 7
SIDE = EDGE + MIDDLE

time_step = 0.4
scale = time_step / 12.0

F32 = jnp.float32


def lanes():
    return lax.broadcasted_iota(jnp.int32, (LEVELS, COLS), 1)


def parity(axis):
    return lax.rem(lax.axis_index(axis), 2)


def swap_near(values, axis):
    return lax.ppermute(values, axis, [(i, i ^ 1) for i in range(lax.axis_size(axis))])


def swap_far(values, axis):
    count = lax.axis_size(axis)
    return lax.ppermute(
        values, axis, [(i, (i + 1) % count if i % 2 else (i - 1) % count) for i in range(count)]
    )


def roll(values, shift):
    if isinstance(shift, int):
        shift = shift % COLS
        if shift == 0:
            return values
    return pltpu.roll(values, shift, values.ndim - 1)


def slots():
    pieces = []
    for k in range(3):
        pieces.append((EDGE * k, EDGE, 0, k))
        pieces.append((ROWS - REACH + EDGE * k, EDGE, 0, 3 + k))
    for k in range(7):
        pieces.append((REACH + MIDDLE * k, MIDDLE, EDGE, k))
    return pieces


def coarse_pack_kernel(wind_ref, temp_ref, out_ref):
    lane = lanes()
    blocks = wind_ref.shape[-1] // COLS

    def windows(values):
        parts = [values[:, COLS * i : COLS * (i + 1)] for i in range(blocks)]
        near = [roll(part, MARGIN) for part in parts]
        far = [roll(part, COLS // 2 + MARGIN) for part in parts]
        result = []
        for i in range(blocks):
            result.append(jnp.where(lane < MARGIN, near[i - 1], near[i]))
            result.append(jnp.where(lane < COLS // 2 + MARGIN, far[i], far[(i + 1) % blocks]))
        return result

    for row in range(2):
        east = windows(wind_ref[0, :, row, :])
        north = windows(wind_ref[1, :, row, :])
        warm = windows(temp_ref[:, row, :])
        for j in range(2 * blocks):
            out_ref[j, row, 0] = jnp.where(lane < WINDOW, east[j], roll(warm[j], WINDOW))
            out_ref[j, row, 1] = jnp.where(lane < WINDOW, north[j], roll(warm[j], HALF))


def acoustic_pack_kernel(start_ref, tile_ref, x_near_ref, x_far_ref, y_near_ref, y_far_ref):
    x_odd, y_odd = parity("gx"), parity("gy")
    for f in range(3):
        for row in range(ROWS):
            tile_ref[f, row] = start_ref[pl.ds(f * LEVELS * ROWS + row, LEVELS, stride=ROWS), :]
    x_near_ref[...] = tile_ref[:, pl.ds((1 - x_odd) * (ROWS - REACH), REACH)]
    x_far_ref[...] = tile_ref[:, pl.ds(x_odd * (ROWS - REACH), REACH)]
    lane = lanes()
    for ref, first in (
        (y_near_ref, (1 - y_odd) * (COLS - REACH)),
        (y_far_ref, y_odd * (COLS - REACH)),
    ):
        for f in range(3):
            for group, size, base in ((0, EDGE, 0), (1, MIDDLE, EDGE)):
                packed = None
                for row, count, register, slot in slots():
                    if register != base:
                        continue
                    shift = lax.rem(REACH * slot - first + COLS, COLS)
                    moved = roll(tile_ref[f, row : row + count], shift)
                    if packed is None:
                        packed = moved
                    else:
                        inside = (lane >= REACH * slot) & (lane < REACH * (slot + 1))
                        packed = jnp.where(inside, moved, packed)
                ref[f, base : base + size] = packed


def second_pack_kernel(coarse_ref, y_near_ref, y_far_ref, x_near_ref, x_far_ref):
    x_odd, y_odd = parity("gx"), parity("gy")
    lane = lanes()
    width = 3 * REACH
    for ref, bottom in ((x_near_ref, 1 - x_odd), (x_far_ref, x_odd)):
        first = bottom * (CROWS - MARGIN)
        for i in range(MARGIN):
            for c in range(2):
                ref[2 * i + c] = coarse_ref[first + i, c]
        for f in range(3):
            for t in range(EDGE):
                start = bottom * width
                near = roll(y_near_ref[f, t], lax.rem((1 - y_odd) * width - start + COLS, COLS))
                far = roll(y_far_ref[f, t], lax.rem(y_odd * width - start + COLS, COLS))
                take_near = (lane >= width).astype(jnp.int32) == 1 - y_odd
                ref[2 * MARGIN + EDGE * f + t] = jnp.where(take_near, near, far)


def rim_of(main, left, right, lane):
    own = jnp.where(lane < RIGHT, roll(main, REACH), roll(main, RIGHT - (COLS - 2 * REACH)))
    own = jnp.where(lane < REACH, left, own)
    return jnp.where(lane >= RIM - REACH, right, own)


def step_rows(src, base, dst, background, c, r, count, stage):
    dx, dy, mid = [], [], []
    for f in range(3):
        block = src[c, f, pl.ds(r - 2, count + 4)]
        centre = block[2 : 2 + count]
        dx.append(8.0 * (block[3 : 3 + count] - block[1 : 1 + count]) - (block[4:] - block[:count]))
        dy.append(8.0 * (roll(centre, -1) - roll(centre, 1)) - (roll(centre, -2) - roll(centre, 2)))
        mid.append(centre)
    east = background[c, 0, pl.ds(r, count)]
    north = background[c, 1, pl.ds(r, count)]
    warm = background[c, 2, pl.ds(r, count)]
    change = (
        east * dx[0] + north * dy[0] + scale * (dx[1] + dy[2]),
        east * dx[1] + north * dy[1] + warm * dx[0],
        east * dx[2] + north * dy[2] + warm * dy[0],
    )
    for f in range(3):
        moved = mid[f] - change[f]
        if stage == 1:
            moved = 0.75 * base[c, f, pl.ds(r, count)] + 0.25 * moved
        elif stage == 2:
            moved = (1.0 / 3.0) * base[c, f, pl.ds(r, count)] + (2.0 / 3.0) * moved
        dst[c, f, pl.ds(r, count)] = moved


def solve_kernel(
    coarse_ref, tile_ref, y_near_ref, y_far_ref, x_near_ref, x_far_ref, s_near_ref, s_far_ref,
    east_table_ref, north_table_ref, out_ref, coarse, refined, background, state, first, second,
):
    x_odd, y_odd = parity("gx"), parity("gy")
    lane = lanes()
    coarse[MARGIN : MARGIN + CROWS] = coarse_ref[...]
    for ref, high in ((s_near_ref, 1 - x_odd), (s_far_ref, x_odd)):
        start = high * (MARGIN + CROWS)
        for i in range(MARGIN):
            for c in range(2):
                coarse[start + i, c] = ref[2 * i + c]

    @pl.loop(0, (CROWS + 2 * MARGIN) // 4)
    def _(step):
        m = step * 4
        products = []
        for c, table in ((0, east_table_ref), (1, north_table_ref)):
            values = coarse[pl.ds(m, 4), c].reshape(4 * LEVELS, COLS)
            high = values.astype(jnp.bfloat16)
            low = (values - high.astype(F32)).astype(jnp.bfloat16)
            both = jnp.concatenate((high, low), axis=1)
            products.append(jnp.dot(both, table[...], preferred_element_type=F32))
        warm = products[0][:, 2 * COLS :] + products[1][:, 2 * COLS :]
        for k in range(2):
            cut = slice(COLS * k, COLS * (k + 1))
            refined[k, 0, pl.ds(m, 4)] = products[0][:, cut].reshape(4, LEVELS, COLS)
            refined[k, 1, pl.ds(m, 4)] = products[1][:, cut].reshape(4, LEVELS, COLS)
            refined[k, 2, pl.ds(m, 4)] = warm[:, cut].reshape(4, LEVELS, COLS)

    @pl.loop(1, CROWS + 2 * MARGIN - 1)
    def _(m):
        for k in range(2):
            for f in range(3):
                block = refined[k, f, pl.ds(m - 1, 3)]
                centre = (0.75 * scale) * block[1]
                background[k, f, 2 * m - 2] = centre + (0.25 * scale) * block[0]
                background[k, f, 2 * m - 1] = centre + (0.25 * scale) * block[2]

    state[0, :, REACH : REACH + ROWS] = tile_ref[...]
    for row, count, register, slot in slots():
        take_near = (lane >= RIGHT).astype(jnp.int32) == 1 - y_odd
        for f in range(3):
            near = y_near_ref[f, register : register + count]
            far = y_far_ref[f, register : register + count]
            near = roll(near, lax.rem((1 - y_odd) * (RIM - REACH) - REACH * slot + COLS, COLS))
            far = roll(far, lax.rem(y_odd * (RIM - REACH) - REACH * slot + COLS, COLS))
            halo = jnp.where(take_near, near, far)
            main = tile_ref[f, row : row + count]
            state[1, f, REACH + row : REACH + row + count] = rim_of(main, halo, halo, lane)
    for main_ref, ref, high in ((x_near_ref, s_near_ref, 1 - x_odd), (x_far_ref, s_far_ref, x_odd)):
        start = high * (REACH + ROWS)
        state[0, :, pl.ds(start, REACH)] = main_ref[...]
        for f in range(3):
            corners = ref[2 * MARGIN + EDGE * f : 2 * MARGIN + EDGE * (f + 1)]
            for k in range(3):
                main = main_ref[f, EDGE * k : EDGE * (k + 1)]
                left = roll(corners, -REACH * k)
                right = roll(corners, RIM - REACH - RIGHT - REACH * k)
                state[1, f, pl.ds(start + EDGE * k, EDGE)] = rim_of(main, left, right, lane)

    buffers = (state, first, second, state)
    for step in range(STAGES):
        stage = step % 3
        low, top = 2 * (step + 1), EXT - 2 * (step + 1)

        @pl.loop(0, (top - low) // 4)
        def _(i):
            for c in range(2):
                step_rows(
                    buffers[stage], state, buffers[stage + 1], background, c, low + 4 * i, 4, stage
                )

    for f in range(3):

        @pl.loop(0, ROWS)
        def _(row):
            main = state[0, f, REACH + row]
            rim = state[1, f, REACH + row]
            value = jnp.where(lane < REACH, roll(rim, -REACH), main)
            value = jnp.where(lane >= COLS - REACH, roll(rim, COLS - 2 * REACH - RIGHT), value)
            out_ref[pl.ds(f * LEVELS * ROWS + row, LEVELS, stride=ROWS), :] = value


def tables():
    columns = np.full((2 * COLS,), -1000)
    columns[:COLS] = np.arange(COLS)
    columns[COLS : COLS + RIGHT] = np.arange(RIGHT) - REACH
    columns[COLS + RIGHT : COLS + RIM] = np.arange(RIGHT) + COLS - 2 * REACH
    window = np.zeros((WINDOW, 2 * COLS), np.float32)
    for j, column in enumerate(columns):
        if column > -1000:
            centre = column // 2 + MARGIN
            window[centre, j] = 0.75
            window[centre - 1 + 2 * (column % 2), j] = 0.25
    pair = []
    for part in (window[:HALF], window[HALF:]):
        table = np.zeros((COLS, 4 * COLS), np.float32)
        table[:WINDOW, : 2 * COLS] = window
        table[WINDOW : WINDOW + HALF, 2 * COLS :] = part
        pair.append(np.concatenate((table, table), axis=0).astype(ml_dtypes.bfloat16))
    return pair


def call(kernel, outputs, scratch=(), limit=48):
    return pl.pallas_call(
        kernel,
        out_shape=[jax.ShapeDtypeStruct(shape, F32) for shape in outputs],
        scratch_shapes=[pltpu.VMEM(shape, F32) for shape in scratch],
        compiler_params=pltpu.CompilerParams(vmem_limit_bytes=limit * 2**20),
    )


def local(les_wind, les_temp, acoustic_start):
    block = (LEVELS, COLS)
    groups = lax.axis_size("gy")
    (packed,) = call(coarse_pack_kernel, [(groups, 2, 2) + block])(les_wind, les_temp)
    coarse = lax.all_to_all(packed, "gy", split_axis=0, concat_axis=0, tiled=True)
    coarse = coarse.reshape((CROWS, 2) + block)
    tile, x_near, x_far, y_near, y_far = call(
        acoustic_pack_kernel,
        [(3, ROWS) + block] + 2 * [(3, REACH) + block] + 2 * [(3, SIDE) + block],
    )(acoustic_start.reshape(3 * LEVELS * ROWS, COLS))
    y_near, y_far = swap_near(y_near, "gy"), swap_far(y_far, "gy")
    x_near, x_far = swap_near(x_near, "gx"), swap_far(x_far, "gx")
    s_near, s_far = call(second_pack_kernel, 2 * [(2 * MARGIN + 3 * EDGE,) + block])(
        coarse, y_near, y_far
    )
    s_near, s_far = swap_near(s_near, "gx"), swap_far(s_far, "gx")
    east_table, north_table = tables()
    (end,) = call(
        solve_kernel,
        [(3 * LEVELS * ROWS, COLS)],
        scratch=[(CROWS + 2 * MARGIN, 2) + block, (2, 3, CROWS + 2 * MARGIN) + block]
        + 4 * [(2, 3, EXT) + block],
    )(
        coarse, tile, y_near, y_far, x_near, x_far, s_near, s_far,
        jnp.asarray(east_table), jnp.asarray(north_table),
    )
    return end.reshape(acoustic_start.shape)


def solution(mesh):
    in_specs = (
        P(None, None, ("gx", "gy"), None),
        P(None, ("gx", "gy"), None),
        P(None, None, "gx", "gy"),
    )
    out_specs = P(None, None, "gx", "gy")
    return jax.shard_map(local, mesh=mesh, in_specs=in_specs, out_specs=out_specs, check_vma=False)
```

profile of v0, /device:TPU:1, one launch (start us, length us, event | category | flops | bytes accessed | tf_op | source)
XLA Modules:
  0.0 91.2 jit_solution(6087837285395509300)
XLA Ops:
  0.0 0.9 copy-done.3
  0.9 0.8 copy-done.4
  1.7 1.0 %shard_map.55 = f32[16,2,2,8,128]{4,3,2,1,0:T(8,128)} custom-call(f32[2,8,2,1024]{3,2,1,0:T(2,128)S(1)} %copy-done.3, f32[8,2,1024]{2,1,0:T(2,128)S(1)} %copy-done.4), custom_call_target="tpu_custom_call" | custom-call | tf_op jit(solution)/shard_map/pallas_call | solution.py:288
  2.8 6.8 %all-to-all-start = ((f32[16,2,2,8,128]{4,3,2,1,0:T(8,128)}), f32[16,2,2,8,128]{4,3,2,1,0:T(8,128)S(1)}, u32[]{:S(2)}, u32[]{:S(2)}) async-start(f32[16,2,2,8,128]{4,3,2,1,0:T(8,128)} %shard_map.55), calls=%async_computation | async-start | bytes 524288 | tf_op jit(solution)/shard_map/all_to_all | solution.py:289
  9.6 0.0 copy-done
  9.6 0.0 copy-start.2
  9.6 0.8 shard_map.56
  10.5 0.0 copy-start.1
  10.5 0.2 collective-permute-start
  10.7 1.7 %collective-permute-start.1 = (f32[3,10,8,128]{3,2,1,0:T(8,128)S(1)}, f32[3,10,8,128]{3,2,1,0:T(8,128)S(1)}, u32[]{:S(2)}, u32[]{:S(2)}) collective-permute-start(f32[3,10,8,128]{3,2,1,0:T(8,128)S(1)} %get-tuple-element.14), channel_id=1, source_target_pairs={{0,15},{1,2},{2,1},{3,4},{4,3},{5,6},{6,5},{7,8},{8,7},{9,10},{10,... | collective-permute-start | bytes 368648 | tf_op jit(solution)/shard_map/ppermute | solution.py:49
  12.3 2.6 %collective-permute-start.2 = (f32[3,18,8,128]{3,2,1,0:T(8,128)S(1)}, f32[3,18,8,128]{3,2,1,0:T(8,128)S(1)}, u32[]{:S(2)}, u32[]{:S(2)}) collective-permute-start(f32[3,18,8,128]{3,2,1,0:T(8,128)S(1)} %get-tuple-element.15), channel_id=1, source_target_pairs={{0,16},{16,0},{32,48},{48,32},{64,80},{80,64},{96,112},{112,96},{1... | collective-permute-start | bytes 663560 | tf_op jit(solution)/shard_map/ppermute | solution.py:44
  15.0 3.8 %collective-permute-start.3 = (f32[3,18,8,128]{3,2,1,0:T(8,128)S(1)}, f32[3,18,8,128]{3,2,1,0:T(8,128)S(1)}, u32[]{:S(2)}, u32[]{:S(2)}) collective-permute-start(f32[3,18,8,128]{3,2,1,0:T(8,128)S(1)} %get-tuple-element.16), channel_id=1, source_target_pairs={{0,112},{16,32},{32,16},{48,64},{64,48},{80,96},{96,80},{112,0},{1... | collective-permute-start | bytes 663560 | tf_op jit(solution)/shard_map/ppermute | solution.py:49
  18.8 0.0 collective-permute-done.y_near_ref
  18.8 0.0 collective-permute-done.1.y_far_ref
  18.8 0.0 all-to-all-done
  18.8 0.2 shard_map.57
  19.0 2.6 %collective-permute-start.4 = (f32[38,8,128]{2,1,0:T(8,128)S(1)}, f32[38,8,128]{2,1,0:T(8,128)S(1)}, u32[]{:S(2)}, u32[]{:S(2)}) collective-permute-start(f32[38,8,128]{2,1,0:T(8,128)S(1)} %get-tuple-element.17), channel_id=1, source_target_pairs={{0,16},{16,0},{32,48},{48,32},{64,80},{80,64},{96,112},{112,96},{1... | collective-permute-start | bytes 466952 | tf_op jit(solution)/shard_map/ppermute | solution.py:44
  21.6 3.6 %collective-permute-start.5 = (f32[38,8,128]{2,1,0:T(8,128)S(1)}, f32[38,8,128]{2,1,0:T(8,128)S(1)}, u32[]{:S(2)}, u32[]{:S(2)}) collective-permute-start(f32[38,8,128]{2,1,0:T(8,128)S(1)} %get-tuple-element.18), channel_id=1, source_target_pairs={{0,112},{16,32},{32,16},{48,64},{64,48},{80,96},{96,80},{112,0},{1... | collective-permute-start | bytes 466952 | tf_op jit(solution)/shard_map/ppermute | solution.py:49
  25.1 1.1 %collective-permute-done.2.x_near_ref = f32[3,18,8,128]{3,2,1,0:T(8,128)S(1)} collective-permute-done((f32[3,18,8,128]{3,2,1,0:T(8,128)S(1)}, f32[3,18,8,128]{3,2,1,0:T(8,128)S(1)}, u32[]{:S(2)}, u32[]{:S(2)}) %collective-permute-start.2) | collective-permute-done | bytes 221216 | tf_op jit(solution)/shard_map/ppermute | solution.py:44
  26.2 8.2 %collective-permute-done.3.x_far_ref = f32[3,18,8,128]{3,2,1,0:T(8,128)S(1)} collective-permute-done((f32[3,18,8,128]{3,2,1,0:T(8,128)S(1)}, f32[3,18,8,128]{3,2,1,0:T(8,128)S(1)}, u32[]{:S(2)}, u32[]{:S(2)}) %collective-permute-start.3) | collective-permute-done | bytes 221216 | tf_op jit(solution)/shard_map/ppermute | solution.py:49
  34.5 0.0 collective-permute-done.4.s_near_ref
  34.5 5.6 %collective-permute-done.5.s_far_ref = f32[38,8,128]{2,1,0:T(8,128)S(1)} collective-permute-done((f32[38,8,128]{2,1,0:T(8,128)S(1)}, f32[38,8,128]{2,1,0:T(8,128)S(1)}, u32[]{:S(2)}, u32[]{:S(2)}) %collective-permute-start.5) | collective-permute-done | bytes 155680 | tf_op jit(solution)/shard_map/ppermute | solution.py:49
  40.1 0.0 copy-done.2
  40.1 51.1 %shard_map.58 = f32[1536,128]{1,0:T(8,128)} custom-call(f32[32,2,8,128]{3,2,1,0:T(8,128)S(1)} %bitcast.4, f32[3,64,8,128]{3,2,1,0:T(8,128)S(1)} %get-tuple-element.12.tile_ref, f32[3,10,8,128]{3,2,1,0:T(8,128)S(1)} %collective-permute-done.y_near_ref, f32[3,10,8,128]{3,2,1,0:T(8,128)S(1)} %collective-permute-done.1.y_far_ref, ...), custom_call_target="tpu_custom_call" | custom-call | tf_op jit(solution)/shard_map/pallas_call | solution.py:302
  (4 shorter events, 0.0 us)
Async XLA Ops:
  0.0 0.9 copy-start.3
  0.9 0.8 copy-start.4
  1.7 7.9 %copy-start = (f32[3,8,64,128]{3,2,1,0:T(8,128)S(1)}, f32[3,8,64,128]{3,2,1,0:T(8,128)}, u32[]{:S(2)}) copy-start(f32[3,8,64,128]{3,2,1,0:T(8,128)} %param.7) | copy-start | bytes 2359300
  2.8 16.0 %all-to-all-start = ((f32[16,2,2,8,128]{4,3,2,1,0:T(8,128)}), f32[16,2,2,8,128]{4,3,2,1,0:T(8,128)S(1)}, u32[]{:S(2)}, u32[]{:S(2)}) async-start(f32[16,2,2,8,128]{4,3,2,1,0:T(8,128)} %shard_map.55), calls=%async_computation | async-start | bytes 524288 | tf_op jit(solution)/shard_map/all_to_all | solution.py:289
  9.6 30.5 %copy-start.2 = (bf16[256,512]{1,0:T(8,128)(2,1)S(1)}, bf16[256,512]{1,0:T(8,128)(2,1)}, u32[]{:S(2)}) copy-start(bf16[256,512]{1,0:T(8,128)(2,1)} %constant.4.clone.east_table_ref) | copy-start | bytes 786436
  10.5 29.6 %copy-start.1 = (bf16[256,512]{1,0:T(8,128)(2,1)S(1)}, bf16[256,512]{1,0:T(8,128)(2,1)}, u32[]{:S(2)}) copy-start(bf16[256,512]{1,0:T(8,128)(2,1)} %constant.5.clone.north_table_ref) | copy-start | bytes 786436
  10.5 8.3 %collective-permute-start = (f32[3,10,8,128]{3,2,1,0:T(8,128)S(1)}, f32[3,10,8,128]{3,2,1,0:T(8,128)S(1)}, u32[]{:S(2)}, u32[]{:S(2)}) collective-permute-start(f32[3,10,8,128]{3,2,1,0:T(8,128)S(1)} %get-tuple-element.13), channel_id=1, source_target_pairs={{0,1},{1,0},{2,3},{3,2},{4,5},{5,4},{6,7},{7,6},{8,9},{9,8},{10,11... | collective-permute-start | bytes 368648 | tf_op jit(solution)/shard_map/ppermute | solution.py:44
  10.7 8.1 %collective-permute-start.1 = (f32[3,10,8,128]{3,2,1,0:T(8,128)S(1)}, f32[3,10,8,128]{3,2,1,0:T(8,128)S(1)}, u32[]{:S(2)}, u32[]{:S(2)}) collective-permute-start(f32[3,10,8,128]{3,2,1,0:T(8,128)S(1)} %get-tuple-element.14), channel_id=1, source_target_pairs={{0,15},{1,2},{2,1},{3,4},{4,3},{5,6},{6,5},{7,8},{8,7},{9,10},{10,... | collective-permute-start | bytes 368648 | tf_op jit(solution)/shard_map/ppermute | solution.py:49
  12.3 13.9 %collective-permute-start.2 = (f32[3,18,8,128]{3,2,1,0:T(8,128)S(1)}, f32[3,18,8,128]{3,2,1,0:T(8,128)S(1)}, u32[]{:S(2)}, u32[]{:S(2)}) collective-permute-start(f32[3,18,8,128]{3,2,1,0:T(8,128)S(1)} %get-tuple-element.15), channel_id=1, source_target_pairs={{0,16},{16,0},{32,48},{48,32},{64,80},{80,64},{96,112},{112,96},{1... | collective-permute-start | bytes 663560 | tf_op jit(solution)/shard_map/ppermute | solution.py:44
  15.0 19.5 %collective-permute-start.3 = (f32[3,18,8,128]{3,2,1,0:T(8,128)S(1)}, f32[3,18,8,128]{3,2,1,0:T(8,128)S(1)}, u32[]{:S(2)}, u32[]{:S(2)}) collective-permute-start(f32[3,18,8,128]{3,2,1,0:T(8,128)S(1)} %get-tuple-element.16), channel_id=1, source_target_pairs={{0,112},{16,32},{32,16},{48,64},{64,48},{80,96},{96,80},{112,0},{1... | collective-permute-start | bytes 663560 | tf_op jit(solution)/shard_map/ppermute | solution.py:49
  19.0 15.5 %collective-permute-start.4 = (f32[38,8,128]{2,1,0:T(8,128)S(1)}, f32[38,8,128]{2,1,0:T(8,128)S(1)}, u32[]{:S(2)}, u32[]{:S(2)}) collective-permute-start(f32[38,8,128]{2,1,0:T(8,128)S(1)} %get-tuple-element.17), channel_id=1, source_target_pairs={{0,16},{16,0},{32,48},{48,32},{64,80},{80,64},{96,112},{112,96},{1... | collective-permute-start | bytes 466952 | tf_op jit(solution)/shard_map/ppermute | solution.py:44
  21.6 18.5 %collective-permute-start.5 = (f32[38,8,128]{2,1,0:T(8,128)S(1)}, f32[38,8,128]{2,1,0:T(8,128)S(1)}, u32[]{:S(2)}, u32[]{:S(2)}) collective-permute-start(f32[38,8,128]{2,1,0:T(8,128)S(1)} %get-tuple-element.18), channel_id=1, source_target_pairs={{0,112},{16,32},{32,16},{48,64},{64,48},{80,96},{96,80},{112,0},{1... | collective-permute-start | bytes 466952 | tf_op jit(solution)/shard_map/ppermute | solution.py:49
where the time goes:
time: 91.4 us; the launch traced here: 91.2 us
  Pallas kernels  53.1 us (58%)
  starting transfers between devices  21.3 us (23%)
  waiting for transfers between devices  15 us (16%)
  local copies, waits for them, and re-layouts  1.76 us (2%)
    pallas_call x1, Pallas kernels, local(): call(solve_kernel, [(3 * LEVELS * ROWS, COLS)], scratch=[(CROWS + 2 * MAR...  51.1 us
    ppermute x3, waiting for transfers between devices, swap_far(): lax.ppermute(values, axis, [(i, (i + 1) % count if i % 2 else (i - 1) % c...  13.8 us
    ppermute x3, starting transfers between devices, swap_far(): lax.ppermute(values, axis, [(i, (i + 1) % count if i % 2 else (i - 1) % c...  9.06 us
    all_to_all x1, starting transfers between devices, local(): lax.all_to_all(packed, 'gy', split_axis=0, concat_axis=0, tiled=True)  6.83 us
    ppermute x3, starting transfers between devices, swap_near(): lax.ppermute(values, axis, [(i, i ^ 1) for i in range(lax.axis_size(axis))])  5.41 us
  transfers between devices with their start and end apart: 7, of which 3 were waited for; matrix products, arithmetic and copies ran while one was open for 0% of the time, Pallas kernels for 1%

commit v1 on v0

--- a/solution.py
+++ b/solution.py
@@ -1,5 +1,3 @@
-import functools
-
 import jax
 import jax.numpy as jnp
 import ml_dtypes
@@ -24,6 +22,8 @@
 RIM = 6 * REACH
 EDGE = REACH // 3
 MIDDLE = (ROWS - 2 * REACH) // 7
+HAND = 6
+CHUNK = 16
 SIDE = EDGE + MIDDLE
 
 time_step = 0.4
@@ -144,113 +144,234 @@
     return jnp.where(lane >= RIM - REACH, right, own)
 
 
-def step_rows(src, base, dst, background, c, r, count, stage):
-    dx, dy, mid = [], [], []
+def products(blocks, table_ref):
+    counts = [block.shape[0] * LEVELS for block in blocks]
+    values = jnp.concatenate(
+        [block.reshape(count, COLS) for block, count in zip(blocks, counts)], axis=0
+    )
+    high = values.astype(jnp.bfloat16)
+    low = (values - high.astype(F32)).astype(jnp.bfloat16)
+    result = jnp.dot(
+        jnp.concatenate((high, low), axis=1), table_ref[...], preferred_element_type=F32
+    )
+    pieces, start = [], 0
+    for count in counts:
+        pieces.append(result[start : start + count])
+        start += count
+    return pieces
+
+
+def stage_blocks(jobs, stage, table_ref):
+    centres = [[rows[2:-2] for rows in source] for source, _, _, _ in jobs]
+    across = products([centre for job in centres for centre in job], table_ref)
+    for index, (source, base, background, store) in enumerate(jobs):
+        mid = centres[index]
+        count = mid[0].shape[0]
+        dy = [across[3 * index + f].reshape(mid[0].shape) for f in range(3)]
+        dx = [
+            8.0 * (rows[3 : 3 + count] - rows[1 : 1 + count]) - (rows[4:] - rows[:count])
+            for rows in source
+        ]
+        east, north, warm = background
+        change = (
+            east * dx[0] + north * dy[0] + scale * (dx[1] + dy[2]),
+            east * dx[1] + north * dy[1] + warm * dx[0],
+            east * dx[2] + north * dy[2] + warm * dy[0],
+        )
+        for f in range(3):
+            moved = mid[f] - change[f]
+            if stage == 1:
+                moved = 0.75 * base[f] + 0.25 * moved
+            elif stage == 2:
+                moved = (1.0 / 3.0) * base[f] + (2.0 / 3.0) * moved
+            store(f, moved)
+
+
+def refine_tables(values, east_table_ref, north_table_ref, store):
+    n = values.shape[0]
+    (first,) = products([values[:, 0]], east_table_ref)
+    (second,) = products([values[:, 1]], north_table_ref)
+    warm = first[:, 2 * COLS :] + second[:, 2 * COLS :]
+    for k in range(2):
+        cut = slice(COLS * k, COLS * (k + 1))
+        for f, result in enumerate((first, second, warm)):
+            store(k, f, result[:, cut].reshape(n, LEVELS, COLS))
+
+
+def merged(main, rim, lane):
+    value = jnp.where(lane < REACH, roll(rim, -REACH), main)
+    return jnp.where(lane >= COLS - REACH, roll(rim, COLS - 2 * REACH - RIGHT), value)
+
+
+def inner_kernel(
+    coarse_ref, tile_ref, y_near_ref, y_far_ref, east_table_ref, north_table_ref, table_ref,
+    edges_ref, inside_ref, refined_ref, background, state, first, second,
+):
+    y_odd = parity("gy")
+    lane = lanes()
+
+    def keep(k, f, start):
+        def store(values):
+            refined_ref[k, f, start : start + values.shape[0]] = values
+
+        return store
+
+    for start in range(0, CROWS, CHUNK):
+        refine_tables(
+            coarse_ref[start : start + CHUNK],
+            east_table_ref,
+            north_table_ref,
+            lambda k, f, values, start=start: keep(k, f, start)(values),
+        )
+    for k in range(2):
+        for f in range(3):
+            refine_rows(refined_ref, k, f, 0, CROWS, background, 0)
+
+    take_near = (lane >= RIGHT).astype(jnp.int32) == 1 - y_odd
+    state[0] = tile_ref[...]
+    for row, count, register, slot in slots():
+        near_shift = lax.rem((1 - y_odd) * (RIM - REACH) - REACH * slot + COLS, COLS)
+        far_shift = lax.rem(y_odd * (RIM - REACH) - REACH * slot + COLS, COLS)
+        for f in range(3):
+            near = roll(y_near_ref[f, register : register + count], near_shift)
+            far = roll(y_far_ref[f, register : register + count], far_shift)
+            halo = jnp.where(take_near, near, far)
+            state[1, f, row : row + count] = rim_of(tile_ref[f, row : row + count], halo, halo, lane)
+
+    buffers = (state, first, second, state)
+    for s in range(STAGES):
+        source, target = buffers[s % 3], buffers[s % 3 + 1]
+        for c in range(2):
+            for f in range(3):
+                edges_ref[s, c, f, :HAND] = source[c, f, 2 * s : 2 * s + HAND]
+                edges_ref[s, c, f, HAND:] = source[c, f, ROWS - 2 * s - HAND : ROWS - 2 * s]
+        low, top = 2 * (s + 1), ROWS - 2 * (s + 1)
+        for start in range(low, top, CHUNK):
+            stop = min(start + CHUNK, top)
+            jobs = []
+            for c in range(2):
+
+                def store(f, values, c=c):
+                    target[c, f, start:stop] = values
+
+                jobs.append((
+                    [source[c, f, start - 2 : stop + 2] for f in range(3)],
+                    [state[c, f, start:stop] for f in range(3)],
+                    [background[c, f, start:stop] for f in range(3)],
+                    store,
+                ))
+            stage_blocks(jobs, s % 3, table_ref)
     for f in range(3):
-        block = src[c, f, pl.ds(r - 2, count + 4)]
-        centre = block[2 : 2 + count]
-        dx.append(8.0 * (block[3 : 3 + count] - block[1 : 1 + count]) - (block[4:] - block[:count]))
-        dy.append(8.0 * (roll(centre, -1) - roll(centre, 1)) - (roll(centre, -2) - roll(centre, 2)))
-        mid.append(centre)
-    east = background[c, 0, pl.ds(r, count)]
-    north = background[c, 1, pl.ds(r, count)]
-    warm = background[c, 2, pl.ds(r, count)]
-    change = (
-        east * dx[0] + north * dy[0] + scale * (dx[1] + dy[2]),
-        east * dx[1] + north * dy[1] + warm * dx[0],
-        east * dx[2] + north * dy[2] + warm * dy[0],
-    )
-    for f in range(3):
-        moved = mid[f] - change[f]
-        if stage == 1:
-            moved = 0.75 * base[c, f, pl.ds(r, count)] + 0.25 * moved
-        elif stage == 2:
-            moved = (1.0 / 3.0) * base[c, f, pl.ds(r, count)] + (2.0 / 3.0) * moved
-        dst[c, f, pl.ds(r, count)] = moved
-
-
-def solve_kernel(
-    coarse_ref, tile_ref, y_near_ref, y_far_ref, x_near_ref, x_far_ref, s_near_ref, s_far_ref,
-    east_table_ref, north_table_ref, out_ref, coarse, refined, background, state, first, second,
+        rows = slice(REACH, ROWS - REACH)
+        inside_ref[f] = merged(state[0, f, rows], state[1, f, rows], lane)
+
+
+def refine_rows(refined, k, f, start, count, background, first):
+    block = refined[k, f, start : start + count]
+    centre = (0.75 * scale) * block
+    side = (0.25 * scale) * block
+    odd = centre[:-1] + side[1:]
+    even = centre[1:] + side[:-1]
+    for i in range(count - 1):
+        background[k, f, first + 2 * i + 1] = odd[i]
+        background[k, f, first + 2 * i + 2] = even[i]
+
+
+def outer_kernel(
+    x_near_ref, x_far_ref, s_near_ref, s_far_ref, edges_ref, inside_ref, refined_ref,
+    east_table_ref, north_table_ref, table_ref, out_ref, coarse, refined, background, state, first, second,
 ):
-    x_odd, y_odd = parity("gx"), parity("gy")
+    x_odd = parity("gx")
     lane = lanes()
-    coarse[MARGIN : MARGIN + CROWS] = coarse_ref[...]
     for ref, high in ((s_near_ref, 1 - x_odd), (s_far_ref, x_odd)):
-        start = high * (MARGIN + CROWS)
         for i in range(MARGIN):
             for c in range(2):
-                coarse[start + i, c] = ref[2 * i + c]
-
-    @pl.loop(0, (CROWS + 2 * MARGIN) // 4)
-    def _(step):
-        m = step * 4
-        products = []
-        for c, table in ((0, east_table_ref), (1, north_table_ref)):
-            values = coarse[pl.ds(m, 4), c].reshape(4 * LEVELS, COLS)
-            high = values.astype(jnp.bfloat16)
-            low = (values - high.astype(F32)).astype(jnp.bfloat16)
-            both = jnp.concatenate((high, low), axis=1)
-            products.append(jnp.dot(both, table[...], preferred_element_type=F32))
-        warm = products[0][:, 2 * COLS :] + products[1][:, 2 * COLS :]
-        for k in range(2):
-            cut = slice(COLS * k, COLS * (k + 1))
-            refined[k, 0, pl.ds(m, 4)] = products[0][:, cut].reshape(4, LEVELS, COLS)
-            refined[k, 1, pl.ds(m, 4)] = products[1][:, cut].reshape(4, LEVELS, COLS)
-            refined[k, 2, pl.ds(m, 4)] = warm[:, cut].reshape(4, LEVELS, COLS)
-
-    @pl.loop(1, CROWS + 2 * MARGIN - 1)
-    def _(m):
+                coarse[high * MARGIN + i, c] = ref[2 * i + c]
+
+    def store(k, f, values):
+        refined[k, f, 0:MARGIN] = values[:MARGIN]
+        refined[k, f, MARGIN : 2 * MARGIN] = refined_ref[k, f, 0:MARGIN]
+        refined[k, f, 2 * MARGIN : 3 * MARGIN] = refined_ref[k, f, CROWS - MARGIN : CROWS]
+        refined[k, f, 3 * MARGIN : 4 * MARGIN] = values[MARGIN:]
+
+    refine_tables(coarse[...], east_table_ref, north_table_ref, store)
+    for side in range(2):
         for k in range(2):
             for f in range(3):
-                block = refined[k, f, pl.ds(m - 1, 3)]
-                centre = (0.75 * scale) * block[1]
-                background[k, f, 2 * m - 2] = centre + (0.25 * scale) * block[0]
-                background[k, f, 2 * m - 1] = centre + (0.25 * scale) * block[2]
-
-    state[0, :, REACH : REACH + ROWS] = tile_ref[...]
-    for row, count, register, slot in slots():
-        take_near = (lane >= RIGHT).astype(jnp.int32) == 1 - y_odd
-        for f in range(3):
-            near = y_near_ref[f, register : register + count]
-            far = y_far_ref[f, register : register + count]
-            near = roll(near, lax.rem((1 - y_odd) * (RIM - REACH) - REACH * slot + COLS, COLS))
-            far = roll(far, lax.rem(y_odd * (RIM - REACH) - REACH * slot + COLS, COLS))
-            halo = jnp.where(take_near, near, far)
-            main = tile_ref[f, row : row + count]
-            state[1, f, REACH + row : REACH + row + count] = rim_of(main, halo, halo, lane)
+                refine_rows(refined, k, f, 2 * MARGIN * side, 2 * MARGIN, background.at[side], 0)
+
     for main_ref, ref, high in ((x_near_ref, s_near_ref, 1 - x_odd), (x_far_ref, s_far_ref, x_odd)):
-        start = high * (REACH + ROWS)
-        state[0, :, pl.ds(start, REACH)] = main_ref[...]
         for f in range(3):
             corners = ref[2 * MARGIN + EDGE * f : 2 * MARGIN + EDGE * (f + 1)]
             for k in range(3):
                 main = main_ref[f, EDGE * k : EDGE * (k + 1)]
                 left = roll(corners, -REACH * k)
                 right = roll(corners, RIM - REACH - RIGHT - REACH * k)
-                state[1, f, pl.ds(start + EDGE * k, EDGE)] = rim_of(main, left, right, lane)
+                start = high * REACH + EDGE * k
+                state[high, 0, f, pl.ds(start, EDGE)] = main
+                state[high, 1, f, pl.ds(start, EDGE)] = rim_of(main, left, right, lane)
 
     buffers = (state, first, second, state)
-    for step in range(STAGES):
-        stage = step % 3
-        low, top = 2 * (step + 1), EXT - 2 * (step + 1)
-
-        @pl.loop(0, (top - low) // 4)
-        def _(i):
+    for s in range(STAGES):
+        source, target = buffers[s % 3], buffers[s % 3 + 1]
+        origin = s - s % 3
+        jobs = []
+        for side in range(2):
             for c in range(2):
-                step_rows(
-                    buffers[stage], state, buffers[stage + 1], background, c, low + 4 * i, 4, stage
-                )
+                if side == 0:
+                    low = 2 * (s + 1)
+                    rows = [
+                        jnp.concatenate((source[0, c, f, low - 2 : REACH + 2 * s], edges_ref[s, c, f, :4]))
+                        for f in range(3)
+                    ]
+                    base = [
+                        jnp.concatenate((
+                            state[0, c, f, low : REACH + 2 * origin],
+                            edges_ref[origin, c, f, : low - 2 * origin],
+                        ))
+                        for f in range(3)
+                    ]
+                else:
+                    low = REACH - 2 * (s + 1)
+                    rows = [
+                        jnp.concatenate((
+                            edges_ref[s, c, f, 2 * HAND - 4 :],
+                            source[1, c, f, REACH - 2 * s : 2 * REACH - 2 * s],
+                        ))
+                        for f in range(3)
+                    ]
+                    base = [
+                        jnp.concatenate((
+                            edges_ref[origin, c, f, 2 * HAND - (REACH - 2 * origin - low) :],
+                            state[1, c, f, REACH - 2 * origin : low + REACH],
+                        ))
+                        for f in range(3)
+                    ]
+
+                def store(f, values, side=side, c=c, low=low):
+                    target[side, c, f, low : low + REACH] = values
+
+                near = [background[side, c, f, low + 2 : low + 2 + REACH] for f in range(3)]
+                jobs.append((rows, base, near, store))
+        stage_blocks(jobs, s % 3, table_ref)
 
     for f in range(3):
-
-        @pl.loop(0, ROWS)
-        def _(row):
-            main = state[0, f, REACH + row]
-            rim = state[1, f, REACH + row]
-            value = jnp.where(lane < REACH, roll(rim, -REACH), main)
-            value = jnp.where(lane >= COLS - REACH, roll(rim, COLS - 2 * REACH - RIGHT), value)
-            out_ref[pl.ds(f * LEVELS * ROWS + row, LEVELS, stride=ROWS), :] = value
+        for side, start in ((0, 0), (1, ROWS - REACH)):
+            rows = slice(REACH * (1 - side), REACH * (1 - side) + REACH)
+            values = merged(state[side, 0, f, rows], state[side, 1, f, rows], lane)
+            for row in range(REACH):
+                out_ref[pl.ds(f * LEVELS * ROWS + start + row, LEVELS, stride=ROWS), :] = values[row]
+        for row in range(ROWS - 2 * REACH):
+            at = f * LEVELS * ROWS + REACH + row
+            out_ref[pl.ds(at, LEVELS, stride=ROWS), :] = inside_ref[f, row]
+
+
+def difference_table():
+    table = np.zeros((COLS, COLS), np.float32)
+    for j in range(COLS):
+        for offset, weight in ((1, 8.0), (-1, -8.0), (2, -1.0), (-2, 1.0)):
+            table[(j + offset) % COLS, j] = weight
+    return np.concatenate((table, table), axis=0).astype(ml_dtypes.bfloat16)
 
 
 def tables():
@@ -273,12 +394,15 @@
     return pair
 
 
-def call(kernel, outputs, scratch=(), limit=48):
+def call(kernel, outputs, scratch=(), limit=48, microseconds=1):
     return pl.pallas_call(
         kernel,
         out_shape=[jax.ShapeDtypeStruct(shape, F32) for shape in outputs],
         scratch_shapes=[pltpu.VMEM(shape, F32) for shape in scratch],
         compiler_params=pltpu.CompilerParams(vmem_limit_bytes=limit * 2**20),
+        cost_estimate=pl.CostEstimate(
+            flops=0, bytes_accessed=3_000_000 * microseconds, transcendentals=0
+        ),
     )
 
 
@@ -298,16 +422,21 @@
         coarse, y_near, y_far
     )
     s_near, s_far = swap_near(s_near, "gx"), swap_far(s_far, "gx")
-    east_table, north_table = tables()
+    east_table, north_table = (jnp.asarray(table) for table in tables())
+    table = jnp.asarray(difference_table())
+    edges, inside, refined = call(
+        inner_kernel,
+        [(STAGES, 2, 3, 2 * HAND) + block, (3, ROWS - 2 * REACH) + block, (2, 3, CROWS) + block],
+        scratch=4 * [(2, 3, ROWS) + block],
+        microseconds=6,
+    )(coarse, tile, y_near, y_far, east_table, north_table, table)
     (end,) = call(
-        solve_kernel,
+        outer_kernel,
         [(3 * LEVELS * ROWS, COLS)],
-        scratch=[(CROWS + 2 * MARGIN, 2) + block, (2, 3, CROWS + 2 * MARGIN) + block]
-        + 4 * [(2, 3, EXT) + block],
-    )(
-        coarse, tile, y_near, y_far, x_near, x_far, s_near, s_far,
-        jnp.asarray(east_table), jnp.asarray(north_table),
-    )
+        scratch=[(2 * MARGIN, 2) + block, (2, 3, 4 * MARGIN) + block, (2, 2, 3, 4 * MARGIN) + block]
+        + 3 * [(2, 2, 3, 2 * REACH) + block],
+        microseconds=6,
+    )(x_near, x_far, s_near, s_far, edges, inside, refined, east_table, north_table, table)
     return end.reshape(acoustic_start.shape)
 
 

time: 91.4 us -> 46.9 us (0.51)
  Pallas kernels: 53.1 us -> 14 us
  waiting for transfers between devices: 15 us -> 5.56 us
  local copies, waits for them, and re-layouts: 1.76 us -> 5.61 us
    pallas_call x1 -> x2, Pallas kernels: 51.1 us -> 11.9 us  [the longest x1 6.18 us: local(): call(outer_kernel, [(3 * LEVELS * ROWS, COLS)], scratch=[(2 * MARGIN, 2)...]
    ppermute x3, waiting for transfers between devices: 13.8 us -> 5.55 us  [swap_far(): lax.ppermute(values, axis, [(i, (i + 1) % count if i % 2 else (i - 1) % c...]
    unnamed x10 -> x12, local copies, waits for them, and re-layouts: 1.76 us -> 5.61 us
    ppermute x3, waiting for transfers between devices: 1.13 us -> 0.01 us  [swap_near(): lax.ppermute(values, axis, [(i, i ^ 1) for i in range(lax.axis_size(axis))])]
  transfers between devices with their start and end apart: 7 -> 7, of which waited for: 3 -> 1; matrix products, arithmetic and copies ran while one was open for 0% -> 0% of each run, Pallas kernels for 1% -> 14%
where the time goes in v1:
time: 46.9 us; the launch traced here: 46.5 us
  starting transfers between devices  21.3 us (45%)
  Pallas kernels  14 us (30%)
  local copies, waits for them, and re-layouts  5.61 us (12%)
  waiting for transfers between devices  5.56 us (12%)
    ppermute x3, starting transfers between devices, swap_far(): lax.ppermute(values, axis, [(i, (i + 1) % count if i % 2 else (i - 1) % c...  9.24 us
    all_to_all x1, starting transfers between devices, local(): lax.all_to_all(packed, 'gy', split_axis=0, concat_axis=0, tiled=True)  6.83 us
    pallas_call x1, Pallas kernels, local(): call(outer_kernel, [(3 * LEVELS * ROWS, COLS)], scratch=[(2 * MARGIN, 2)...  6.18 us
    pallas_call x1, Pallas kernels, local(): call(inner_kernel, [(STAGES, 2, 3, 2 * HAND) + block, (3, ROWS - 2 * REAC...  5.76 us
    unnamed x12, local copies, waits for them, and re-layouts  5.61 us
    ppermute x3, waiting for transfers between devices, swap_far(): lax.ppermute(values, axis, [(i, (i + 1) % count if i % 2 else (i - 1) % c...  5.55 us
    ppermute x3, starting transfers between devices, swap_near(): lax.ppermute(values, axis, [(i, i ^ 1) for i in range(lax.axis_size(axis))])  5.22 us
    pallas_call x1, Pallas kernels, local(): call(coarse_pack_kernel, [(groups, 2, 2) + block])(les_wind, les_temp)  1.04 us
  transfers between devices with their start and end apart: 7, of which 1 were waited for; matrix products, arithmetic and copies ran while one was open for 0% of the time, Pallas kernels for 14%

profile of v1, /device:TPU:1, one launch (start us, length us, event | category | flops | bytes accessed | tf_op | source)
XLA Modules:
  0.0 46.5 jit_solution(2164371329339350186)
XLA Ops:
  0.0 0.9 %copy-done.4 = f32[2,8,2,1024]{3,2,1,0:T(2,128)S(1)} copy-done((f32[2,8,2,1024]{3,2,1,0:T(2,128)S(1)}, f32[2,8,2,1024]{3,2,1,0:T(2,128)}, u32[]{:S(2)}) %copy-start.4) | copy-done | bytes 131096
  0.9 0.8 %copy-done.5 = f32[8,2,1024]{2,1,0:T(2,128)S(1)} copy-done((f32[8,2,1024]{2,1,0:T(2,128)S(1)}, f32[8,2,1024]{2,1,0:T(2,128)}, u32[]{:S(2)}) %copy-start.5) | copy-done | bytes 65560
  1.7 1.0 %shard_map.65 = f32[16,2,2,8,128]{4,3,2,1,0:T(8,128)} custom-call(f32[2,8,2,1024]{3,2,1,0:T(2,128)S(1)} %copy-done.4, f32[8,2,1024]{2,1,0:T(2,128)S(1)} %copy-done.5), custom_call_target="tpu_custom_call" | custom-call | bytes 3000000 | tf_op jit(solution)/shard_map/pallas_call | solution.py:412
  2.8 6.8 %all-to-all-start = ((f32[16,2,2,8,128]{4,3,2,1,0:T(8,128)}), f32[16,2,2,8,128]{4,3,2,1,0:T(8,128)S(1)}, u32[]{:S(2)}, u32[]{:S(2)}) async-start(f32[16,2,2,8,128]{4,3,2,1,0:T(8,128)} %shard_map.65), calls=%async_computation | async-start | bytes 524288 | tf_op jit(solution)/shard_map/all_to_all | solution.py:413
  9.6 1.1 %copy-done.2 = f32[3,8,64,128]{3,2,1,0:T(8,128)S(1)} copy-done((f32[3,8,64,128]{3,2,1,0:T(8,128)S(1)}, f32[3,8,64,128]{3,2,1,0:T(8,128)}, u32[]{:S(2)}) %copy-start.2) | copy-done | bytes 786456
  10.7 0.8 %shard_map.64 = (f32[3,64,8,128]{3,2,1,0:T(8,128)S(1)}, f32[3,18,8,128]{3,2,1,0:T(8,128)S(1)}, f32[3,18,8,128]{3,2,1,0:T(8,128)S(1)}, f32[3,10,8,128]{3,2,1,0:T(8,128)S(1)}, f32[3,10,8,128]{3,2,1,0:T(8,128)S(1)}) custom-call(f32[1536,128]{1,0:T(8,128)S(1)} %bitcast.5), custom_call_target="tpu_custom_call" | custom-call | bytes 3000000 | tf_op jit(solution)/shard_map/pallas_call | solution.py:415
  11.6 0.2 collective-permute-start.2
  11.7 1.7 %collective-permute-start.3 = (f32[3,10,8,128]{3,2,1,0:T(8,128)S(1)}, f32[3,10,8,128]{3,2,1,0:T(8,128)S(1)}, u32[]{:S(2)}, u32[]{:S(2)}) collective-permute-start(f32[3,10,8,128]{3,2,1,0:T(8,128)S(1)} %get-tuple-element.18), channel_id=1, source_target_pairs={{0,15},{1,2},{2,1},{3,4},{4,3},{5,6},{6,5},{7,8},{8,7},{9,10},{10,... | collective-permute-start | bytes 368648 | tf_op jit(solution)/shard_map/ppermute | solution.py:49
  13.4 2.6 %collective-permute-start = (f32[3,18,8,128]{3,2,1,0:T(8,128)S(1)}, f32[3,18,8,128]{3,2,1,0:T(8,128)S(1)}, u32[]{:S(2)}, u32[]{:S(2)}) collective-permute-start(f32[3,18,8,128]{3,2,1,0:T(8,128)S(1)} %get-tuple-element.15), channel_id=1, source_target_pairs={{0,16},{16,0},{32,48},{48,32},{64,80},{80,64},{96,112},{112,96},{1... | collective-permute-start | bytes 663560 | tf_op jit(solution)/shard_map/ppermute | solution.py:44
  16.1 3.8 %collective-permute-start.1 = (f32[3,18,8,128]{3,2,1,0:T(8,128)S(1)}, f32[3,18,8,128]{3,2,1,0:T(8,128)S(1)}, u32[]{:S(2)}, u32[]{:S(2)}) collective-permute-start(f32[3,18,8,128]{3,2,1,0:T(8,128)S(1)} %get-tuple-element.16), channel_id=1, source_target_pairs={{0,112},{16,32},{32,16},{48,64},{64,48},{80,96},{96,80},{112,0},{1... | collective-permute-start | bytes 663560 | tf_op jit(solution)/shard_map/ppermute | solution.py:49
  19.9 0.0 collective-permute-done.2.y_near_ref
  19.9 0.0 collective-permute-done.3.y_far_ref
  19.9 0.0 all-to-all-done
  19.9 0.2 shard_map.66
  20.1 2.4 %collective-permute-start.4 = (f32[38,8,128]{2,1,0:T(8,128)S(1)}, f32[38,8,128]{2,1,0:T(8,128)S(1)}, u32[]{:S(2)}, u32[]{:S(2)}) collective-permute-start(f32[38,8,128]{2,1,0:T(8,128)S(1)} %get-tuple-element.19), channel_id=1, source_target_pairs={{0,16},{16,0},{32,48},{48,32},{64,80},{80,64},{96,112},{112,96},{1... | collective-permute-start | bytes 466952 | tf_op jit(solution)/shard_map/ppermute | solution.py:44
  22.5 3.7 %collective-permute-start.5 = (f32[38,8,128]{2,1,0:T(8,128)S(1)}, f32[38,8,128]{2,1,0:T(8,128)S(1)}, u32[]{:S(2)}, u32[]{:S(2)}) collective-permute-start(f32[38,8,128]{2,1,0:T(8,128)S(1)} %get-tuple-element.20), channel_id=1, source_target_pairs={{0,112},{16,32},{32,16},{48,64},{64,48},{80,96},{96,80},{112,0},{1... | collective-permute-start | bytes 466952 | tf_op jit(solution)/shard_map/ppermute | solution.py:49
  26.2 0.9 %copy-done = bf16[256,512]{1,0:T(8,128)(2,1)S(1)} copy-done((bf16[256,512]{1,0:T(8,128)(2,1)S(1)}, bf16[256,512]{1,0:T(8,128)(2,1)}, u32[]{:S(2)}) %copy-start) | copy-done | bytes 262168
  27.2 0.9 %copy-done.1 = bf16[256,512]{1,0:T(8,128)(2,1)S(1)} copy-done((bf16[256,512]{1,0:T(8,128)(2,1)S(1)}, bf16[256,512]{1,0:T(8,128)(2,1)}, u32[]{:S(2)}) %copy-start.1) | copy-done | bytes 262168
  28.1 0.8 %copy-done.3 = bf16[256,128]{1,0:T(8,128)(2,1)S(1)} copy-done((bf16[256,128]{1,0:T(8,128)(2,1)S(1)}, bf16[256,128]{1,0:T(8,128)(2,1)}, u32[]{:S(2)}) %copy-start.3) | copy-done | bytes 65560
  29.0 5.8 %shard_map.67 = (f32[9,2,3,12,8,128]{5,4,3,2,1,0:T(8,128)S(1)}, f32[3,28,8,128]{3,2,1,0:T(8,128)S(1)}, f32[2,3,32,8,128]{4,3,2,1,0:T(8,128)S(1)}) custom-call(f32[32,2,8,128]{3,2,1,0:T(8,128)S(1)} %bitcast.4, f32[3,64,8,128]{3,2,1,0:T(8,128)S(1)} %get-tuple-element.21.tile_ref, f32[3,10,8,128]{3,2,1,0:T(8,128)S(1)} %collective-permute-done.2.y_near_ref, ...), custom_call_target="tpu_custom_call" | custom-call | bytes 18000000 | tf_op jit(solution)/shard_map/pallas_call | solution.py:427
  34.7 0.0 collective-permute-done.x_near_ref
  34.7 0.0 collective-permute-done.1.x_far_ref
  34.8 5.5 %collective-permute-done.5.s_far_ref = f32[38,8,128]{2,1,0:T(8,128)S(1)} collective-permute-done((f32[38,8,128]{2,1,0:T(8,128)S(1)}, f32[38,8,128]{2,1,0:T(8,128)S(1)}, u32[]{:S(2)}, u32[]{:S(2)}) %collective-permute-start.5) | collective-permute-done | bytes 155680 | tf_op jit(solution)/shard_map/ppermute | solution.py:49
  40.3 6.2 %shard_map.68 = f32[1536,128]{1,0:T(8,128)} custom-call(f32[3,18,8,128]{3,2,1,0:T(8,128)S(1)} %collective-permute-done.x_near_ref, f32[3,18,8,128]{3,2,1,0:T(8,128)S(1)} %collective-permute-done.1.x_far_ref, f32[38,8,128]{2,1,0:T(8,128)S(1)} %collective-permute-done.4.s_near_ref, f32[38,8,128]{2,1,0:T(8,128)S(1)} %collective-permute-done.5.s_far_ref, ...), custom_call_target="tpu_custom_call" | custom-call | bytes 18000000 | tf_op jit(solution)/shard_map/pallas_call | solution.py:433
  (7 shorter events, 0.0 us)
Async XLA Ops:
  0.0 0.9 %copy-start.4 = (f32[2,8,2,1024]{3,2,1,0:T(2,128)S(1)}, f32[2,8,2,1024]{3,2,1,0:T(2,128)}, u32[]{:S(2)}) copy-start(f32[2,8,2,1024]{3,2,1,0:T(2,128)} %wind_ref.1) | copy-start | bytes 393220
  0.9 0.8 %copy-start.5 = (f32[8,2,1024]{2,1,0:T(2,128)S(1)}, f32[8,2,1024]{2,1,0:T(2,128)}, u32[]{:S(2)}) copy-start(f32[8,2,1024]{2,1,0:T(2,128)} %temp_ref.1) | copy-start | bytes 196612
  2.8 17.1 %all-to-all-start = ((f32[16,2,2,8,128]{4,3,2,1,0:T(8,128)}), f32[16,2,2,8,128]{4,3,2,1,0:T(8,128)S(1)}, u32[]{:S(2)}, u32[]{:S(2)}) async-start(f32[16,2,2,8,128]{4,3,2,1,0:T(8,128)} %shard_map.65), calls=%async_computation | async-start | bytes 524288 | tf_op jit(solution)/shard_map/all_to_all | solution.py:413
  9.6 1.1 %copy-start.2 = (f32[3,8,64,128]{3,2,1,0:T(8,128)S(1)}, f32[3,8,64,128]{3,2,1,0:T(8,128)}, u32[]{:S(2)}) copy-start(f32[3,8,64,128]{3,2,1,0:T(8,128)} %param.8) | copy-start | bytes 2359300
  11.6 8.3 %collective-permute-start.2 = (f32[3,10,8,128]{3,2,1,0:T(8,128)S(1)}, f32[3,10,8,128]{3,2,1,0:T(8,128)S(1)}, u32[]{:S(2)}, u32[]{:S(2)}) collective-permute-start(f32[3,10,8,128]{3,2,1,0:T(8,128)S(1)} %get-tuple-element.17), channel_id=1, source_target_pairs={{0,1},{1,0},{2,3},{3,2},{4,5},{5,4},{6,7},{7,6},{8,9},{9,8},{10,11... | collective-permute-start | bytes 368648 | tf_op jit(solution)/shard_map/ppermute | solution.py:44
  11.7 8.1 %collective-permute-start.3 = (f32[3,10,8,128]{3,2,1,0:T(8,128)S(1)}, f32[3,10,8,128]{3,2,1,0:T(8,128)S(1)}, u32[]{:S(2)}, u32[]{:S(2)}) collective-permute-start(f32[3,10,8,128]{3,2,1,0:T(8,128)S(1)} %get-tuple-element.18), channel_id=1, source_target_pairs={{0,15},{1,2},{2,1},{3,4},{4,3},{5,6},{6,5},{7,8},{8,7},{9,10},{10,... | collective-permute-start | bytes 368648 | tf_op jit(solution)/shard_map/ppermute | solution.py:49
  13.4 21.3 %collective-permute-start = (f32[3,18,8,128]{3,2,1,0:T(8,128)S(1)}, f32[3,18,8,128]{3,2,1,0:T(8,128)S(1)}, u32[]{:S(2)}, u32[]{:S(2)}) collective-permute-start(f32[3,18,8,128]{3,2,1,0:T(8,128)S(1)} %get-tuple-element.15), channel_id=1, source_target_pairs={{0,16},{16,0},{32,48},{48,32},{64,80},{80,64},{96,112},{112,96},{1... | collective-permute-start | bytes 663560 | tf_op jit(solution)/shard_map/ppermute | solution.py:44
  16.1 18.7 %collective-permute-start.1 = (f32[3,18,8,128]{3,2,1,0:T(8,128)S(1)}, f32[3,18,8,128]{3,2,1,0:T(8,128)S(1)}, u32[]{:S(2)}, u32[]{:S(2)}) collective-permute-start(f32[3,18,8,128]{3,2,1,0:T(8,128)S(1)} %get-tuple-element.16), channel_id=1, source_target_pairs={{0,112},{16,32},{32,16},{48,64},{64,48},{80,96},{96,80},{112,0},{1... | collective-permute-start | bytes 663560 | tf_op jit(solution)/shard_map/ppermute | solution.py:49
  20.1 14.7 %collective-permute-start.4 = (f32[38,8,128]{2,1,0:T(8,128)S(1)}, f32[38,8,128]{2,1,0:T(8,128)S(1)}, u32[]{:S(2)}, u32[]{:S(2)}) collective-permute-start(f32[38,8,128]{2,1,0:T(8,128)S(1)} %get-tuple-element.19), channel_id=1, source_target_pairs={{0,16},{16,0},{32,48},{48,32},{64,80},{80,64},{96,112},{112,96},{1... | collective-permute-start | bytes 466952 | tf_op jit(solution)/shard_map/ppermute | solution.py:44
  22.5 17.8 %collective-permute-start.5 = (f32[38,8,128]{2,1,0:T(8,128)S(1)}, f32[38,8,128]{2,1,0:T(8,128)S(1)}, u32[]{:S(2)}, u32[]{:S(2)}) collective-permute-start(f32[38,8,128]{2,1,0:T(8,128)S(1)} %get-tuple-element.20), channel_id=1, source_target_pairs={{0,112},{16,32},{32,16},{48,64},{64,48},{80,96},{96,80},{112,0},{1... | collective-permute-start | bytes 466952 | tf_op jit(solution)/shard_map/ppermute | solution.py:49
  26.2 0.9 %copy-start = (bf16[256,512]{1,0:T(8,128)(2,1)S(1)}, bf16[256,512]{1,0:T(8,128)(2,1)}, u32[]{:S(2)}) copy-start(bf16[256,512]{1,0:T(8,128)(2,1)} %constant.6.clone.east_table_ref) | copy-start | bytes 786436
  27.2 0.9 %copy-start.1 = (bf16[256,512]{1,0:T(8,128)(2,1)S(1)}, bf16[256,512]{1,0:T(8,128)(2,1)}, u32[]{:S(2)}) copy-start(bf16[256,512]{1,0:T(8,128)(2,1)} %constant.7.clone.north_table_ref) | copy-start | bytes 786436
  28.1 0.8 %copy-start.3 = (bf16[256,128]{1,0:T(8,128)(2,1)S(1)}, bf16[256,128]{1,0:T(8,128)(2,1)}, u32[]{:S(2)}) copy-start(bf16[256,128]{1,0:T(8,128)(2,1)} %constant.8.clone.table_ref) | copy-start | bytes 196612

commit v2 on v1

--- a/solution.py
+++ b/solution.py
@@ -22,8 +22,13 @@
 RIM = 6 * REACH
 EDGE = REACH // 3
 MIDDLE = (ROWS - 2 * REACH) // 7
+HROWS = REACH // 2
+PAIRS = REACH // 2
+PER = COLS // REACH
+CREGS = -(-2 * PAIRS // PER)
 HAND = 6
 CHUNK = 16
+PACK_LIMIT = 60
 SIDE = EDGE + MIDDLE
 
 time_step = 0.4
@@ -69,7 +74,7 @@
     return pieces
 
 
-def coarse_pack_kernel(wind_ref, temp_ref, out_ref):
+def pack_coarse(wind_ref, temp_ref, out_ref):
     lane = lanes()
     blocks = wind_ref.shape[-1] // COLS
 
@@ -92,8 +97,21 @@
             out_ref[j, row, 1] = jnp.where(lane < WINDOW, north[j], roll(warm[j], HALF))
 
 
-def acoustic_pack_kernel(start_ref, tile_ref, x_near_ref, x_far_ref, y_near_ref, y_far_ref):
+def pack_kernel(
+    wind_hbm, temp_hbm, start_hbm, out_ref, tile_ref, x_near_ref, x_far_ref, y_near_ref, y_far_ref,
+    wind_ref, temp_ref, start_ref, sems,
+):
     x_odd, y_odd = parity("gx"), parity("gy")
+    wind_copy = pltpu.make_async_copy(wind_hbm, wind_ref, sems.at[0])
+    temp_copy = pltpu.make_async_copy(temp_hbm, temp_ref, sems.at[1])
+    start_copy = pltpu.make_async_copy(start_hbm, start_ref, sems.at[2])
+    wind_copy.start()
+    temp_copy.start()
+    start_copy.start()
+    wind_copy.wait()
+    temp_copy.wait()
+    pack_coarse(wind_ref, temp_ref, out_ref)
+    start_copy.wait()
     for f in range(3):
         for row in range(ROWS):
             tile_ref[f, row] = start_ref[pl.ds(f * LEVELS * ROWS + row, LEVELS, stride=ROWS), :]
@@ -105,7 +123,7 @@
         (y_far_ref, y_odd * (COLS - REACH)),
     ):
         for f in range(3):
-            for group, size, base in ((0, EDGE, 0), (1, MIDDLE, EDGE)):
+            for size, base in ((EDGE, 0), (MIDDLE, EDGE)):
                 packed = None
                 for row, count, register, slot in slots():
                     if register != base:
@@ -120,22 +138,53 @@
                 ref[f, base : base + size] = packed
 
 
+def corner_slot(away, right):
+    pair = min(away, REACH - 2 - away)
+    register, slot = divmod(pair + PAIRS * right, PER)
+    offset = 0
+    if away > pair:
+        offset = (REACH - 1 - pair) * (1 if right else -1)
+    return register, REACH * slot, offset
+
+
+def corner_lanes(away, right, lane):
+    _, first, _ = corner_slot(away, right)
+    pair = min(away, REACH - 2 - away)
+    if away == pair:
+        low, high = (0, REACH - 1 - away) if right else (1 + away, REACH)
+    else:
+        low, high = (REACH - 1 - pair, REACH) if right else (0, pair + 1)
+    return (lane >= first + low) & (lane < first + high)
+
+
 def second_pack_kernel(coarse_ref, y_near_ref, y_far_ref, x_near_ref, x_far_ref):
     x_odd, y_odd = parity("gx"), parity("gy")
     lane = lanes()
-    width = 3 * REACH
     for ref, bottom in ((x_near_ref, 1 - x_odd), (x_far_ref, x_odd)):
-        first = bottom * (CROWS - MARGIN)
-        for i in range(MARGIN):
+        first = bottom * (CROWS - HROWS)
+        for i in range(HROWS):
             for c in range(2):
                 ref[2 * i + c] = coarse_ref[first + i, c]
         for f in range(3):
-            for t in range(EDGE):
-                start = bottom * width
-                near = roll(y_near_ref[f, t], lax.rem((1 - y_odd) * width - start + COLS, COLS))
-                far = roll(y_far_ref[f, t], lax.rem(y_odd * width - start + COLS, COLS))
-                take_near = (lane >= width).astype(jnp.int32) == 1 - y_odd
-                ref[2 * MARGIN + EDGE * f + t] = jnp.where(take_near, near, far)
+            packed = [None] * CREGS
+            for away in range(REACH - 1):
+                slot, t = divmod(away, EDGE)
+                register = t + bottom * (EDGE - 1 - 2 * t)
+                source = REACH * (slot + bottom * (5 - 2 * slot))
+                for right in range(2):
+                    target, start, offset = corner_slot(away, right)
+                    take_far = y_odd if right else 1 - y_odd
+                    near = y_near_ref[f, register]
+                    far = y_far_ref[f, register]
+                    halo = jnp.where(jnp.full_like(lane, take_far) == 1, far, near)
+                    moved = roll(halo, lax.rem(start + offset - source + 3 * COLS, COLS))
+                    if packed[target] is None:
+                        packed[target] = moved
+                    else:
+                        inside = corner_lanes(away, right, lane)
+                        packed[target] = jnp.where(inside, moved, packed[target])
+            for target in range(CREGS):
+                ref[2 * HROWS + CREGS * f + target] = packed[target]
 
 
 def rim_of(main, left, right, lane):
@@ -161,11 +210,13 @@
     return pieces
 
 
-def stage_blocks(jobs, stage, table_ref):
-    centres = [[rows[2:-2] for rows in source] for source, _, _, _ in jobs]
-    across = products([centre for job in centres for centre in job], table_ref)
+def stage_products(jobs, table_ref):
+    return products([rows[2:-2] for source, _, _, _ in jobs for rows in source], table_ref)
+
+
+def stage_sums(jobs, across, stage):
     for index, (source, base, background, store) in enumerate(jobs):
-        mid = centres[index]
+        mid = [rows[2:-2] for rows in source]
         count = mid[0].shape[0]
         dy = [across[3 * index + f].reshape(mid[0].shape) for f in range(3)]
         dx = [
@@ -260,7 +311,7 @@
                     [background[c, f, start:stop] for f in range(3)],
                     store,
                 ))
-            stage_blocks(jobs, s % 3, table_ref)
+            stage_sums(jobs, stage_products(jobs, table_ref), s % 3)
     for f in range(3):
         rows = slice(REACH, ROWS - REACH)
         inside_ref[f] = merged(state[0, f, rows], state[1, f, rows], lane)
@@ -279,81 +330,93 @@
 
 def outer_kernel(
     x_near_ref, x_far_ref, s_near_ref, s_far_ref, edges_ref, inside_ref, refined_ref,
-    east_table_ref, north_table_ref, table_ref, out_ref, coarse, refined, background, state, first, second,
+    east_table_ref, north_table_ref, table_ref, out_ref, refined, background, state, first, second,
 ):
     x_odd = parity("gx")
     lane = lanes()
+    own = MARGIN + HROWS
+    for k in range(2):
+        for f in range(3):
+            refined[k, f, HROWS:own] = refined_ref[k, f, 0:MARGIN]
+            refined[k, f, own : own + MARGIN] = refined_ref[k, f, CROWS - MARGIN : CROWS]
     for ref, high in ((s_near_ref, 1 - x_odd), (s_far_ref, x_odd)):
-        for i in range(MARGIN):
-            for c in range(2):
-                coarse[high * MARGIN + i, c] = ref[2 * i + c]
-
-    def store(k, f, values):
-        refined[k, f, 0:MARGIN] = values[:MARGIN]
-        refined[k, f, MARGIN : 2 * MARGIN] = refined_ref[k, f, 0:MARGIN]
-        refined[k, f, 2 * MARGIN : 3 * MARGIN] = refined_ref[k, f, CROWS - MARGIN : CROWS]
-        refined[k, f, 3 * MARGIN : 4 * MARGIN] = values[MARGIN:]
-
-    refine_tables(coarse[...], east_table_ref, north_table_ref, store)
+
+        def store(k, f, values, high=high):
+            refined[k, f, pl.ds(high * (own + MARGIN), HROWS)] = values
+
+        values = ref[: 2 * HROWS].reshape(HROWS, 2, LEVELS, COLS)
+        refine_tables(values, east_table_ref, north_table_ref, store)
     for side in range(2):
         for k in range(2):
             for f in range(3):
-                refine_rows(refined, k, f, 2 * MARGIN * side, 2 * MARGIN, background.at[side], 0)
+                refine_rows(refined, k, f, own * side, own, background.at[side], 0)
 
     for main_ref, ref, high in ((x_near_ref, s_near_ref, 1 - x_odd), (x_far_ref, s_far_ref, x_odd)):
         for f in range(3):
-            corners = ref[2 * MARGIN + EDGE * f : 2 * MARGIN + EDGE * (f + 1)]
-            for k in range(3):
-                main = main_ref[f, EDGE * k : EDGE * (k + 1)]
-                left = roll(corners, -REACH * k)
-                right = roll(corners, RIM - REACH - RIGHT - REACH * k)
-                start = high * REACH + EDGE * k
-                state[high, 0, f, pl.ds(start, EDGE)] = main
-                state[high, 1, f, pl.ds(start, EDGE)] = rim_of(main, left, right, lane)
+            state[high, 0, f, pl.ds(high * REACH, REACH)] = main_ref[f]
+            for away in range(REACH):
+                row = REACH - 1 - away + high * (2 * away - REACH + 1)
+                main = main_ref[f, row]
+                halo = []
+                for right in range(2):
+                    register, start, offset = corner_slot(min(away, REACH - 2), right)
+                    values = ref[2 * HROWS + CREGS * f + register]
+                    halo.append(roll(values, (RIM - REACH) * right - start - offset))
+                state[high, 1, f, high * REACH + row] = rim_of(main, halo[0], halo[1], lane)
 
     buffers = (state, first, second, state)
-    for s in range(STAGES):
+
+    def jobs_of(side, s):
         source, target = buffers[s % 3], buffers[s % 3 + 1]
         origin = s - s % 3
         jobs = []
+        for c in range(2):
+            if side == 0:
+                low = 2 * (s + 1)
+                rows = [
+                    jnp.concatenate((source[0, c, f, low - 2 : REACH + 2 * s], edges_ref[s, c, f, :4]))
+                    for f in range(3)
+                ]
+                base = [
+                    jnp.concatenate((
+                        state[0, c, f, low : REACH + 2 * origin],
+                        edges_ref[origin, c, f, : low - 2 * origin],
+                    ))
+                    for f in range(3)
+                ]
+            else:
+                low = REACH - 2 * (s + 1)
+                rows = [
+                    jnp.concatenate((
+                        edges_ref[s, c, f, 2 * HAND - 4 :],
+                        source[1, c, f, REACH - 2 * s : 2 * REACH - 2 * s],
+                    ))
+                    for f in range(3)
+                ]
+                base = [
+                    jnp.concatenate((
+                        edges_ref[origin, c, f, 2 * HAND - (REACH - 2 * origin - low) :],
+                        state[1, c, f, REACH - 2 * origin : low + REACH],
+                    ))
+                    for f in range(3)
+                ]
+
+            def store(f, values, c=c):
+                target[side, c, f, low : low + REACH] = values
+
+            start = low + 2 * side
+            near = [background[side, c, f, start : start + REACH] for f in range(3)]
+            jobs.append((rows, base, near, store))
+        return jobs
+
+    waiting = [None, None]
+    for s in range(STAGES + 1):
         for side in range(2):
-            for c in range(2):
-                if side == 0:
-                    low = 2 * (s + 1)
-                    rows = [
-                        jnp.concatenate((source[0, c, f, low - 2 : REACH + 2 * s], edges_ref[s, c, f, :4]))
-                        for f in range(3)
-                    ]
-                    base = [
-                        jnp.concatenate((
-                            state[0, c, f, low : REACH + 2 * origin],
-                            edges_ref[origin, c, f, : low - 2 * origin],
-                        ))
-                        for f in range(3)
-                    ]
-                else:
-                    low = REACH - 2 * (s + 1)
-                    rows = [
-                        jnp.concatenate((
-                            edges_ref[s, c, f, 2 * HAND - 4 :],
-                            source[1, c, f, REACH - 2 * s : 2 * REACH - 2 * s],
-                        ))
-                        for f in range(3)
-                    ]
-                    base = [
-                        jnp.concatenate((
-                            edges_ref[origin, c, f, 2 * HAND - (REACH - 2 * origin - low) :],
-                            state[1, c, f, REACH - 2 * origin : low + REACH],
-                        ))
-                        for f in range(3)
-                    ]
-
-                def store(f, values, side=side, c=c, low=low):
-                    target[side, c, f, low : low + REACH] = values
-
-                near = [background[side, c, f, low + 2 : low + 2 + REACH] for f in range(3)]
-                jobs.append((rows, base, near, store))
-        stage_blocks(jobs, s % 3, table_ref)
+            if waiting[side] is not None:
+                stage_sums(waiting[side][0], waiting[side][1], (s - 1) % 3)
+            if s < STAGES:
+                jobs = jobs_of(side, s)
+                waiting[side] = (jobs, stage_products(jobs, table_ref))
 
     for f in range(3):
         for side, start in ((0, 0), (1, ROWS - REACH)):
@@ -394,11 +457,14 @@
     return pair
 
 
-def call(kernel, outputs, scratch=(), limit=48, microseconds=1):
+def call(kernel, outputs, scratch=(), limit=48, microseconds=1, copies=0):
+    specs = {"in_specs": [pl.BlockSpec(memory_space=pltpu.HBM)] * copies} if copies else {}
     return pl.pallas_call(
         kernel,
         out_shape=[jax.ShapeDtypeStruct(shape, F32) for shape in outputs],
-        scratch_shapes=[pltpu.VMEM(shape, F32) for shape in scratch],
+        **specs,
+        scratch_shapes=[pltpu.VMEM(shape, F32) for shape in scratch]
+        + ([pltpu.SemaphoreType.DMA((copies,))] if copies else []),
         compiler_params=pltpu.CompilerParams(vmem_limit_bytes=limit * 2**20),
         cost_estimate=pl.CostEstimate(
             flops=0, bytes_accessed=3_000_000 * microseconds, transcendentals=0
@@ -409,16 +475,20 @@
 def local(les_wind, les_temp, acoustic_start):
     block = (LEVELS, COLS)
     groups = lax.axis_size("gy")
-    (packed,) = call(coarse_pack_kernel, [(groups, 2, 2) + block])(les_wind, les_temp)
+    packed, tile, x_near, x_far, y_near, y_far = call(
+        pack_kernel,
+        [(groups, 2, 2) + block, (3, ROWS) + block]
+        + 2 * [(3, REACH) + block]
+        + 2 * [(3, SIDE) + block],
+        scratch=[les_wind.shape, les_temp.shape, (3 * LEVELS * ROWS, COLS)],
+        copies=3,
+        limit=PACK_LIMIT,
+    )(les_wind, les_temp, acoustic_start.reshape(3 * LEVELS * ROWS, COLS))
     coarse = lax.all_to_all(packed, "gy", split_axis=0, concat_axis=0, tiled=True)
     coarse = coarse.reshape((CROWS, 2) + block)
-    tile, x_near, x_far, y_near, y_far = call(
-        acoustic_pack_kernel,
-        [(3, ROWS) + block] + 2 * [(3, REACH) + block] + 2 * [(3, SIDE) + block],
-    )(acoustic_start.reshape(3 * LEVELS * ROWS, COLS))
     y_near, y_far = swap_near(y_near, "gy"), swap_far(y_far, "gy")
     x_near, x_far = swap_near(x_near, "gx"), swap_far(x_far, "gx")
-    s_near, s_far = call(second_pack_kernel, 2 * [(2 * MARGIN + 3 * EDGE,) + block])(
+    s_near, s_far = call(second_pack_kernel, 2 * [(2 * HROWS + 3 * CREGS,) + block])(
         coarse, y_near, y_far
     )
     s_near, s_far = swap_near(s_near, "gx"), swap_far(s_far, "gx")
@@ -433,7 +503,7 @@
     (end,) = call(
         outer_kernel,
         [(3 * LEVELS * ROWS, COLS)],
-        scratch=[(2 * MARGIN, 2) + block, (2, 3, 4 * MARGIN) + block, (2, 2, 3, 4 * MARGIN) + block]
+        scratch=[(2, 3, 2 * (MARGIN + HROWS)) + block, (2, 2, 3, 2 * (MARGIN + HROWS)) + block]
         + 3 * [(2, 2, 3, 2 * REACH) + block],
         microseconds=6,
     )(x_near, x_far, s_near, s_far, edges, inside, refined, east_table, north_table, table)

time: 46.9 us -> 45.1 us (0.962)
  Pallas kernels: 14 us -> 16 us
  waiting for transfers between devices: 5.56 us -> 3.81 us
  local copies, waits for them, and re-layouts: 5.61 us -> 3.87 us
    pallas_call x4 -> x3, Pallas kernels: 8.2 us -> 10.2 us  [the longest x1 6.76 us: local(): call(outer_kernel, [(3 * LEVELS * ROWS, COLS)], scratch=[(2, 3, 2 * (MARG...]
    ppermute x3, waiting for transfers between devices: 5.55 us -> 3.8 us  [swap_far(): lax.ppermute(values, axis, [(i, (i + 1) % count if i % 2 else (i - 1) % c...]
    unnamed x12 -> x8, local copies, waits for them, and re-layouts: 5.61 us -> 3.87 us
where the time goes in v2:
time: 45.1 us; the launch traced here: 44.7 us
  starting transfers between devices  21 us (47%)
  Pallas kernels  16 us (35%)
  local copies, waits for them, and re-layouts  3.87 us (9%)
  waiting for transfers between devices  3.81 us (8%)
    ppermute x3, starting transfers between devices, swap_far(): lax.ppermute(values, axis, [(i, (i + 1) % count if i % 2 else (i - 1) % c...  9.17 us
    all_to_all x1, starting transfers between devices, local(): lax.all_to_all(packed, 'gy', split_axis=0, concat_axis=0, tiled=True)  6.84 us
    pallas_call x1, Pallas kernels, local(): call(outer_kernel, [(3 * LEVELS * ROWS, COLS)], scratch=[(2, 3, 2 * (MARG...  6.76 us
    pallas_call x1, Pallas kernels, local(): call(inner_kernel, [(STAGES, 2, 3, 2 * HAND) + block, (3, ROWS - 2 * REAC...  5.77 us
    ppermute x3, starting transfers between devices, swap_near(): lax.ppermute(values, axis, [(i, i ^ 1) for i in range(lax.axis_size(axis))])  4.96 us
    unnamed x8, local copies, waits for them, and re-layouts  3.87 us
    ppermute x3, waiting for transfers between devices, swap_far(): lax.ppermute(values, axis, [(i, (i + 1) % count if i % 2 else (i - 1) % c...  3.8 us
    pallas_call x1, Pallas kernels, local(): call(pack_kernel, [(groups, 2, 2) + block, (3, ROWS) + block] + 2 * [(3,...  3.17 us
  transfers between devices with their start and end apart: 7, of which 1 were waited for; matrix products, arithmetic and copies ran while one was open for 0% of the time, Pallas kernels for 14%

profile of v2, /device:TPU:1, one launch (start us, length us, event | category | flops | bytes accessed | tf_op | source)
XLA Modules:
  0.0 44.7 jit_solution(13831830093812587430)
XLA Ops:
  0.0 3.2 %shard_map.64 = (f32[16,2,2,8,128]{4,3,2,1,0:T(8,128)}, f32[3,64,8,128]{3,2,1,0:T(8,128)}, f32[3,18,8,128]{3,2,1,0:T(8,128)}, f32[3,18,8,128]{3,2,1,0:T(8,128)},...) custom-call(f32[2,8,2,1024]{3,2,1,0:T(2,128)} %wind_hbm.1, f32[8,2,1024]{2,1,0:T(2,128)} %temp_hbm.1, ...), custom_call_target="tpu_custom_call" | custom-call | bytes 3000000 | tf_op jit(solution)/shard_map/pallas_call | solution.py:478
  3.2 6.8 %all-to-all-start = ((f32[16,2,2,8,128]{4,3,2,1,0:T(8,128)}), f32[16,2,2,8,128]{4,3,2,1,0:T(8,128)S(1)}, u32[]{:S(2)}, u32[]{:S(2)}) async-start(f32[16,2,2,8,128]{4,3,2,1,0:T(8,128)} %get-tuple-element.18), calls=%async_computation | async-start | bytes 524288 | tf_op jit(solution)/shard_map/all_to_all | solution.py:487
  10.0 0.2 collective-permute-start.2
  10.2 1.6 %collective-permute-start.3 = (f32[3,10,8,128]{3,2,1,0:T(8,128)}, f32[3,10,8,128]{3,2,1,0:T(8,128)S(1)}, u32[]{:S(2)}, u32[]{:S(2)}) collective-permute-start(f32[3,10,8,128]{3,2,1,0:T(8,128)} %get-tuple-element.20), channel_id=1, source_target_pairs={{0,15},{1,2},{2,1},{3,4},{4,3},{5,6},{6,5},{7,8},{8,7},{9,10},{10,... | collective-permute-start | bytes 368648 | tf_op jit(solution)/shard_map/ppermute | solution.py:54
  11.8 2.6 %collective-permute-start = (f32[3,18,8,128]{3,2,1,0:T(8,128)}, f32[3,18,8,128]{3,2,1,0:T(8,128)S(1)}, u32[]{:S(2)}, u32[]{:S(2)}) collective-permute-start(f32[3,18,8,128]{3,2,1,0:T(8,128)} %get-tuple-element.16), channel_id=1, source_target_pairs={{0,16},{16,0},{32,48},{48,32},{64,80},{80,64},{96,112},{112,96},{1... | collective-permute-start | bytes 663560 | tf_op jit(solution)/shard_map/ppermute | solution.py:49
  14.4 3.8 %collective-permute-start.1 = (f32[3,18,8,128]{3,2,1,0:T(8,128)}, f32[3,18,8,128]{3,2,1,0:T(8,128)S(1)}, u32[]{:S(2)}, u32[]{:S(2)}) collective-permute-start(f32[3,18,8,128]{3,2,1,0:T(8,128)} %get-tuple-element.17), channel_id=1, source_target_pairs={{0,112},{16,32},{32,16},{48,64},{64,48},{80,96},{96,80},{112,0},{1... | collective-permute-start | bytes 663560 | tf_op jit(solution)/shard_map/ppermute | solution.py:54
  18.2 0.0 collective-permute-done.2.y_near_ref
  18.3 0.0 collective-permute-done.3.y_far_ref
  18.3 0.0 all-to-all-done
  18.3 0.3 shard_map.65
  18.6 2.2 %collective-permute-start.4 = (f32[27,8,128]{2,1,0:T(8,128)S(1)}, f32[27,8,128]{2,1,0:T(8,128)S(1)}, u32[]{:S(2)}, u32[]{:S(2)}) collective-permute-start(f32[27,8,128]{2,1,0:T(8,128)S(1)} %get-tuple-element.21), channel_id=1, source_target_pairs={{0,16},{16,0},{32,48},{48,32},{64,80},{80,64},{96,112},{112,96},{1... | collective-permute-start | bytes 331784 | tf_op jit(solution)/shard_map/ppermute | solution.py:49
  20.7 3.7 %collective-permute-start.5 = (f32[27,8,128]{2,1,0:T(8,128)S(1)}, f32[27,8,128]{2,1,0:T(8,128)S(1)}, u32[]{:S(2)}, u32[]{:S(2)}) collective-permute-start(f32[27,8,128]{2,1,0:T(8,128)S(1)} %get-tuple-element.22), channel_id=1, source_target_pairs={{0,112},{16,32},{32,16},{48,64},{64,48},{80,96},{96,80},{112,0},{1... | collective-permute-start | bytes 331784 | tf_op jit(solution)/shard_map/ppermute | solution.py:54
  24.5 0.0 copy-start
  24.5 0.9 %copy-done = bf16[256,512]{1,0:T(8,128)(2,1)S(1)} copy-done((bf16[256,512]{1,0:T(8,128)(2,1)S(1)}, bf16[256,512]{1,0:T(8,128)(2,1)}, u32[]{:S(2)}) %copy-start) | copy-done | bytes 262168
  25.4 0.0 copy-start.1
  25.4 0.9 %copy-done.1 = bf16[256,512]{1,0:T(8,128)(2,1)S(1)} copy-done((bf16[256,512]{1,0:T(8,128)(2,1)S(1)}, bf16[256,512]{1,0:T(8,128)(2,1)}, u32[]{:S(2)}) %copy-start.1) | copy-done | bytes 262168
  26.4 1.1 %copy-done.2 = f32[3,64,8,128]{3,2,1,0:T(8,128)S(1)} copy-done((f32[3,64,8,128]{3,2,1,0:T(8,128)S(1)}, f32[3,64,8,128]{3,2,1,0:T(8,128)}, u32[]{:S(2)}) %copy-start.2) | copy-done | bytes 786456
  27.5 0.8 %copy-done.3 = bf16[256,128]{1,0:T(8,128)(2,1)S(1)} copy-done((bf16[256,128]{1,0:T(8,128)(2,1)S(1)}, bf16[256,128]{1,0:T(8,128)(2,1)}, u32[]{:S(2)}) %copy-start.3) | copy-done | bytes 65560
  28.4 5.8 %shard_map.66 = (f32[9,2,3,12,8,128]{5,4,3,2,1,0:T(8,128)S(1)}, f32[3,28,8,128]{3,2,1,0:T(8,128)S(1)}, f32[2,3,32,8,128]{4,3,2,1,0:T(8,128)S(1)}) custom-call(f32[32,2,8,128]{3,2,1,0:T(8,128)S(1)} %bitcast.4, f32[3,64,8,128]{3,2,1,0:T(8,128)S(1)} %copy-done.2, f32[3,10,8,128]{3,2,1,0:T(8,128)S(1)} %collective-permute-done.2.y_near_ref, ...), custom_call_target="tpu_custom_call" | custom-call | bytes 18000000 | tf_op jit(solution)/shard_map/pallas_call | solution.py:497
  34.1 0.0 collective-permute-done.x_near_ref
  34.1 0.0 collective-permute-done.1.x_far_ref
  34.2 0.0 collective-permute-done.4.s_near_ref
  34.2 3.8 %collective-permute-done.5.s_far_ref = f32[27,8,128]{2,1,0:T(8,128)S(1)} collective-permute-done((f32[27,8,128]{2,1,0:T(8,128)S(1)}, f32[27,8,128]{2,1,0:T(8,128)S(1)}, u32[]{:S(2)}, u32[]{:S(2)}) %collective-permute-start.5) | collective-permute-done | bytes 110624 | tf_op jit(solution)/shard_map/ppermute | solution.py:54
  38.0 6.8 %shard_map.67 = f32[1536,128]{1,0:T(8,128)} custom-call(f32[3,18,8,128]{3,2,1,0:T(8,128)S(1)} %collective-permute-done.x_near_ref, f32[3,18,8,128]{3,2,1,0:T(8,128)S(1)} %collective-permute-done.1.x_far_ref, f32[27,8,128]{2,1,0:T(8,128)S(1)} %collective-permute-done.4.s_near_ref, f32[27,8,128]{2,1,0:T(8,128)S(1)} %collective-permute-done.5.s_far_ref, ...), custom_call_target="tpu_custom_call" | custom-call | bytes 18000000 | tf_op jit(solution)/shard_map/pallas_call | solution.py:503
  (2 shorter events, 0.0 us)
Async XLA Ops:
  3.2 15.1 %all-to-all-start = ((f32[16,2,2,8,128]{4,3,2,1,0:T(8,128)}), f32[16,2,2,8,128]{4,3,2,1,0:T(8,128)S(1)}, u32[]{:S(2)}, u32[]{:S(2)}) async-start(f32[16,2,2,8,128]{4,3,2,1,0:T(8,128)} %get-tuple-element.18), calls=%async_computation | async-start | bytes 524288 | tf_op jit(solution)/shard_map/all_to_all | solution.py:487
  10.0 8.2 %collective-permute-start.2 = (f32[3,10,8,128]{3,2,1,0:T(8,128)}, f32[3,10,8,128]{3,2,1,0:T(8,128)S(1)}, u32[]{:S(2)}, u32[]{:S(2)}) collective-permute-start(f32[3,10,8,128]{3,2,1,0:T(8,128)} %get-tuple-element.19), channel_id=1, source_target_pairs={{0,1},{1,0},{2,3},{3,2},{4,5},{5,4},{6,7},{7,6},{8,9},{9,8},{10,11... | collective-permute-start | bytes 368648 | tf_op jit(solution)/shard_map/ppermute | solution.py:49
  10.2 8.1 %collective-permute-start.3 = (f32[3,10,8,128]{3,2,1,0:T(8,128)}, f32[3,10,8,128]{3,2,1,0:T(8,128)S(1)}, u32[]{:S(2)}, u32[]{:S(2)}) collective-permute-start(f32[3,10,8,128]{3,2,1,0:T(8,128)} %get-tuple-element.20), channel_id=1, source_target_pairs={{0,15},{1,2},{2,1},{3,4},{4,3},{5,6},{6,5},{7,8},{8,7},{9,10},{10,... | collective-permute-start | bytes 368648 | tf_op jit(solution)/shard_map/ppermute | solution.py:54
  11.8 22.3 %collective-permute-start = (f32[3,18,8,128]{3,2,1,0:T(8,128)}, f32[3,18,8,128]{3,2,1,0:T(8,128)S(1)}, u32[]{:S(2)}, u32[]{:S(2)}) collective-permute-start(f32[3,18,8,128]{3,2,1,0:T(8,128)} %get-tuple-element.16), channel_id=1, source_target_pairs={{0,16},{16,0},{32,48},{48,32},{64,80},{80,64},{96,112},{112,96},{1... | collective-permute-start | bytes 663560 | tf_op jit(solution)/shard_map/ppermute | solution.py:49
  14.4 19.7 %collective-permute-start.1 = (f32[3,18,8,128]{3,2,1,0:T(8,128)}, f32[3,18,8,128]{3,2,1,0:T(8,128)S(1)}, u32[]{:S(2)}, u32[]{:S(2)}) collective-permute-start(f32[3,18,8,128]{3,2,1,0:T(8,128)} %get-tuple-element.17), channel_id=1, source_target_pairs={{0,112},{16,32},{32,16},{48,64},{64,48},{80,96},{96,80},{112,0},{1... | collective-permute-start | bytes 663560 | tf_op jit(solution)/shard_map/ppermute | solution.py:54
  18.6 15.6 %collective-permute-start.4 = (f32[27,8,128]{2,1,0:T(8,128)S(1)}, f32[27,8,128]{2,1,0:T(8,128)S(1)}, u32[]{:S(2)}, u32[]{:S(2)}) collective-permute-start(f32[27,8,128]{2,1,0:T(8,128)S(1)} %get-tuple-element.21), channel_id=1, source_target_pairs={{0,16},{16,0},{32,48},{48,32},{64,80},{80,64},{96,112},{112,96},{1... | collective-permute-start | bytes 331784 | tf_op jit(solution)/shard_map/ppermute | solution.py:49
  20.7 17.2 %collective-permute-start.5 = (f32[27,8,128]{2,1,0:T(8,128)S(1)}, f32[27,8,128]{2,1,0:T(8,128)S(1)}, u32[]{:S(2)}, u32[]{:S(2)}) collective-permute-start(f32[27,8,128]{2,1,0:T(8,128)S(1)} %get-tuple-element.22), channel_id=1, source_target_pairs={{0,112},{16,32},{32,16},{48,64},{64,48},{80,96},{96,80},{112,0},{1... | collective-permute-start | bytes 331784 | tf_op jit(solution)/shard_map/ppermute | solution.py:54
  24.5 0.9 %copy-start = (bf16[256,512]{1,0:T(8,128)(2,1)S(1)}, bf16[256,512]{1,0:T(8,128)(2,1)}, u32[]{:S(2)}) copy-start(bf16[256,512]{1,0:T(8,128)(2,1)} %constant.6.clone.east_table_ref) | copy-start | bytes 786436
  25.4 0.9 %copy-start.1 = (bf16[256,512]{1,0:T(8,128)(2,1)S(1)}, bf16[256,512]{1,0:T(8,128)(2,1)}, u32[]{:S(2)}) copy-start(bf16[256,512]{1,0:T(8,128)(2,1)} %constant.7.clone.north_table_ref) | copy-start | bytes 786436
  26.4 1.1 %copy-start.2 = (f32[3,64,8,128]{3,2,1,0:T(8,128)S(1)}, f32[3,64,8,128]{3,2,1,0:T(8,128)}, u32[]{:S(2)}) copy-start(f32[3,64,8,128]{3,2,1,0:T(8,128)} %get-tuple-element.23.tile_ref) | copy-start | bytes 2359300
  27.5 0.8 %copy-start.3 = (bf16[256,128]{1,0:T(8,128)(2,1)S(1)}, bf16[256,128]{1,0:T(8,128)(2,1)}, u32[]{:S(2)}) copy-start(bf16[256,128]{1,0:T(8,128)(2,1)} %constant.8.clone.table_ref) | copy-start | bytes 196612

commit v3 on v2

--- a/solution.py
+++ b/solution.py
@@ -1,7 +1,5 @@
 import jax
 import jax.numpy as jnp
-import ml_dtypes
-import numpy as np
 from jax import lax
 from jax.experimental import pallas as pl
 from jax.experimental.pallas import tpu as pltpu
@@ -193,7 +191,7 @@
     return jnp.where(lane >= RIM - REACH, right, own)
 
 
-def products(blocks, table_ref):
+def products(blocks, table):
     counts = [block.shape[0] * LEVELS for block in blocks]
     values = jnp.concatenate(
         [block.reshape(count, COLS) for block, count in zip(blocks, counts)], axis=0
@@ -201,7 +199,9 @@
     high = values.astype(jnp.bfloat16)
     low = (values - high.astype(F32)).astype(jnp.bfloat16)
     result = jnp.dot(
-        jnp.concatenate((high, low), axis=1), table_ref[...], preferred_element_type=F32
+        jnp.concatenate((high, low), axis=1),
+        jnp.concatenate((table, table), axis=0),
+        preferred_element_type=F32,
     )
     pieces, start = [], 0
     for count in counts:
@@ -210,8 +210,8 @@
     return pieces
 
 
-def stage_products(jobs, table_ref):
-    return products([rows[2:-2] for source, _, _, _ in jobs for rows in source], table_ref)
+def stage_products(jobs, table):
+    return products([rows[2:-2] for source, _, _, _ in jobs for rows in source], table)
 
 
 def stage_sums(jobs, across, stage):
@@ -238,10 +238,10 @@
             store(f, moved)
 
 
-def refine_tables(values, east_table_ref, north_table_ref, store):
+def refine_columns(values, east_table, north_table, store):
     n = values.shape[0]
-    (first,) = products([values[:, 0]], east_table_ref)
-    (second,) = products([values[:, 1]], north_table_ref)
+    (first,) = products([values[:, 0]], east_table)
+    (second,) = products([values[:, 1]], north_table)
     warm = first[:, 2 * COLS :] + second[:, 2 * COLS :]
     for k in range(2):
         cut = slice(COLS * k, COLS * (k + 1))
@@ -254,32 +254,11 @@
     return jnp.where(lane >= COLS - REACH, roll(rim, COLS - 2 * REACH - RIGHT), value)
 
 
-def inner_kernel(
-    coarse_ref, tile_ref, y_near_ref, y_far_ref, east_table_ref, north_table_ref, table_ref,
-    edges_ref, inside_ref, refined_ref, background, state, first, second,
-):
+def compose_kernel(tile_ref, y_near_ref, y_far_ref, state_ref):
     y_odd = parity("gy")
     lane = lanes()
-
-    def keep(k, f, start):
-        def store(values):
-            refined_ref[k, f, start : start + values.shape[0]] = values
-
-        return store
-
-    for start in range(0, CROWS, CHUNK):
-        refine_tables(
-            coarse_ref[start : start + CHUNK],
-            east_table_ref,
-            north_table_ref,
-            lambda k, f, values, start=start: keep(k, f, start)(values),
-        )
-    for k in range(2):
-        for f in range(3):
-            refine_rows(refined_ref, k, f, 0, CROWS, background, 0)
-
     take_near = (lane >= RIGHT).astype(jnp.int32) == 1 - y_odd
-    state[0] = tile_ref[...]
+    state_ref[0] = tile_ref[...]
     for row, count, register, slot in slots():
         near_shift = lax.rem((1 - y_odd) * (RIM - REACH) - REACH * slot + COLS, COLS)
         far_shift = lax.rem(y_odd * (RIM - REACH) - REACH * slot + COLS, COLS)
@@ -287,10 +266,30 @@
             near = roll(y_near_ref[f, register : register + count], near_shift)
             far = roll(y_far_ref[f, register : register + count], far_shift)
             halo = jnp.where(take_near, near, far)
-            state[1, f, row : row + count] = rim_of(tile_ref[f, row : row + count], halo, halo, lane)
-
-    buffers = (state, first, second, state)
+            main = tile_ref[f, row : row + count]
+            state_ref[1, f, row : row + count] = rim_of(main, halo, halo, lane)
+
+
+def inner_kernel(
+    coarse_ref, start_ref, edges_ref, inside_ref, refined_ref,
+    background, state, first, second,
+):
+    lane = lanes()
+    east_table, north_table, table = refine_table(0), refine_table(1), difference_table()
+
+    for start in range(0, CROWS, CHUNK):
+
+        def keep(k, f, values, start=start):
+            refined_ref[k, f, start : start + CHUNK] = values
+
+        refine_columns(coarse_ref[start : start + CHUNK], east_table, north_table, keep)
+    for k in range(2):
+        for f in range(3):
+            refine_rows(refined_ref, k, f, 0, CROWS, background, 0)
+
     for s in range(STAGES):
+        origin = start_ref if s < 3 else state
+        buffers = (origin, first, second, state)
         source, target = buffers[s % 3], buffers[s % 3 + 1]
         for c in range(2):
             for f in range(3):
@@ -307,11 +306,11 @@
 
                 jobs.append((
                     [source[c, f, start - 2 : stop + 2] for f in range(3)],
-                    [state[c, f, start:stop] for f in range(3)],
+                    [origin[c, f, start:stop] for f in range(3)],
                     [background[c, f, start:stop] for f in range(3)],
                     store,
                 ))
-            stage_sums(jobs, stage_products(jobs, table_ref), s % 3)
+            stage_sums(jobs, stage_products(jobs, table), s % 3)
     for f in range(3):
         rows = slice(REACH, ROWS - REACH)
         inside_ref[f] = merged(state[0, f, rows], state[1, f, rows], lane)
@@ -328,148 +327,149 @@
         background[k, f, first + 2 * i + 2] = even[i]
 
 
-def outer_kernel(
-    x_near_ref, x_far_ref, s_near_ref, s_far_ref, edges_ref, inside_ref, refined_ref,
-    east_table_ref, north_table_ref, table_ref, out_ref, refined, background, state, first, second,
+def outer_end(
+    side, main_ref, message_ref, edges_ref, refined_ref, refined, background, state, first, second
 ):
-    x_odd = parity("gx")
     lane = lanes()
+    east_table, north_table, table = refine_table(0), refine_table(1), difference_table()
     own = MARGIN + HROWS
     for k in range(2):
         for f in range(3):
-            refined[k, f, HROWS:own] = refined_ref[k, f, 0:MARGIN]
-            refined[k, f, own : own + MARGIN] = refined_ref[k, f, CROWS - MARGIN : CROWS]
-    for ref, high in ((s_near_ref, 1 - x_odd), (s_far_ref, x_odd)):
-
-        def store(k, f, values, high=high):
-            refined[k, f, pl.ds(high * (own + MARGIN), HROWS)] = values
-
-        values = ref[: 2 * HROWS].reshape(HROWS, 2, LEVELS, COLS)
-        refine_tables(values, east_table_ref, north_table_ref, store)
-    for side in range(2):
-        for k in range(2):
-            for f in range(3):
-                refine_rows(refined, k, f, own * side, own, background.at[side], 0)
-
-    for main_ref, ref, high in ((x_near_ref, s_near_ref, 1 - x_odd), (x_far_ref, s_far_ref, x_odd)):
-        for f in range(3):
-            state[high, 0, f, pl.ds(high * REACH, REACH)] = main_ref[f]
-            for away in range(REACH):
-                row = REACH - 1 - away + high * (2 * away - REACH + 1)
-                main = main_ref[f, row]
-                halo = []
-                for right in range(2):
-                    register, start, offset = corner_slot(min(away, REACH - 2), right)
-                    values = ref[2 * HROWS + CREGS * f + register]
-                    halo.append(roll(values, (RIM - REACH) * right - start - offset))
-                state[high, 1, f, high * REACH + row] = rim_of(main, halo[0], halo[1], lane)
+            refined[k, f, pl.ds((1 - side) * HROWS, MARGIN)] = refined_ref[
+                k, f, pl.ds(side * (CROWS - MARGIN), MARGIN)
+            ]
+
+    def keep(k, f, values):
+        refined[k, f, pl.ds(side * MARGIN, HROWS)] = values
+
+    values = message_ref[: 2 * HROWS].reshape(HROWS, 2, LEVELS, COLS)
+    refine_columns(values, east_table, north_table, keep)
+    for k in range(2):
+        for f in range(3):
+            refine_rows(refined, k, f, 0, own, background, 0)
+
+    halo = side * (REACH + HAND)
+    for f in range(3):
+        state[0, f, pl.ds(halo, REACH)] = main_ref[f]
+        for away in range(REACH):
+            row = REACH - 1 - away + side * (2 * away - REACH + 1)
+            sides = []
+            for right in range(2):
+                register, start, offset = corner_slot(min(away, REACH - 2), right)
+                corner = message_ref[2 * HROWS + CREGS * f + register]
+                sides.append(roll(corner, (RIM - REACH) * right - start - offset))
+            state[1, f, halo + row] = rim_of(main_ref[f, row], sides[0], sides[1], lane)
 
     buffers = (state, first, second, state)
 
-    def jobs_of(side, s):
+    def job_of(c, s):
         source, target = buffers[s % 3], buffers[s % 3 + 1]
-        origin = s - s % 3
-        jobs = []
-        for c in range(2):
-            if side == 0:
-                low = 2 * (s + 1)
-                rows = [
-                    jnp.concatenate((source[0, c, f, low - 2 : REACH + 2 * s], edges_ref[s, c, f, :4]))
-                    for f in range(3)
-                ]
-                base = [
-                    jnp.concatenate((
-                        state[0, c, f, low : REACH + 2 * origin],
-                        edges_ref[origin, c, f, : low - 2 * origin],
-                    ))
-                    for f in range(3)
-                ]
-            else:
-                low = REACH - 2 * (s + 1)
-                rows = [
-                    jnp.concatenate((
-                        edges_ref[s, c, f, 2 * HAND - 4 :],
-                        source[1, c, f, REACH - 2 * s : 2 * REACH - 2 * s],
-                    ))
-                    for f in range(3)
-                ]
-                base = [
-                    jnp.concatenate((
-                        edges_ref[origin, c, f, 2 * HAND - (REACH - 2 * origin - low) :],
-                        state[1, c, f, REACH - 2 * origin : low + REACH],
-                    ))
-                    for f in range(3)
-                ]
-
-            def store(f, values, c=c):
-                target[side, c, f, low : low + REACH] = values
-
-            start = low + 2 * side
-            near = [background[side, c, f, start : start + REACH] for f in range(3)]
-            jobs.append((rows, base, near, store))
-        return jobs
+        low = 2 * (s + 1) + side * (REACH + 2 - 4 * s)
+        handed = REACH + 2 * s - side * 4 * s
+        for f in range(3):
+            source[c, f, pl.ds(handed, HAND)] = edges_ref[s, c, f, pl.ds(side * HAND, HAND)]
+
+        def store(f, values):
+            target[c, f, pl.ds(low, REACH)] = values
+
+        return (
+            [source[c, f, pl.ds(low - 2, REACH + 4)] for f in range(3)],
+            [state[c, f, pl.ds(low, REACH)] for f in range(3)],
+            [background[c, f, pl.ds(low - 4 * side, REACH)] for f in range(3)],
+            store,
+        )
 
     waiting = [None, None]
     for s in range(STAGES + 1):
-        for side in range(2):
-            if waiting[side] is not None:
-                stage_sums(waiting[side][0], waiting[side][1], (s - 1) % 3)
+        for c in range(2):
+            if waiting[c] is not None:
+                stage_sums(waiting[c][0], waiting[c][1], (s - 1) % 3)
             if s < STAGES:
-                jobs = jobs_of(side, s)
-                waiting[side] = (jobs, stage_products(jobs, table_ref))
-
+                jobs = [job_of(c, s)]
+                waiting[c] = (jobs, stage_products(jobs, table))
+    rows = pl.ds(REACH - 2 * HAND * side, REACH)
+    return [merged(state[0, f, rows], state[1, f, rows], lane) for f in range(3)]
+
+
+def near_end_kernel(
+    main_ref, message_ref, edges_ref, refined_ref, end_ref, refined, background, state, first, second
+):
+    side = 1 - parity("gx")
+    ends = outer_end(
+        side, main_ref, message_ref, edges_ref, refined_ref, refined, background, state, first, second
+    )
     for f in range(3):
-        for side, start in ((0, 0), (1, ROWS - REACH)):
-            rows = slice(REACH * (1 - side), REACH * (1 - side) + REACH)
-            values = merged(state[side, 0, f, rows], state[side, 1, f, rows], lane)
-            for row in range(REACH):
-                out_ref[pl.ds(f * LEVELS * ROWS + start + row, LEVELS, stride=ROWS), :] = values[row]
+        end_ref[f] = ends[f]
+
+
+def far_end_kernel(
+    main_ref, message_ref, edges_ref, refined_ref, near_ref, inside_ref, out_ref,
+    refined, background, state, first, second,
+):
+    side = parity("gx")
+    for f in range(3):
         for row in range(ROWS - 2 * REACH):
             at = f * LEVELS * ROWS + REACH + row
             out_ref[pl.ds(at, LEVELS, stride=ROWS), :] = inside_ref[f, row]
+        for row in range(REACH):
+            at = f * LEVELS * ROWS + row + (1 - side) * (ROWS - REACH)
+            out_ref[pl.ds(at, LEVELS, stride=ROWS), :] = near_ref[f, row]
+    ends = outer_end(
+        side, main_ref, message_ref, edges_ref, refined_ref, refined, background, state, first, second
+    )
+    for f in range(3):
+        for row in range(REACH):
+            at = f * LEVELS * ROWS + row + side * (ROWS - REACH)
+            out_ref[pl.ds(at, LEVELS, stride=ROWS), :] = ends[f][row]
+
+
+def refine_table(north):
+    row = lax.broadcasted_iota(jnp.int32, (COLS, 2 * COLS), 0)
+    lane = lax.broadcasted_iota(jnp.int32, (COLS, 2 * COLS), 1)
+    rim = lane - COLS
+    column = jnp.where(rim < RIGHT, rim - REACH, rim - RIGHT + COLS - 2 * REACH)
+    column = jnp.where(lane < COLS, lane, column)
+    centre = lax.shift_right_arithmetic(column, 1) + MARGIN
+    side = centre - 1 + 2 * (column & 1)
+
+    def weights(window, used):
+        weight = jnp.where(window == centre, 0.75, jnp.where(window == side, 0.25, 0.0))
+        return jnp.where(used & (rim < RIM), weight, 0.0).astype(jnp.bfloat16)
+
+    wind = weights(row, row < WINDOW)
+    warm = weights(row - WINDOW + HALF * north, (row >= WINDOW) & (row < WINDOW + HALF))
+    return jnp.concatenate((wind, warm), axis=1)
 
 
 def difference_table():
-    table = np.zeros((COLS, COLS), np.float32)
-    for j in range(COLS):
-        for offset, weight in ((1, 8.0), (-1, -8.0), (2, -1.0), (-2, 1.0)):
-            table[(j + offset) % COLS, j] = weight
-    return np.concatenate((table, table), axis=0).astype(ml_dtypes.bfloat16)
-
-
-def tables():
-    columns = np.full((2 * COLS,), -1000)
-    columns[:COLS] = np.arange(COLS)
-    columns[COLS : COLS + RIGHT] = np.arange(RIGHT) - REACH
-    columns[COLS + RIGHT : COLS + RIM] = np.arange(RIGHT) + COLS - 2 * REACH
-    window = np.zeros((WINDOW, 2 * COLS), np.float32)
-    for j, column in enumerate(columns):
-        if column > -1000:
-            centre = column // 2 + MARGIN
-            window[centre, j] = 0.75
-            window[centre - 1 + 2 * (column % 2), j] = 0.25
-    pair = []
-    for part in (window[:HALF], window[HALF:]):
-        table = np.zeros((COLS, 4 * COLS), np.float32)
-        table[:WINDOW, : 2 * COLS] = window
-        table[WINDOW : WINDOW + HALF, 2 * COLS :] = part
-        pair.append(np.concatenate((table, table), axis=0).astype(ml_dtypes.bfloat16))
-    return pair
-
-
-def call(kernel, outputs, scratch=(), limit=48, microseconds=1, copies=0):
-    specs = {"in_specs": [pl.BlockSpec(memory_space=pltpu.HBM)] * copies} if copies else {}
-    return pl.pallas_call(
-        kernel,
-        out_shape=[jax.ShapeDtypeStruct(shape, F32) for shape in outputs],
-        **specs,
-        scratch_shapes=[pltpu.VMEM(shape, F32) for shape in scratch]
-        + ([pltpu.SemaphoreType.DMA((copies,))] if copies else []),
-        compiler_params=pltpu.CompilerParams(vmem_limit_bytes=limit * 2**20),
-        cost_estimate=pl.CostEstimate(
-            flops=0, bytes_accessed=3_000_000 * microseconds, transcendentals=0
-        ),
-    )
+    source = lax.broadcasted_iota(jnp.int32, (COLS, COLS), 0)
+    lane = lax.broadcasted_iota(jnp.int32, (COLS, COLS), 1)
+    ahead = (source - lane) & (COLS - 1)
+    table = jnp.where(ahead == 1, 8.0, 0.0) - jnp.where(ahead == COLS - 1, 8.0, 0.0)
+    table = table - jnp.where(ahead == 2, 1.0, 0.0) + jnp.where(ahead == COLS - 2, 1.0, 0.0)
+    return table.astype(jnp.bfloat16)
+
+
+def call(
+    kernel, outputs, scratch=(), limit=48, microseconds=1, fetched=(), sent=False, semaphores=0
+):
+    here, there = pl.BlockSpec(memory_space=pltpu.VMEM), pl.BlockSpec(memory_space=pltpu.HBM)
+
+    def run(*operands):
+        return pl.pallas_call(
+            kernel,
+            out_shape=[jax.ShapeDtypeStruct(shape, F32) for shape in outputs],
+            in_specs=[there if i in fetched else here for i in range(len(operands))],
+            out_specs=[there if sent else here] * len(outputs),
+            scratch_shapes=[pltpu.VMEM(shape, F32) for shape in scratch]
+            + ([pltpu.SemaphoreType.DMA((semaphores,))] if semaphores else []),
+            compiler_params=pltpu.CompilerParams(vmem_limit_bytes=limit * 2**20),
+            cost_estimate=pl.CostEstimate(
+                flops=0, bytes_accessed=3_000_000 * microseconds, transcendentals=0
+            ),
+        )(*operands)
+
+    return run
 
 
 def local(les_wind, les_temp, acoustic_start):
@@ -481,32 +481,33 @@
         + 2 * [(3, REACH) + block]
         + 2 * [(3, SIDE) + block],
         scratch=[les_wind.shape, les_temp.shape, (3 * LEVELS * ROWS, COLS)],
-        copies=3,
+        fetched=(0, 1, 2),
+        semaphores=3,
         limit=PACK_LIMIT,
     )(les_wind, les_temp, acoustic_start.reshape(3 * LEVELS * ROWS, COLS))
     coarse = lax.all_to_all(packed, "gy", split_axis=0, concat_axis=0, tiled=True)
     coarse = coarse.reshape((CROWS, 2) + block)
+    x_near, x_far = swap_near(x_near, "gx"), swap_far(x_far, "gx")
     y_near, y_far = swap_near(y_near, "gy"), swap_far(y_far, "gy")
-    x_near, x_far = swap_near(x_near, "gx"), swap_far(x_far, "gx")
     s_near, s_far = call(second_pack_kernel, 2 * [(2 * HROWS + 3 * CREGS,) + block])(
         coarse, y_near, y_far
     )
     s_near, s_far = swap_near(s_near, "gx"), swap_far(s_far, "gx")
-    east_table, north_table = (jnp.asarray(table) for table in tables())
-    table = jnp.asarray(difference_table())
+    (state,) = call(compose_kernel, [(2, 3, ROWS) + block])(tile, y_near, y_far)
     edges, inside, refined = call(
         inner_kernel,
         [(STAGES, 2, 3, 2 * HAND) + block, (3, ROWS - 2 * REACH) + block, (2, 3, CROWS) + block],
         scratch=4 * [(2, 3, ROWS) + block],
         microseconds=6,
-    )(coarse, tile, y_near, y_far, east_table, north_table, table)
-    (end,) = call(
-        outer_kernel,
-        [(3 * LEVELS * ROWS, COLS)],
-        scratch=[(2, 3, 2 * (MARGIN + HROWS)) + block, (2, 2, 3, 2 * (MARGIN + HROWS)) + block]
-        + 3 * [(2, 2, 3, 2 * REACH) + block],
-        microseconds=6,
-    )(x_near, x_far, s_near, s_far, edges, inside, refined, east_table, north_table, table)
+    )(coarse, state)
+    scratch = [(2, 3, MARGIN + HROWS) + block, (2, 3, 2 * (MARGIN + HROWS)) + block]
+    scratch += 3 * [(2, 3, REACH + REACH + HAND) + block]
+    (near,) = call(near_end_kernel, [(3, REACH) + block], scratch=scratch, microseconds=3)(
+        x_near, s_near, edges, refined
+    )
+    (end,) = call(far_end_kernel, [(3 * LEVELS * ROWS, COLS)], scratch=scratch, microseconds=3)(
+        x_far, s_far, edges, refined, near, inside
+    )
     return end.reshape(acoustic_start.shape)
 
 

time: 45.1 us -> 43.3 us (0.960)
  Pallas kernels: 16 us -> 19 us
  local copies, waits for them, and re-layouts: 3.87 us -> 1.13 us
  waiting for transfers between devices: 3.81 us -> 1.85 us
    pallas_call x4 -> x6, Pallas kernels: 16 us -> 19 us  [run(): pl.pallas_call(kernel, out_shape=[jax.ShapeDtypeStruct(shape, F32) for sh...]
    unnamed x8 -> x2, local copies, waits for them, and re-layouts: 3.87 us -> 1.13 us
    ppermute x3, waiting for transfers between devices: 3.8 us -> 1.27 us  [swap_far(): lax.ppermute(values, axis, [(i, (i + 1) % count if i % 2 else (i - 1) % c...]
    ppermute x3, waiting for transfers between devices: 0.01 us -> 0.58 us  [swap_near(): lax.ppermute(values, axis, [(i, i ^ 1) for i in range(lax.axis_size(axis))])]
  transfers between devices with their start and end apart: 7 -> 7, of which waited for: 1 -> 2; matrix products, arithmetic and copies ran while one was open for 0% -> 0% of each run, Pallas kernels for 14% -> 25%
where the time goes in v3:
time: 43.3 us; the launch traced here: 43 us
  starting transfers between devices  21 us (48%)
  Pallas kernels  19 us (44%)
  waiting for transfers between devices  1.85 us (4%)
  local copies, waits for them, and re-layouts  1.13 us (3%)
    pallas_call x6, Pallas kernels, run(): pl.pallas_call(kernel, out_shape=[jax.ShapeDtypeStruct(shape, F32) for sh...  19 us
    ppermute x3, starting transfers between devices, swap_far(): lax.ppermute(values, axis, [(i, (i + 1) % count if i % 2 else (i - 1) % c...  9.17 us
    all_to_all x1, starting transfers between devices, local(): lax.all_to_all(packed, 'gy', split_axis=0, concat_axis=0, tiled=True)  6.84 us
    ppermute x3, starting transfers between devices, swap_near(): lax.ppermute(values, axis, [(i, i ^ 1) for i in range(lax.axis_size(axis))])  4.96 us
    ppermute x3, waiting for transfers between devices, swap_far(): lax.ppermute(values, axis, [(i, (i + 1) % count if i % 2 else (i - 1) % c...  1.27 us
    unnamed x2, local copies, waits for them, and re-layouts  1.13 us
  transfers between devices with their start and end apart: 7, of which 2 were waited for; matrix products, arithmetic and copies ran while one was open for 0% of the time, Pallas kernels for 25%

profile of v3, /device:TPU:1, one launch (start us, length us, event | category | flops | bytes accessed | tf_op | source)
XLA Modules:
  0.0 43.0 jit_solution(3610059627913766939)
XLA Ops:
  0.0 3.2 %shard_map.37 = (f32[16,2,2,8,128]{4,3,2,1,0:T(8,128)}, f32[3,64,8,128]{3,2,1,0:T(8,128)}, f32[3,18,8,128]{3,2,1,0:T(8,128)}, f32[3,18,8,128]{3,2,1,0:T(8,128)},...) custom-call(f32[2,8,2,1024]{3,2,1,0:T(2,128)} %wind_hbm.1, f32[8,2,1024]{2,1,0:T(2,128)} %temp_hbm.1, ...), custom_call_target="tpu_custom_call" | custom-call | bytes 3000000 | tf_op jit(solution)/shard_map/pallas_call | solution.py:459
  3.2 6.8 %all-to-all-start = ((f32[16,2,2,8,128]{4,3,2,1,0:T(8,128)}), f32[16,2,2,8,128]{4,3,2,1,0:T(8,128)S(1)}, u32[]{:S(2)}, u32[]{:S(2)}) async-start(f32[16,2,2,8,128]{4,3,2,1,0:T(8,128)} %get-tuple-element.17), calls=%async_computation | async-start | bytes 524288 | tf_op jit(solution)/shard_map/all_to_all | solution.py:488
  10.0 0.2 collective-permute-start.1
  10.2 1.6 %collective-permute-start.2 = (f32[3,10,8,128]{3,2,1,0:T(8,128)}, f32[3,10,8,128]{3,2,1,0:T(8,128)S(1)}, u32[]{:S(2)}, u32[]{:S(2)}) collective-permute-start(f32[3,10,8,128]{3,2,1,0:T(8,128)} %get-tuple-element.19), channel_id=1, source_target_pairs={{0,15},{1,2},{2,1},{3,4},{4,3},{5,6},{6,5},{7,8},{8,7},{9,10},{10,... | collective-permute-start | bytes 368648 | tf_op jit(solution)/shard_map/ppermute | solution.py:52
  11.8 2.6 %collective-permute-start.4 = (f32[3,18,8,128]{3,2,1,0:T(8,128)}, f32[3,18,8,128]{3,2,1,0:T(8,128)S(1)}, u32[]{:S(2)}, u32[]{:S(2)}) collective-permute-start(f32[3,18,8,128]{3,2,1,0:T(8,128)} %get-tuple-element.24), channel_id=1, source_target_pairs={{0,16},{16,0},{32,48},{48,32},{64,80},{80,64},{96,112},{112,96},{1... | collective-permute-start | bytes 663560 | tf_op jit(solution)/shard_map/ppermute | solution.py:47
  14.4 3.8 %collective-permute-start = (f32[3,18,8,128]{3,2,1,0:T(8,128)}, f32[3,18,8,128]{3,2,1,0:T(8,128)S(1)}, u32[]{:S(2)}, u32[]{:S(2)}) collective-permute-start(f32[3,18,8,128]{3,2,1,0:T(8,128)} %get-tuple-element.16), channel_id=1, source_target_pairs={{0,112},{16,32},{32,16},{48,64},{64,48},{80,96},{96,80},{112,0},{1... | collective-permute-start | bytes 663560 | tf_op jit(solution)/shard_map/ppermute | solution.py:52
  18.2 0.0 collective-permute-done.1.y_near_ref
  18.2 0.0 collective-permute-done.2.y_far_ref
  18.2 0.0 all-to-all-done
  18.3 0.3 shard_map.38
  18.6 2.2 %collective-permute-start.5 = (f32[27,8,128]{2,1,0:T(8,128)S(1)}, f32[27,8,128]{2,1,0:T(8,128)S(1)}, u32[]{:S(2)}, u32[]{:S(2)}) collective-permute-start(f32[27,8,128]{2,1,0:T(8,128)S(1)} %get-tuple-element.25), channel_id=1, source_target_pairs={{0,16},{16,0},{32,48},{48,32},{64,80},{80,64},{96,112},{112,96},{1... | collective-permute-start | bytes 331784 | tf_op jit(solution)/shard_map/ppermute | solution.py:47
  20.7 3.7 %collective-permute-start.3 = (f32[27,8,128]{2,1,0:T(8,128)S(1)}, f32[27,8,128]{2,1,0:T(8,128)S(1)}, u32[]{:S(2)}, u32[]{:S(2)}) collective-permute-start(f32[27,8,128]{2,1,0:T(8,128)S(1)} %get-tuple-element.20), channel_id=1, source_target_pairs={{0,112},{16,32},{32,16},{48,64},{64,48},{80,96},{96,80},{112,0},{1... | collective-permute-start | bytes 331784 | tf_op jit(solution)/shard_map/ppermute | solution.py:52
  24.5 0.0 copy-start
  24.5 1.1 %copy-done = f32[3,64,8,128]{3,2,1,0:T(8,128)S(1)} copy-done((f32[3,64,8,128]{3,2,1,0:T(8,128)S(1)}, f32[3,64,8,128]{3,2,1,0:T(8,128)}, u32[]{:S(2)}) %copy-start) | copy-done | bytes 786456
  25.6 0.9 %shard_map.39.start_ref = f32[2,3,64,8,128]{4,3,2,1,0:T(8,128)S(1)} custom-call(f32[3,64,8,128]{3,2,1,0:T(8,128)S(1)} %copy-done, f32[3,10,8,128]{3,2,1,0:T(8,128)S(1)} %collective-permute-done.1.y_near_ref, f32[3,10,8,128]{3,2,1,0:T(8,128)S(1)} %collective-permute-done.2.y_far_ref), custom_call_target="tpu_custom_call" | custom-call | bytes 3000000 | tf_op jit(solution)/shard_map/pallas_call | solution.py:459
  26.5 5.7 %shard_map.40 = (f32[9,2,3,12,8,128]{5,4,3,2,1,0:T(8,128)S(1)}, f32[3,28,8,128]{3,2,1,0:T(8,128)S(1)}, f32[2,3,32,8,128]{4,3,2,1,0:T(8,128)S(1)}) custom-call(f32[32,2,8,128]{3,2,1,0:T(8,128)S(1)} %bitcast.4, f32[2,3,64,8,128]{4,3,2,1,0:T(8,128)S(1)} %shard_map.39.start_ref), custom_call_target="tpu_custom_call" | custom-call | bytes 18000000 | tf_op jit(solution)/shard_map/pallas_call | solution.py:459
  32.2 0.0 collective-permute-done.4.main_ref
  32.3 0.6 %collective-permute-done.5.message_ref = f32[27,8,128]{2,1,0:T(8,128)S(1)} collective-permute-done((f32[27,8,128]{2,1,0:T(8,128)S(1)}, f32[27,8,128]{2,1,0:T(8,128)S(1)}, u32[]{:S(2)}, u32[]{:S(2)}) %collective-permute-start.5) | collective-permute-done | bytes 110624 | tf_op jit(solution)/shard_map/ppermute | solution.py:47
  32.8 3.9 %shard_map.41.near_ref = f32[3,18,8,128]{3,2,1,0:T(8,128)S(1)} custom-call(f32[3,18,8,128]{3,2,1,0:T(8,128)S(1)} %collective-permute-done.4.main_ref, f32[27,8,128]{2,1,0:T(8,128)S(1)} %collective-permute-done.5.message_ref, f32[9,2,3,12,8,128]{5,4,3,2,1,0:T(8,128)S(1)} %get-tuple-element.22.edges_ref, f32[2,3,32,8,128]{4,3,2,1,0:T(8,128)S(1)} %get-tuple-element.23.refined_ref), custom_call_target="tpu_custom_call" | custom-call | bytes 9000000 | tf_op jit(solution)/shard_map/pallas_call | solution.py:459
  36.7 0.0 collective-permute-done.main_ref
  36.7 1.3 %collective-permute-done.3.message_ref = f32[27,8,128]{2,1,0:T(8,128)S(1)} collective-permute-done((f32[27,8,128]{2,1,0:T(8,128)S(1)}, f32[27,8,128]{2,1,0:T(8,128)S(1)}, u32[]{:S(2)}, u32[]{:S(2)}) %collective-permute-start.3) | collective-permute-done | bytes 110624 | tf_op jit(solution)/shard_map/ppermute | solution.py:52
  38.0 5.0 %shard_map.42 = f32[1536,128]{1,0:T(8,128)} custom-call(f32[3,18,8,128]{3,2,1,0:T(8,128)S(1)} %collective-permute-done.main_ref, f32[27,8,128]{2,1,0:T(8,128)S(1)} %collective-permute-done.3.message_ref, f32[9,2,3,12,8,128]{5,4,3,2,1,0:T(8,128)S(1)} %get-tuple-element.22.edges_ref, f32[2,3,32,8,128]{4,3,2,1,0:T(8,128)S(1)} %get-tuple-element.23.refined_ref, ...), custom_call_target="tpu_custom_call" | custom-call | bytes 9000000 | tf_op jit(solution)/shard_map/pallas_call | solution.py:459
Async XLA Ops:
  3.2 15.1 %all-to-all-start = ((f32[16,2,2,8,128]{4,3,2,1,0:T(8,128)}), f32[16,2,2,8,128]{4,3,2,1,0:T(8,128)S(1)}, u32[]{:S(2)}, u32[]{:S(2)}) async-start(f32[16,2,2,8,128]{4,3,2,1,0:T(8,128)} %get-tuple-element.17), calls=%async_computation | async-start | bytes 524288 | tf_op jit(solution)/shard_map/all_to_all | solution.py:488
  10.0 8.2 %collective-permute-start.1 = (f32[3,10,8,128]{3,2,1,0:T(8,128)}, f32[3,10,8,128]{3,2,1,0:T(8,128)S(1)}, u32[]{:S(2)}, u32[]{:S(2)}) collective-permute-start(f32[3,10,8,128]{3,2,1,0:T(8,128)} %get-tuple-element.18), channel_id=1, source_target_pairs={{0,1},{1,0},{2,3},{3,2},{4,5},{5,4},{6,7},{7,6},{8,9},{9,8},{10,11... | collective-permute-start | bytes 368648 | tf_op jit(solution)/shard_map/ppermute | solution.py:47
  10.2 8.1 %collective-permute-start.2 = (f32[3,10,8,128]{3,2,1,0:T(8,128)}, f32[3,10,8,128]{3,2,1,0:T(8,128)S(1)}, u32[]{:S(2)}, u32[]{:S(2)}) collective-permute-start(f32[3,10,8,128]{3,2,1,0:T(8,128)} %get-tuple-element.19), channel_id=1, source_target_pairs={{0,15},{1,2},{2,1},{3,4},{4,3},{5,6},{6,5},{7,8},{8,7},{9,10},{10,... | collective-permute-start | bytes 368648 | tf_op jit(solution)/shard_map/ppermute | solution.py:52
  11.8 20.4 %collective-permute-start.4 = (f32[3,18,8,128]{3,2,1,0:T(8,128)}, f32[3,18,8,128]{3,2,1,0:T(8,128)S(1)}, u32[]{:S(2)}, u32[]{:S(2)}) collective-permute-start(f32[3,18,8,128]{3,2,1,0:T(8,128)} %get-tuple-element.24), channel_id=1, source_target_pairs={{0,16},{16,0},{32,48},{48,32},{64,80},{80,64},{96,112},{112,96},{1... | collective-permute-start | bytes 663560 | tf_op jit(solution)/shard_map/ppermute | solution.py:47
  14.4 22.3 %collective-permute-start = (f32[3,18,8,128]{3,2,1,0:T(8,128)}, f32[3,18,8,128]{3,2,1,0:T(8,128)S(1)}, u32[]{:S(2)}, u32[]{:S(2)}) collective-permute-start(f32[3,18,8,128]{3,2,1,0:T(8,128)} %get-tuple-element.16), channel_id=1, source_target_pairs={{0,112},{16,32},{32,16},{48,64},{64,48},{80,96},{96,80},{112,0},{1... | collective-permute-start | bytes 663560 | tf_op jit(solution)/shard_map/ppermute | solution.py:52
  18.6 14.3 %collective-permute-start.5 = (f32[27,8,128]{2,1,0:T(8,128)S(1)}, f32[27,8,128]{2,1,0:T(8,128)S(1)}, u32[]{:S(2)}, u32[]{:S(2)}) collective-permute-start(f32[27,8,128]{2,1,0:T(8,128)S(1)} %get-tuple-element.25), channel_id=1, source_target_pairs={{0,16},{16,0},{32,48},{48,32},{64,80},{80,64},{96,112},{112,96},{1... | collective-permute-start | bytes 331784 | tf_op jit(solution)/shard_map/ppermute | solution.py:47
  20.7 17.2 %collective-permute-start.3 = (f32[27,8,128]{2,1,0:T(8,128)S(1)}, f32[27,8,128]{2,1,0:T(8,128)S(1)}, u32[]{:S(2)}, u32[]{:S(2)}) collective-permute-start(f32[27,8,128]{2,1,0:T(8,128)S(1)} %get-tuple-element.20), channel_id=1, source_target_pairs={{0,112},{16,32},{32,16},{48,64},{64,48},{80,96},{96,80},{112,0},{1... | collective-permute-start | bytes 331784 | tf_op jit(solution)/shard_map/ppermute | solution.py:52
  24.5 1.1 %copy-start = (f32[3,64,8,128]{3,2,1,0:T(8,128)S(1)}, f32[3,64,8,128]{3,2,1,0:T(8,128)}, u32[]{:S(2)}) copy-start(f32[3,64,8,128]{3,2,1,0:T(8,128)} %get-tuple-element.21.tile_ref) | copy-start | bytes 2359300

commit v4 on v3

--- a/solution.py
+++ b/solution.py
@@ -24,9 +24,10 @@
 PAIRS = REACH // 2
 PER = COLS // REACH
 CREGS = -(-2 * PAIRS // PER)
+OWN = -(-REACH // 8) * 8
 HAND = 6
 CHUNK = 16
-PACK_LIMIT = 60
+PACK_LIMIT = 57
 SIDE = EDGE + MIDDLE
 
 time_step = 0.4
@@ -95,24 +96,22 @@
             out_ref[j, row, 1] = jnp.where(lane < WINDOW, north[j], roll(warm[j], HALF))
 
 
-def pack_kernel(
-    wind_hbm, temp_hbm, start_hbm, out_ref, tile_ref, x_near_ref, x_far_ref, y_near_ref, y_far_ref,
-    wind_ref, temp_ref, start_ref, sems,
-):
-    x_odd, y_odd = parity("gx"), parity("gy")
+def strip_kernel(wind_hbm, temp_hbm, packed_ref, wind_ref, temp_ref, sems):
     wind_copy = pltpu.make_async_copy(wind_hbm, wind_ref, sems.at[0])
     temp_copy = pltpu.make_async_copy(temp_hbm, temp_ref, sems.at[1])
-    start_copy = pltpu.make_async_copy(start_hbm, start_ref, sems.at[2])
     wind_copy.start()
     temp_copy.start()
-    start_copy.start()
     wind_copy.wait()
     temp_copy.wait()
-    pack_coarse(wind_ref, temp_ref, out_ref)
-    start_copy.wait()
+    pack_coarse(wind_ref, temp_ref, packed_ref)
+
+
+def tile_kernel(start_ref, tile_ref, x_near_ref, x_far_ref, y_near_ref, y_far_ref):
+    x_odd, y_odd = parity("gx"), parity("gy")
     for f in range(3):
         for row in range(ROWS):
-            tile_ref[f, row] = start_ref[pl.ds(f * LEVELS * ROWS + row, LEVELS, stride=ROWS), :]
+            values = start_ref[pl.ds(f * LEVELS * ROWS + row, LEVELS, stride=ROWS), :]
+            tile_ref[f, row] = values * (1.0 / scale) if f == 0 else values
     x_near_ref[...] = tile_ref[:, pl.ds((1 - x_odd) * (ROWS - REACH), REACH)]
     x_far_ref[...] = tile_ref[:, pl.ds(x_odd * (ROWS - REACH), REACH)]
     lane = lanes()
@@ -225,16 +224,18 @@
         ]
         east, north, warm = background
         change = (
-            east * dx[0] + north * dy[0] + scale * (dx[1] + dy[2]),
+            east * dx[0] + north * dy[0] + (dx[1] + dy[2]),
             east * dx[1] + north * dy[1] + warm * dx[0],
             east * dx[2] + north * dy[2] + warm * dy[0],
         )
         for f in range(3):
             moved = mid[f] - change[f]
-            if stage == 1:
-                moved = 0.75 * base[f] + 0.25 * moved
-            elif stage == 2:
-                moved = (1.0 / 3.0) * base[f] + (2.0 / 3.0) * moved
+            if stage == 0:
+                moved = (1.0 / 6.0) * moved
+            elif stage == 1:
+                moved = 0.5 * base[f] + moved
+            else:
+                moved = (1.0 / 3.0) * base[f] + moved
             store(f, moved)
 
 
@@ -249,16 +250,31 @@
             store(k, f, result[:, cut].reshape(n, LEVELS, COLS))
 
 
-def merged(main, rim, lane):
+def merged(f, main, rim, lane):
     value = jnp.where(lane < REACH, roll(rim, -REACH), main)
-    return jnp.where(lane >= COLS - REACH, roll(rim, COLS - 2 * REACH - RIGHT), value)
-
-
-def compose_kernel(tile_ref, y_near_ref, y_far_ref, state_ref):
+    value = jnp.where(lane >= COLS - REACH, roll(rim, COLS - 2 * REACH - RIGHT), value)
+    return value * scale if f == 0 else value
+
+
+def inner_kernel(
+    coarse_ref, tile_ref, y_near_ref, y_far_ref, edges_ref, inside_ref, refined_ref,
+    background, state, first, second, rim_ref,
+):
     y_odd = parity("gy")
     lane = lanes()
+    east_table, north_table, table = refine_table(0), refine_table(1), difference_table()
+
+    for start in range(0, CROWS, CHUNK):
+
+        def keep(k, f, values, start=start):
+            refined_ref[k, f, start : start + CHUNK] = values
+
+        refine_columns(coarse_ref[start : start + CHUNK], east_table, north_table, keep)
+    for k in range(2):
+        for f in range(3):
+            refine_rows(refined_ref, k, f, 0, CROWS, background, 0)
+
     take_near = (lane >= RIGHT).astype(jnp.int32) == 1 - y_odd
-    state_ref[0] = tile_ref[...]
     for row, count, register, slot in slots():
         near_shift = lax.rem((1 - y_odd) * (RIM - REACH) - REACH * slot + COLS, COLS)
         far_shift = lax.rem(y_odd * (RIM - REACH) - REACH * slot + COLS, COLS)
@@ -266,29 +282,16 @@
             near = roll(y_near_ref[f, register : register + count], near_shift)
             far = roll(y_far_ref[f, register : register + count], far_shift)
             halo = jnp.where(take_near, near, far)
-            main = tile_ref[f, row : row + count]
-            state_ref[1, f, row : row + count] = rim_of(main, halo, halo, lane)
-
-
-def inner_kernel(
-    coarse_ref, start_ref, edges_ref, inside_ref, refined_ref,
-    background, state, first, second,
-):
-    lane = lanes()
-    east_table, north_table, table = refine_table(0), refine_table(1), difference_table()
-
-    for start in range(0, CROWS, CHUNK):
-
-        def keep(k, f, values, start=start):
-            refined_ref[k, f, start : start + CHUNK] = values
-
-        refine_columns(coarse_ref[start : start + CHUNK], east_table, north_table, keep)
-    for k in range(2):
-        for f in range(3):
-            refine_rows(refined_ref, k, f, 0, CROWS, background, 0)
-
+            rim_ref[f, row : row + count] = rim_of(tile_ref[f, row : row + count], halo, halo, lane)
+
+    class Start:
+        def __getitem__(self, index):
+            c, f, rows = index
+            return (rim_ref if c else tile_ref)[f, rows]
+
+    start_state = Start()
     for s in range(STAGES):
-        origin = start_ref if s < 3 else state
+        origin = start_state if s < 3 else state
         buffers = (origin, first, second, state)
         source, target = buffers[s % 3], buffers[s % 3 + 1]
         for c in range(2):
@@ -313,13 +316,14 @@
             stage_sums(jobs, stage_products(jobs, table), s % 3)
     for f in range(3):
         rows = slice(REACH, ROWS - REACH)
-        inside_ref[f] = merged(state[0, f, rows], state[1, f, rows], lane)
+        inside_ref[f] = merged(f, state[0, f, rows], state[1, f, rows], lane)
 
 
 def refine_rows(refined, k, f, start, count, background, first):
     block = refined[k, f, start : start + count]
-    centre = (0.75 * scale) * block
-    side = (0.25 * scale) * block
+    factor = scale * scale if f == 2 else scale
+    centre = (0.75 * factor) * block
+    side = (0.25 * factor) * block
     odd = centre[:-1] + side[1:]
     even = centre[1:] + side[:-1]
     for i in range(count - 1):
@@ -388,39 +392,62 @@
                 jobs = [job_of(c, s)]
                 waiting[c] = (jobs, stage_products(jobs, table))
     rows = pl.ds(REACH - 2 * HAND * side, REACH)
-    return [merged(state[0, f, rows], state[1, f, rows], lane) for f in range(3)]
+    return [merged(f, state[0, f, rows], state[1, f, rows], lane) for f in range(3)]
+
+
+def place(out_ref, f, row, value):
+    rows = out_ref.shape[0] // (3 * LEVELS)
+    out_ref[pl.ds(f * LEVELS * rows + row, LEVELS, stride=rows), :] = value
 
 
 def near_end_kernel(
-    main_ref, message_ref, edges_ref, refined_ref, end_ref, refined, background, state, first, second
+    main_ref, message_ref, edges_ref, refined_ref, inside_ref, end_ref,
+    refined, background, state, first, second, out_ref, sem,
 ):
     side = 1 - parity("gx")
+    for f in range(3):
+        for row in range(ROWS - 2 * REACH):
+            place(out_ref, f, REACH + row, inside_ref[f, row])
     ends = outer_end(
         side, main_ref, message_ref, edges_ref, refined_ref, refined, background, state, first, second
     )
     for f in range(3):
-        end_ref[f] = ends[f]
+        for row in range(REACH):
+            place(out_ref, f, row + side * (ROWS - REACH), ends[f][row])
+    source = out_ref.reshape(3 * LEVELS, ROWS, COLS)
+    rows = pl.ds(pl.multiple_of(side * OWN, 8), ROWS - OWN)
+    copy = pltpu.make_async_copy(source.at[:, rows], end_ref.at[:, rows], sem.at[0])
+    copy.start()
+    copy.wait()
 
 
 def far_end_kernel(
-    main_ref, message_ref, edges_ref, refined_ref, near_ref, inside_ref, out_ref,
-    refined, background, state, first, second,
+    main_ref, message_ref, edges_ref, refined_ref, inside_ref, before_ref, end_ref,
+    refined, background, state, first, second, out_ref, sems,
 ):
+    del before_ref
     side = parity("gx")
-    for f in range(3):
-        for row in range(ROWS - 2 * REACH):
-            at = f * LEVELS * ROWS + REACH + row
-            out_ref[pl.ds(at, LEVELS, stride=ROWS), :] = inside_ref[f, row]
-        for row in range(REACH):
-            at = f * LEVELS * ROWS + row + (1 - side) * (ROWS - REACH)
-            out_ref[pl.ds(at, LEVELS, stride=ROWS), :] = near_ref[f, row]
+    spare = OWN - REACH
+    for f in range(3):
+        for row in range(spare):
+            inner = row + side * (ROWS - 2 * REACH - spare)
+            place(out_ref, f, row + (1 - side) * REACH, inside_ref[f, inner])
     ends = outer_end(
         side, main_ref, message_ref, edges_ref, refined_ref, refined, background, state, first, second
     )
+    target = out_ref.reshape(3 * LEVELS, OWN, COLS)
+    rows = pl.ds(pl.multiple_of(side * (ROWS - OWN), 8), OWN)
+    copies = []
     for f in range(3):
         for row in range(REACH):
-            at = f * LEVELS * ROWS + row + side * (ROWS - REACH)
-            out_ref[pl.ds(at, LEVELS, stride=ROWS), :] = ends[f][row]
+            place(out_ref, f, row + side * spare, ends[f][row])
+        field = pl.ds(f * LEVELS, LEVELS)
+        copies.append(
+            pltpu.make_async_copy(target.at[field], end_ref.at[field, rows], sems.at[f])
+        )
+        copies[f].start()
+    for copy in copies:
+        copy.wait()
 
 
 def refine_table(north):
@@ -451,7 +478,8 @@
 
 
 def call(
-    kernel, outputs, scratch=(), limit=48, microseconds=1, fetched=(), sent=False, semaphores=0
+    kernel, outputs, scratch=(), limit=48, microseconds=1, fetched=(), sent=False, semaphores=0,
+    aliases=None,
 ):
     here, there = pl.BlockSpec(memory_space=pltpu.VMEM), pl.BlockSpec(memory_space=pltpu.HBM)
 
@@ -463,6 +491,7 @@
             out_specs=[there if sent else here] * len(outputs),
             scratch_shapes=[pltpu.VMEM(shape, F32) for shape in scratch]
             + ([pltpu.SemaphoreType.DMA((semaphores,))] if semaphores else []),
+            input_output_aliases=aliases or {},
             compiler_params=pltpu.CompilerParams(vmem_limit_bytes=limit * 2**20),
             cost_estimate=pl.CostEstimate(
                 flops=0, bytes_accessed=3_000_000 * microseconds, transcendentals=0
@@ -475,16 +504,17 @@
 def local(les_wind, les_temp, acoustic_start):
     block = (LEVELS, COLS)
     groups = lax.axis_size("gy")
-    packed, tile, x_near, x_far, y_near, y_far = call(
-        pack_kernel,
-        [(groups, 2, 2) + block, (3, ROWS) + block]
-        + 2 * [(3, REACH) + block]
-        + 2 * [(3, SIDE) + block],
-        scratch=[les_wind.shape, les_temp.shape, (3 * LEVELS * ROWS, COLS)],
-        fetched=(0, 1, 2),
-        semaphores=3,
+    (packed,) = call(
+        strip_kernel,
+        [(groups, 2, 2) + block],
+        scratch=[les_wind.shape, les_temp.shape],
+        fetched=(0, 1),
+        semaphores=2,
         limit=PACK_LIMIT,
-    )(les_wind, les_temp, acoustic_start.reshape(3 * LEVELS * ROWS, COLS))
+    )(les_wind, les_temp)
+    tile, x_near, x_far, y_near, y_far = call(
+        tile_kernel, [(3, ROWS) + block] + 2 * [(3, REACH) + block] + 2 * [(3, SIDE) + block]
+    )(acoustic_start.reshape(3 * LEVELS * ROWS, COLS))
     coarse = lax.all_to_all(packed, "gy", split_axis=0, concat_axis=0, tiled=True)
     coarse = coarse.reshape((CROWS, 2) + block)
     x_near, x_far = swap_near(x_near, "gx"), swap_far(x_far, "gx")
@@ -493,21 +523,33 @@
         coarse, y_near, y_far
     )
     s_near, s_far = swap_near(s_near, "gx"), swap_far(s_far, "gx")
-    (state,) = call(compose_kernel, [(2, 3, ROWS) + block])(tile, y_near, y_far)
     edges, inside, refined = call(
         inner_kernel,
         [(STAGES, 2, 3, 2 * HAND) + block, (3, ROWS - 2 * REACH) + block, (2, 3, CROWS) + block],
-        scratch=4 * [(2, 3, ROWS) + block],
+        scratch=4 * [(2, 3, ROWS) + block] + [(3, ROWS) + block],
         microseconds=6,
-    )(coarse, state)
+    )(coarse, tile, y_near, y_far)
     scratch = [(2, 3, MARGIN + HROWS) + block, (2, 3, 2 * (MARGIN + HROWS)) + block]
     scratch += 3 * [(2, 3, REACH + REACH + HAND) + block]
-    (near,) = call(near_end_kernel, [(3, REACH) + block], scratch=scratch, microseconds=3)(
-        x_near, s_near, edges, refined
-    )
-    (end,) = call(far_end_kernel, [(3 * LEVELS * ROWS, COLS)], scratch=scratch, microseconds=3)(
-        x_far, s_far, edges, refined, near, inside
-    )
+    whole = (3 * LEVELS, ROWS, COLS)
+    (near,) = call(
+        near_end_kernel,
+        [whole],
+        scratch=scratch + [(3 * LEVELS * ROWS, COLS)],
+        microseconds=3,
+        sent=True,
+        semaphores=1,
+    )(x_near, s_near, edges, refined, inside)
+    (end,) = call(
+        far_end_kernel,
+        [whole],
+        scratch=scratch + [(3 * LEVELS * OWN, COLS)],
+        microseconds=3,
+        fetched=(5,),
+        sent=True,
+        semaphores=3,
+        aliases={5: 0},
+    )(x_far, s_far, edges, refined, inside, near)
     return end.reshape(acoustic_start.shape)
 
 

time: 43.3 us -> 42.5 us (0.982)
  waiting for transfers between devices: 1.85 us -> 1.1 us
  Pallas kernels: 19 us -> 18.5 us
    ppermute x3, waiting for transfers between devices: 1.27 us -> 0.31 us  [swap_far(): lax.ppermute(values, axis, [(i, (i + 1) % count if i % 2 else (i - 1) % c...]
    pallas_call x6, Pallas kernels: 19 us -> 18.5 us  [run(): pl.pallas_call(kernel, out_shape=[jax.ShapeDtypeStruct(shape, F32) for sh...]
  transfers between devices with their start and end apart: 7 -> 7, of which waited for: 2 -> 2; matrix products, arithmetic and copies ran while one was open for 0% -> 0% of each run, Pallas kernels for 25% -> 28%
where the time goes in v4:
time: 42.5 us; the launch traced here: 42.3 us
  starting transfers between devices  21.3 us (50%)
  Pallas kernels  18.5 us (44%)
  local copies, waits for them, and re-layouts  1.13 us (3%)
  waiting for transfers between devices  1.1 us (3%)
    pallas_call x6, Pallas kernels, run(): pl.pallas_call(kernel, out_shape=[jax.ShapeDtypeStruct(shape, F32) for sh...  18.5 us
    ppermute x3, starting transfers between devices, swap_far(): lax.ppermute(values, axis, [(i, (i + 1) % count if i % 2 else (i - 1) % c...  9.25 us
    all_to_all x1, starting transfers between devices, local(): lax.all_to_all(packed, 'gy', split_axis=0, concat_axis=0, tiled=True)  6.84 us
    ppermute x3, starting transfers between devices, swap_near(): lax.ppermute(values, axis, [(i, i ^ 1) for i in range(lax.axis_size(axis))])  5.18 us
    unnamed x2, local copies, waits for them, and re-layouts  1.13 us
  transfers between devices with their start and end apart: 7, of which 2 were waited for; matrix products, arithmetic and copies ran while one was open for 0% of the time, Pallas kernels for 28%

profile of v4, /device:TPU:1, one launch (start us, length us, event | category | flops | bytes accessed | tf_op | source)
XLA Modules:
  0.0 42.3 jit_solution(4528794395679776565)
XLA Ops:
  0.0 2.0 %shard_map.38 = f32[16,2,2,8,128]{4,3,2,1,0:T(8,128)} custom-call(f32[2,8,2,1024]{3,2,1,0:T(2,128)} %wind_hbm.1, f32[8,2,1024]{2,1,0:T(2,128)} %temp_hbm.1), custom_call_target="tpu_custom_call" | custom-call | bytes 3000000 | tf_op jit(solution)/shard_map/pallas_call | solution.py:487
  2.0 6.8 %all-to-all-start = ((f32[16,2,2,8,128]{4,3,2,1,0:T(8,128)}), f32[16,2,2,8,128]{4,3,2,1,0:T(8,128)S(1)}, u32[]{:S(2)}, u32[]{:S(2)}) async-start(f32[16,2,2,8,128]{4,3,2,1,0:T(8,128)} %shard_map.38), calls=%async_computation | async-start | bytes 524288 | tf_op jit(solution)/shard_map/all_to_all | solution.py:518
  8.8 0.0 copy-start
  8.8 1.1 %copy-done = f32[3,8,64,128]{3,2,1,0:T(8,128)S(1)} copy-done((f32[3,8,64,128]{3,2,1,0:T(8,128)S(1)}, f32[3,8,64,128]{3,2,1,0:T(8,128)}, u32[]{:S(2)}) %copy-start) | copy-done | bytes 786456
  9.9 0.8 %shard_map.37 = (f32[3,64,8,128]{3,2,1,0:T(8,128)S(1)}, f32[3,18,8,128]{3,2,1,0:T(8,128)S(1)}, f32[3,18,8,128]{3,2,1,0:T(8,128)S(1)}, f32[3,10,8,128]{3,2,1,0:T(8,128)S(1)}, f32[3,10,8,128]{3,2,1,0:T(8,128)S(1)}) custom-call(f32[1536,128]{1,0:T(8,128)S(1)} %bitcast.5), custom_call_target="tpu_custom_call" | custom-call | bytes 3000000 | tf_op jit(solution)/shard_map/pallas_call | solution.py:487
  10.8 0.2 collective-permute-start.1
  11.0 1.7 %collective-permute-start.2 = (f32[3,10,8,128]{3,2,1,0:T(8,128)S(1)}, f32[3,10,8,128]{3,2,1,0:T(8,128)S(1)}, u32[]{:S(2)}, u32[]{:S(2)}) collective-permute-start(f32[3,10,8,128]{3,2,1,0:T(8,128)S(1)} %get-tuple-element.17), channel_id=1, source_target_pairs={{0,15},{1,2},{2,1},{3,4},{4,3},{5,6},{6,5},{7,8},{8,7},{9,10},{10,... | collective-permute-start | bytes 368648 | tf_op jit(solution)/shard_map/ppermute | solution.py:53
  12.6 2.6 %collective-permute-start.4 = (f32[3,18,8,128]{3,2,1,0:T(8,128)S(1)}, f32[3,18,8,128]{3,2,1,0:T(8,128)S(1)}, u32[]{:S(2)}, u32[]{:S(2)}) collective-permute-start(f32[3,18,8,128]{3,2,1,0:T(8,128)S(1)} %get-tuple-element.23), channel_id=1, source_target_pairs={{0,16},{16,0},{32,48},{48,32},{64,80},{80,64},{96,112},{112,96},{1... | collective-permute-start | bytes 663560 | tf_op jit(solution)/shard_map/ppermute | solution.py:48
  15.3 3.8 %collective-permute-start = (f32[3,18,8,128]{3,2,1,0:T(8,128)S(1)}, f32[3,18,8,128]{3,2,1,0:T(8,128)S(1)}, u32[]{:S(2)}, u32[]{:S(2)}) collective-permute-start(f32[3,18,8,128]{3,2,1,0:T(8,128)S(1)} %get-tuple-element.15), channel_id=1, source_target_pairs={{0,112},{16,32},{32,16},{48,64},{64,48},{80,96},{96,80},{112,0},{1... | collective-permute-start | bytes 663560 | tf_op jit(solution)/shard_map/ppermute | solution.py:53
  19.1 0.0 collective-permute-done.1.y_near_ref
  19.1 0.0 collective-permute-done.2.y_far_ref
  19.1 0.0 all-to-all-done
  19.1 0.3 shard_map.39
  19.4 2.4 %collective-permute-start.5 = (f32[27,8,128]{2,1,0:T(8,128)S(1)}, f32[27,8,128]{2,1,0:T(8,128)S(1)}, u32[]{:S(2)}, u32[]{:S(2)}) collective-permute-start(f32[27,8,128]{2,1,0:T(8,128)S(1)} %get-tuple-element.24), channel_id=1, source_target_pairs={{0,16},{16,0},{32,48},{48,32},{64,80},{80,64},{96,112},{112,96},{1... | collective-permute-start | bytes 331784 | tf_op jit(solution)/shard_map/ppermute | solution.py:48
  21.8 3.7 %collective-permute-start.3 = (f32[27,8,128]{2,1,0:T(8,128)S(1)}, f32[27,8,128]{2,1,0:T(8,128)S(1)}, u32[]{:S(2)}, u32[]{:S(2)}) collective-permute-start(f32[27,8,128]{2,1,0:T(8,128)S(1)} %get-tuple-element.18), channel_id=1, source_target_pairs={{0,112},{16,32},{32,16},{48,64},{64,48},{80,96},{96,80},{112,0},{1... | collective-permute-start | bytes 331784 | tf_op jit(solution)/shard_map/ppermute | solution.py:53
  25.5 6.0 %shard_map.40 = (f32[9,2,3,12,8,128]{5,4,3,2,1,0:T(8,128)S(1)}, f32[3,28,8,128]{3,2,1,0:T(8,128)S(1)}, f32[2,3,32,8,128]{4,3,2,1,0:T(8,128)S(1)}) custom-call(f32[32,2,8,128]{3,2,1,0:T(8,128)S(1)} %bitcast.4, f32[3,64,8,128]{3,2,1,0:T(8,128)S(1)} %get-tuple-element.19.tile_ref, f32[3,10,8,128]{3,2,1,0:T(8,128)S(1)} %collective-permute-done.1.y_near_ref, ...), custom_call_target="tpu_custom_call" | custom-call | bytes 18000000 | tf_op jit(solution)/shard_map/pallas_call | solution.py:487
  31.5 0.0 collective-permute-done.4.main_ref
  31.6 0.8 %collective-permute-done.5.message_ref = f32[27,8,128]{2,1,0:T(8,128)S(1)} collective-permute-done((f32[27,8,128]{2,1,0:T(8,128)S(1)}, f32[27,8,128]{2,1,0:T(8,128)S(1)}, u32[]{:S(2)}, u32[]{:S(2)}) %collective-permute-start.5) | collective-permute-done | bytes 110624 | tf_op jit(solution)/shard_map/ppermute | solution.py:48
  32.3 4.9 %shard_map.41.before_ref = f32[24,64,128]{2,1,0:T(8,128)} custom-call(f32[3,18,8,128]{3,2,1,0:T(8,128)S(1)} %collective-permute-done.4.main_ref, f32[27,8,128]{2,1,0:T(8,128)S(1)} %collective-permute-done.5.message_ref, f32[9,2,3,12,8,128]{5,4,3,2,1,0:T(8,128)S(1)} %get-tuple-element.20.edges_ref, f32[2,3,32,8,128]{4,3,2,1,0:T(8,128)S(1)} %get-tuple-element.21.refined_ref, ...), custom_call_target="tpu_custom_call" | custom-call | bytes 9000000 | tf_op jit(solution)/shard_map/pallas_call | solution.py:487
  37.3 0.0 collective-permute-done.main_ref
  37.3 0.3 collective-permute-done.3.message_ref
  37.6 4.6 %shard_map.42 = f32[24,64,128]{2,1,0:T(8,128)} custom-call(f32[3,18,8,128]{3,2,1,0:T(8,128)S(1)} %collective-permute-done.main_ref, f32[27,8,128]{2,1,0:T(8,128)S(1)} %collective-permute-done.3.message_ref, f32[9,2,3,12,8,128]{5,4,3,2,1,0:T(8,128)S(1)} %get-tuple-element.20.edges_ref, ...), custom_call_target="tpu_custom_call", output_to_operand_aliasing={{}: (5, {})} | custom-call | bytes 9000000 | tf_op jit(solution)/shard_map/pallas_call | solution.py:487
Async XLA Ops:
  2.0 17.1 %all-to-all-start = ((f32[16,2,2,8,128]{4,3,2,1,0:T(8,128)}), f32[16,2,2,8,128]{4,3,2,1,0:T(8,128)S(1)}, u32[]{:S(2)}, u32[]{:S(2)}) async-start(f32[16,2,2,8,128]{4,3,2,1,0:T(8,128)} %shard_map.38), calls=%async_computation | async-start | bytes 524288 | tf_op jit(solution)/shard_map/all_to_all | solution.py:518
  8.8 1.1 %copy-start = (f32[3,8,64,128]{3,2,1,0:T(8,128)S(1)}, f32[3,8,64,128]{3,2,1,0:T(8,128)}, u32[]{:S(2)}) copy-start(f32[3,8,64,128]{3,2,1,0:T(8,128)} %param.5) | copy-start | bytes 2359300
  10.8 8.3 %collective-permute-start.1 = (f32[3,10,8,128]{3,2,1,0:T(8,128)S(1)}, f32[3,10,8,128]{3,2,1,0:T(8,128)S(1)}, u32[]{:S(2)}, u32[]{:S(2)}) collective-permute-start(f32[3,10,8,128]{3,2,1,0:T(8,128)S(1)} %get-tuple-element.16), channel_id=1, source_target_pairs={{0,1},{1,0},{2,3},{3,2},{4,5},{5,4},{6,7},{7,6},{8,9},{9,8},{10,11... | collective-permute-start | bytes 368648 | tf_op jit(solution)/shard_map/ppermute | solution.py:48
  11.0 8.1 %collective-permute-start.2 = (f32[3,10,8,128]{3,2,1,0:T(8,128)S(1)}, f32[3,10,8,128]{3,2,1,0:T(8,128)S(1)}, u32[]{:S(2)}, u32[]{:S(2)}) collective-permute-start(f32[3,10,8,128]{3,2,1,0:T(8,128)S(1)} %get-tuple-element.17), channel_id=1, source_target_pairs={{0,15},{1,2},{2,1},{3,4},{4,3},{5,6},{6,5},{7,8},{8,7},{9,10},{10,... | collective-permute-start | bytes 368648 | tf_op jit(solution)/shard_map/ppermute | solution.py:53
  12.6 18.9 %collective-permute-start.4 = (f32[3,18,8,128]{3,2,1,0:T(8,128)S(1)}, f32[3,18,8,128]{3,2,1,0:T(8,128)S(1)}, u32[]{:S(2)}, u32[]{:S(2)}) collective-permute-start(f32[3,18,8,128]{3,2,1,0:T(8,128)S(1)} %get-tuple-element.23), channel_id=1, source_target_pairs={{0,16},{16,0},{32,48},{48,32},{64,80},{80,64},{96,112},{112,96},{1... | collective-permute-start | bytes 663560 | tf_op jit(solution)/shard_map/ppermute | solution.py:48
  15.3 22.0 %collective-permute-start = (f32[3,18,8,128]{3,2,1,0:T(8,128)S(1)}, f32[3,18,8,128]{3,2,1,0:T(8,128)S(1)}, u32[]{:S(2)}, u32[]{:S(2)}) collective-permute-start(f32[3,18,8,128]{3,2,1,0:T(8,128)S(1)} %get-tuple-element.15), channel_id=1, source_target_pairs={{0,112},{16,32},{32,16},{48,64},{64,48},{80,96},{96,80},{112,0},{1... | collective-permute-start | bytes 663560 | tf_op jit(solution)/shard_map/ppermute | solution.py:53
  19.4 12.9 %collective-permute-start.5 = (f32[27,8,128]{2,1,0:T(8,128)S(1)}, f32[27,8,128]{2,1,0:T(8,128)S(1)}, u32[]{:S(2)}, u32[]{:S(2)}) collective-permute-start(f32[27,8,128]{2,1,0:T(8,128)S(1)} %get-tuple-element.24), channel_id=1, source_target_pairs={{0,16},{16,0},{32,48},{48,32},{64,80},{80,64},{96,112},{112,96},{1... | collective-permute-start | bytes 331784 | tf_op jit(solution)/shard_map/ppermute | solution.py:48
  21.8 15.8 %collective-permute-start.3 = (f32[27,8,128]{2,1,0:T(8,128)S(1)}, f32[27,8,128]{2,1,0:T(8,128)S(1)}, u32[]{:S(2)}, u32[]{:S(2)}) collective-permute-start(f32[27,8,128]{2,1,0:T(8,128)S(1)} %get-tuple-element.18), channel_id=1, source_target_pairs={{0,112},{16,32},{32,16},{48,64},{64,48},{80,96},{96,80},{112,0},{1... | collective-permute-start | bytes 331784 | tf_op jit(solution)/shard_map/ppermute | solution.py:53

commit v5 on v4

--- a/solution.py
+++ b/solution.py
@@ -73,7 +73,7 @@
     return pieces
 
 
-def pack_coarse(wind_ref, temp_ref, out_ref):
+def pack_coarse(wind_ref, temp_ref, out_ref, sent):
     lane = lanes()
     blocks = wind_ref.shape[-1] // COLS
 
@@ -94,16 +94,23 @@
         for j in range(2 * blocks):
             out_ref[j, row, 0] = jnp.where(lane < WINDOW, east[j], roll(warm[j], WINDOW))
             out_ref[j, row, 1] = jnp.where(lane < WINDOW, north[j], roll(warm[j], HALF))
-
-
-def strip_kernel(wind_hbm, temp_hbm, packed_ref, wind_ref, temp_ref, sems):
+        sent[row].start()
+
+
+def strip_kernel(wind_hbm, temp_hbm, packed_hbm, wind_ref, temp_ref, packed_ref, sems):
     wind_copy = pltpu.make_async_copy(wind_hbm, wind_ref, sems.at[0])
     temp_copy = pltpu.make_async_copy(temp_hbm, temp_ref, sems.at[1])
     wind_copy.start()
     temp_copy.start()
+    sent = [
+        pltpu.make_async_copy(packed_ref.at[:, row], packed_hbm.at[:, row], sems.at[2 + row])
+        for row in range(2)
+    ]
     wind_copy.wait()
     temp_copy.wait()
-    pack_coarse(wind_ref, temp_ref, packed_ref)
+    pack_coarse(wind_ref, temp_ref, packed_ref, sent)
+    sent[0].wait()
+    sent[1].wait()
 
 
 def tile_kernel(start_ref, tile_ref, x_near_ref, x_far_ref, y_near_ref, y_far_ref):
@@ -344,9 +351,9 @@
             ]
 
     def keep(k, f, values):
-        refined[k, f, pl.ds(side * MARGIN, HROWS)] = values
-
-    values = message_ref[: 2 * HROWS].reshape(HROWS, 2, LEVELS, COLS)
+        refined[k, f, pl.ds(side * MARGIN, HROWS)] = values[:HROWS]
+
+    values = message_ref[: 2 * HROWS + 2].reshape(HROWS + 1, 2, LEVELS, COLS)
     refine_columns(values, east_table, north_table, keep)
     for k in range(2):
         for f in range(3):
@@ -507,9 +514,10 @@
     (packed,) = call(
         strip_kernel,
         [(groups, 2, 2) + block],
-        scratch=[les_wind.shape, les_temp.shape],
+        scratch=[les_wind.shape, les_temp.shape, (groups, 2, 2) + block],
         fetched=(0, 1),
-        semaphores=2,
+        sent=True,
+        semaphores=4,
         limit=PACK_LIMIT,
     )(les_wind, les_temp)
     tile, x_near, x_far, y_near, y_far = call(

time: 42.5 us -> 42.5 us (level)
  no operation moved by 1% of the time
where the time goes in v5:
time: 42.5 us; the launch traced here: 42.3 us
  starting transfers between devices  21.3 us (50%)
  Pallas kernels  18.5 us (44%)
  local copies, waits for them, and re-layouts  1.13 us (3%)
  waiting for transfers between devices  1.11 us (3%)
    pallas_call x6, Pallas kernels, run(): pl.pallas_call(kernel, out_shape=[jax.ShapeDtypeStruct(shape, F32) for sh...  18.5 us
    ppermute x3, starting transfers between devices, swap_far(): lax.ppermute(values, axis, [(i, (i + 1) % count if i % 2 else (i - 1) % c...  9.25 us
    all_to_all x1, starting transfers between devices, local(): lax.all_to_all(packed, 'gy', split_axis=0, concat_axis=0, tiled=True)  6.84 us
    ppermute x3, starting transfers between devices, swap_near(): lax.ppermute(values, axis, [(i, i ^ 1) for i in range(lax.axis_size(axis))])  5.18 us
    unnamed x2, local copies, waits for them, and re-layouts  1.13 us
  transfers between devices with their start and end apart: 7, of which 2 were waited for; matrix products, arithmetic and copies ran while one was open for 0% of the time, Pallas kernels for 28%

profile of v5, /device:TPU:1, one launch (start us, length us, event | category | flops | bytes accessed | tf_op | source)
XLA Modules:
  0.0 42.3 jit_solution(17532119999735591754)
XLA Ops:
  0.0 1.9 %shard_map.38 = f32[16,2,2,8,128]{4,3,2,1,0:T(8,128)} custom-call(f32[2,8,2,1024]{3,2,1,0:T(2,128)} %wind_hbm.1, f32[8,2,1024]{2,1,0:T(2,128)} %temp_hbm.1), custom_call_target="tpu_custom_call" | custom-call | bytes 3000000 | tf_op jit(solution)/shard_map/pallas_call | solution.py:494
  1.9 6.8 %all-to-all-start = ((f32[16,2,2,8,128]{4,3,2,1,0:T(8,128)}), f32[16,2,2,8,128]{4,3,2,1,0:T(8,128)S(1)}, u32[]{:S(2)}, u32[]{:S(2)}) async-start(f32[16,2,2,8,128]{4,3,2,1,0:T(8,128)} %shard_map.38), calls=%async_computation | async-start | bytes 524288 | tf_op jit(solution)/shard_map/all_to_all | solution.py:526
  8.8 0.0 copy-start
  8.8 1.1 %copy-done = f32[3,8,64,128]{3,2,1,0:T(8,128)S(1)} copy-done((f32[3,8,64,128]{3,2,1,0:T(8,128)S(1)}, f32[3,8,64,128]{3,2,1,0:T(8,128)}, u32[]{:S(2)}) %copy-start) | copy-done | bytes 786456
  9.9 0.8 %shard_map.37 = (f32[3,64,8,128]{3,2,1,0:T(8,128)S(1)}, f32[3,18,8,128]{3,2,1,0:T(8,128)S(1)}, f32[3,18,8,128]{3,2,1,0:T(8,128)S(1)}, f32[3,10,8,128]{3,2,1,0:T(8,128)S(1)}, f32[3,10,8,128]{3,2,1,0:T(8,128)S(1)}) custom-call(f32[1536,128]{1,0:T(8,128)S(1)} %bitcast.5), custom_call_target="tpu_custom_call" | custom-call | bytes 3000000 | tf_op jit(solution)/shard_map/pallas_call | solution.py:494
  10.7 0.2 collective-permute-start.1
  10.9 1.7 %collective-permute-start.2 = (f32[3,10,8,128]{3,2,1,0:T(8,128)S(1)}, f32[3,10,8,128]{3,2,1,0:T(8,128)S(1)}, u32[]{:S(2)}, u32[]{:S(2)}) collective-permute-start(f32[3,10,8,128]{3,2,1,0:T(8,128)S(1)} %get-tuple-element.17), channel_id=1, source_target_pairs={{0,15},{1,2},{2,1},{3,4},{4,3},{5,6},{6,5},{7,8},{8,7},{9,10},{10,... | collective-permute-start | bytes 368648 | tf_op jit(solution)/shard_map/ppermute | solution.py:53
  12.6 2.6 %collective-permute-start.4 = (f32[3,18,8,128]{3,2,1,0:T(8,128)S(1)}, f32[3,18,8,128]{3,2,1,0:T(8,128)S(1)}, u32[]{:S(2)}, u32[]{:S(2)}) collective-permute-start(f32[3,18,8,128]{3,2,1,0:T(8,128)S(1)} %get-tuple-element.23), channel_id=1, source_target_pairs={{0,16},{16,0},{32,48},{48,32},{64,80},{80,64},{96,112},{112,96},{1... | collective-permute-start | bytes 663560 | tf_op jit(solution)/shard_map/ppermute | solution.py:48
  15.2 3.8 %collective-permute-start = (f32[3,18,8,128]{3,2,1,0:T(8,128)S(1)}, f32[3,18,8,128]{3,2,1,0:T(8,128)S(1)}, u32[]{:S(2)}, u32[]{:S(2)}) collective-permute-start(f32[3,18,8,128]{3,2,1,0:T(8,128)S(1)} %get-tuple-element.15), channel_id=1, source_target_pairs={{0,112},{16,32},{32,16},{48,64},{64,48},{80,96},{96,80},{112,0},{1... | collective-permute-start | bytes 663560 | tf_op jit(solution)/shard_map/ppermute | solution.py:53
  19.1 0.0 collective-permute-done.1.y_near_ref
  19.1 0.0 collective-permute-done.2.y_far_ref
  19.1 0.0 all-to-all-done
  19.1 0.3 shard_map.39
  19.4 2.4 %collective-permute-start.5 = (f32[27,8,128]{2,1,0:T(8,128)S(1)}, f32[27,8,128]{2,1,0:T(8,128)S(1)}, u32[]{:S(2)}, u32[]{:S(2)}) collective-permute-start(f32[27,8,128]{2,1,0:T(8,128)S(1)} %get-tuple-element.24), channel_id=1, source_target_pairs={{0,16},{16,0},{32,48},{48,32},{64,80},{80,64},{96,112},{112,96},{1... | collective-permute-start | bytes 331784 | tf_op jit(solution)/shard_map/ppermute | solution.py:48
  21.8 3.7 %collective-permute-start.3 = (f32[27,8,128]{2,1,0:T(8,128)S(1)}, f32[27,8,128]{2,1,0:T(8,128)S(1)}, u32[]{:S(2)}, u32[]{:S(2)}) collective-permute-start(f32[27,8,128]{2,1,0:T(8,128)S(1)} %get-tuple-element.18), channel_id=1, source_target_pairs={{0,112},{16,32},{32,16},{48,64},{64,48},{80,96},{96,80},{112,0},{1... | collective-permute-start | bytes 331784 | tf_op jit(solution)/shard_map/ppermute | solution.py:53
  25.5 6.0 %shard_map.40 = (f32[9,2,3,12,8,128]{5,4,3,2,1,0:T(8,128)S(1)}, f32[3,28,8,128]{3,2,1,0:T(8,128)S(1)}, f32[2,3,32,8,128]{4,3,2,1,0:T(8,128)S(1)}) custom-call(f32[32,2,8,128]{3,2,1,0:T(8,128)S(1)} %bitcast.4, f32[3,64,8,128]{3,2,1,0:T(8,128)S(1)} %get-tuple-element.19.tile_ref, f32[3,10,8,128]{3,2,1,0:T(8,128)S(1)} %collective-permute-done.1.y_near_ref, ...), custom_call_target="tpu_custom_call" | custom-call | bytes 18000000 | tf_op jit(solution)/shard_map/pallas_call | solution.py:494
  31.5 0.0 collective-permute-done.4.main_ref
  31.5 0.8 %collective-permute-done.5.message_ref = f32[27,8,128]{2,1,0:T(8,128)S(1)} collective-permute-done((f32[27,8,128]{2,1,0:T(8,128)S(1)}, f32[27,8,128]{2,1,0:T(8,128)S(1)}, u32[]{:S(2)}, u32[]{:S(2)}) %collective-permute-start.5) | collective-permute-done | bytes 110624 | tf_op jit(solution)/shard_map/ppermute | solution.py:48
  32.3 4.9 %shard_map.41.before_ref = f32[24,64,128]{2,1,0:T(8,128)} custom-call(f32[3,18,8,128]{3,2,1,0:T(8,128)S(1)} %collective-permute-done.4.main_ref, f32[27,8,128]{2,1,0:T(8,128)S(1)} %collective-permute-done.5.message_ref, f32[9,2,3,12,8,128]{5,4,3,2,1,0:T(8,128)S(1)} %get-tuple-element.20.edges_ref, f32[2,3,32,8,128]{4,3,2,1,0:T(8,128)S(1)} %get-tuple-element.21.refined_ref, ...), custom_call_target="tpu_custom_call" | custom-call | bytes 9000000 | tf_op jit(solution)/shard_map/pallas_call | solution.py:494
  37.2 0.0 collective-permute-done.main_ref
  37.2 0.3 collective-permute-done.3.message_ref
  37.5 4.5 %shard_map.42 = f32[24,64,128]{2,1,0:T(8,128)} custom-call(f32[3,18,8,128]{3,2,1,0:T(8,128)S(1)} %collective-permute-done.main_ref, f32[27,8,128]{2,1,0:T(8,128)S(1)} %collective-permute-done.3.message_ref, f32[9,2,3,12,8,128]{5,4,3,2,1,0:T(8,128)S(1)} %get-tuple-element.20.edges_ref, ...), custom_call_target="tpu_custom_call", output_to_operand_aliasing={{}: (5, {})} | custom-call | bytes 9000000 | tf_op jit(solution)/shard_map/pallas_call | solution.py:494
Async XLA Ops:
  1.9 17.1 %all-to-all-start = ((f32[16,2,2,8,128]{4,3,2,1,0:T(8,128)}), f32[16,2,2,8,128]{4,3,2,1,0:T(8,128)S(1)}, u32[]{:S(2)}, u32[]{:S(2)}) async-start(f32[16,2,2,8,128]{4,3,2,1,0:T(8,128)} %shard_map.38), calls=%async_computation | async-start | bytes 524288 | tf_op jit(solution)/shard_map/all_to_all | solution.py:526
  8.8 1.1 %copy-start = (f32[3,8,64,128]{3,2,1,0:T(8,128)S(1)}, f32[3,8,64,128]{3,2,1,0:T(8,128)}, u32[]{:S(2)}) copy-start(f32[3,8,64,128]{3,2,1,0:T(8,128)} %param.5) | copy-start | bytes 2359300
  10.7 8.3 %collective-permute-start.1 = (f32[3,10,8,128]{3,2,1,0:T(8,128)S(1)}, f32[3,10,8,128]{3,2,1,0:T(8,128)S(1)}, u32[]{:S(2)}, u32[]{:S(2)}) collective-permute-start(f32[3,10,8,128]{3,2,1,0:T(8,128)S(1)} %get-tuple-element.16), channel_id=1, source_target_pairs={{0,1},{1,0},{2,3},{3,2},{4,5},{5,4},{6,7},{7,6},{8,9},{9,8},{10,11... | collective-permute-start | bytes 368648 | tf_op jit(solution)/shard_map/ppermute | solution.py:48
  10.9 8.1 %collective-permute-start.2 = (f32[3,10,8,128]{3,2,1,0:T(8,128)S(1)}, f32[3,10,8,128]{3,2,1,0:T(8,128)S(1)}, u32[]{:S(2)}, u32[]{:S(2)}) collective-permute-start(f32[3,10,8,128]{3,2,1,0:T(8,128)S(1)} %get-tuple-element.17), channel_id=1, source_target_pairs={{0,15},{1,2},{2,1},{3,4},{4,3},{5,6},{6,5},{7,8},{8,7},{9,10},{10,... | collective-permute-start | bytes 368648 | tf_op jit(solution)/shard_map/ppermute | solution.py:53
  12.6 18.9 %collective-permute-start.4 = (f32[3,18,8,128]{3,2,1,0:T(8,128)S(1)}, f32[3,18,8,128]{3,2,1,0:T(8,128)S(1)}, u32[]{:S(2)}, u32[]{:S(2)}) collective-permute-start(f32[3,18,8,128]{3,2,1,0:T(8,128)S(1)} %get-tuple-element.23), channel_id=1, source_target_pairs={{0,16},{16,0},{32,48},{48,32},{64,80},{80,64},{96,112},{112,96},{1... | collective-permute-start | bytes 663560 | tf_op jit(solution)/shard_map/ppermute | solution.py:48
  15.2 22.0 %collective-permute-start = (f32[3,18,8,128]{3,2,1,0:T(8,128)S(1)}, f32[3,18,8,128]{3,2,1,0:T(8,128)S(1)}, u32[]{:S(2)}, u32[]{:S(2)}) collective-permute-start(f32[3,18,8,128]{3,2,1,0:T(8,128)S(1)} %get-tuple-element.15), channel_id=1, source_target_pairs={{0,112},{16,32},{32,16},{48,64},{64,48},{80,96},{96,80},{112,0},{1... | collective-permute-start | bytes 663560 | tf_op jit(solution)/shard_map/ppermute | solution.py:53
  19.4 12.9 %collective-permute-start.5 = (f32[27,8,128]{2,1,0:T(8,128)S(1)}, f32[27,8,128]{2,1,0:T(8,128)S(1)}, u32[]{:S(2)}, u32[]{:S(2)}) collective-permute-start(f32[27,8,128]{2,1,0:T(8,128)S(1)} %get-tuple-element.24), channel_id=1, source_target_pairs={{0,16},{16,0},{32,48},{48,32},{64,80},{80,64},{96,112},{112,96},{1... | collective-permute-start | bytes 331784 | tf_op jit(solution)/shard_map/ppermute | solution.py:48
  21.8 15.8 %collective-permute-start.3 = (f32[27,8,128]{2,1,0:T(8,128)S(1)}, f32[27,8,128]{2,1,0:T(8,128)S(1)}, u32[]{:S(2)}, u32[]{:S(2)}) collective-permute-start(f32[27,8,128]{2,1,0:T(8,128)S(1)} %get-tuple-element.18), channel_id=1, source_target_pairs={{0,112},{16,32},{32,16},{48,64},{64,48},{80,96},{96,80},{112,0},{1... | collective-permute-start | bytes 331784 | tf_op jit(solution)/shard_map/ppermute | solution.py:53

commit v6 on v5

--- a/solution.py
+++ b/solution.py
@@ -265,11 +265,12 @@
 
 def inner_kernel(
     coarse_ref, tile_ref, y_near_ref, y_far_ref, edges_ref, inside_ref, refined_ref,
-    background, state, first, second, rim_ref,
+    east_ref, north_ref, table_ref, background, state, first, second, rim_ref,
 ):
     y_odd = parity("gy")
     lane = lanes()
     east_table, north_table, table = refine_table(0), refine_table(1), difference_table()
+    east_ref[...], north_ref[...], table_ref[...] = east_table, north_table, table
 
     for start in range(0, CROWS, CHUNK):
 
@@ -339,10 +340,10 @@
 
 
 def outer_end(
-    side, main_ref, message_ref, edges_ref, refined_ref, refined, background, state, first, second
+    side, main_ref, message_ref, edges_ref, refined_ref, tables, refined, background, state, first, second
 ):
     lane = lanes()
-    east_table, north_table, table = refine_table(0), refine_table(1), difference_table()
+    east_table, north_table, table = (ref[...] for ref in tables)
     own = MARGIN + HROWS
     for k in range(2):
         for f in range(3):
@@ -408,7 +409,7 @@
 
 
 def near_end_kernel(
-    main_ref, message_ref, edges_ref, refined_ref, inside_ref, end_ref,
+    main_ref, message_ref, edges_ref, refined_ref, inside_ref, east_ref, north_ref, table_ref, end_ref,
     refined, background, state, first, second, out_ref, sem,
 ):
     side = 1 - parity("gx")
@@ -416,7 +417,8 @@
         for row in range(ROWS - 2 * REACH):
             place(out_ref, f, REACH + row, inside_ref[f, row])
     ends = outer_end(
-        side, main_ref, message_ref, edges_ref, refined_ref, refined, background, state, first, second
+        side, main_ref, message_ref, edges_ref, refined_ref, (east_ref, north_ref, table_ref),
+        refined, background, state, first, second,
     )
     for f in range(3):
         for row in range(REACH):
@@ -429,7 +431,8 @@
 
 
 def far_end_kernel(
-    main_ref, message_ref, edges_ref, refined_ref, inside_ref, before_ref, end_ref,
+    main_ref, message_ref, edges_ref, refined_ref, inside_ref, east_ref, north_ref, table_ref,
+    before_ref, end_ref,
     refined, background, state, first, second, out_ref, sems,
 ):
     del before_ref
@@ -440,7 +443,8 @@
             inner = row + side * (ROWS - 2 * REACH - spare)
             place(out_ref, f, row + (1 - side) * REACH, inside_ref[f, inner])
     ends = outer_end(
-        side, main_ref, message_ref, edges_ref, refined_ref, refined, background, state, first, second
+        side, main_ref, message_ref, edges_ref, refined_ref, (east_ref, north_ref, table_ref),
+        refined, background, state, first, second,
     )
     target = out_ref.reshape(3 * LEVELS, OWN, COLS)
     rows = pl.ds(pl.multiple_of(side * (ROWS - OWN), 8), OWN)
@@ -493,7 +497,10 @@
     def run(*operands):
         return pl.pallas_call(
             kernel,
-            out_shape=[jax.ShapeDtypeStruct(shape, F32) for shape in outputs],
+            out_shape=[
+                jax.ShapeDtypeStruct(shape, F32) if isinstance(shape, tuple) else shape
+                for shape in outputs
+            ],
             in_specs=[there if i in fetched else here for i in range(len(operands))],
             out_specs=[there if sent else here] * len(outputs),
             scratch_shapes=[pltpu.VMEM(shape, F32) for shape in scratch]
@@ -531,9 +538,10 @@
         coarse, y_near, y_far
     )
     s_near, s_far = swap_near(s_near, "gx"), swap_far(s_far, "gx")
-    edges, inside, refined = call(
+    edges, inside, refined, *made = call(
         inner_kernel,
-        [(STAGES, 2, 3, 2 * HAND) + block, (3, ROWS - 2 * REACH) + block, (2, 3, CROWS) + block],
+        [(STAGES, 2, 3, 2 * HAND) + block, (3, ROWS - 2 * REACH) + block, (2, 3, CROWS) + block]
+        + [jax.ShapeDtypeStruct((COLS, n * COLS), jnp.bfloat16) for n in (4, 4, 1)],
         scratch=4 * [(2, 3, ROWS) + block] + [(3, ROWS) + block],
         microseconds=6,
     )(coarse, tile, y_near, y_far)
@@ -547,17 +555,17 @@
         microseconds=3,
         sent=True,
         semaphores=1,
-    )(x_near, s_near, edges, refined, inside)
+    )(x_near, s_near, edges, refined, inside, *made)
     (end,) = call(
         far_end_kernel,
         [whole],
         scratch=scratch + [(3 * LEVELS * OWN, COLS)],
         microseconds=3,
-        fetched=(5,),
+        fetched=(8,),
         sent=True,
         semaphores=3,
-        aliases={5: 0},
-    )(x_far, s_far, edges, refined, inside, near)
+        aliases={8: 0},
+    )(x_far, s_far, edges, refined, inside, *made, near)
     return end.reshape(acoustic_start.shape)
 
 

time: 42.5 us -> 42.5 us (level)
  no operation moved by 1% of the time
where the time goes in v6:
time: 42.5 us; the launch traced here: 42.3 us
  starting transfers between devices  21.3 us (50%)
  Pallas kernels  18.4 us (43%)
  waiting for transfers between devices  1.2 us (3%)
  local copies, waits for them, and re-layouts  1.13 us (3%)
    pallas_call x6, Pallas kernels, run(): pl.pallas_call(kernel, out_shape=[jax.ShapeDtypeStruct(shape, F32) if isi...  18.4 us
    ppermute x3, starting transfers between devices, swap_far(): lax.ppermute(values, axis, [(i, (i + 1) % count if i % 2 else (i - 1) % c...  9.24 us
    all_to_all x1, starting transfers between devices, local(): lax.all_to_all(packed, 'gy', split_axis=0, concat_axis=0, tiled=True)  6.84 us
    ppermute x3, starting transfers between devices, swap_near(): lax.ppermute(values, axis, [(i, i ^ 1) for i in range(lax.axis_size(axis))])  5.2 us
    unnamed x2, local copies, waits for them, and re-layouts  1.13 us
    ppermute x3, waiting for transfers between devices, swap_near(): lax.ppermute(values, axis, [(i, i ^ 1) for i in range(lax.axis_size(axis))])  0.89 us
  transfers between devices with their start and end apart: 7, of which 2 were waited for; matrix products, arithmetic and copies ran while one was open for 0% of the time, Pallas kernels for 28%

profile of v6, /device:TPU:1, one launch (start us, length us, event | category | flops | bytes accessed | tf_op | source)
XLA Modules:
  0.0 42.3 jit_solution(3388457544771675367)
XLA Ops:
  0.0 1.9 %shard_map.38 = f32[16,2,2,8,128]{4,3,2,1,0:T(8,128)} custom-call(f32[2,8,2,1024]{3,2,1,0:T(2,128)} %wind_hbm.1, f32[8,2,1024]{2,1,0:T(2,128)} %temp_hbm.1), custom_call_target="tpu_custom_call" | custom-call | bytes 3000000 | tf_op jit(solution)/shard_map/pallas_call | solution.py:498
  1.9 6.8 %all-to-all-start = ((f32[16,2,2,8,128]{4,3,2,1,0:T(8,128)}), f32[16,2,2,8,128]{4,3,2,1,0:T(8,128)S(1)}, u32[]{:S(2)}, u32[]{:S(2)}) async-start(f32[16,2,2,8,128]{4,3,2,1,0:T(8,128)} %shard_map.38), calls=%async_computation | async-start | bytes 524288 | tf_op jit(solution)/shard_map/all_to_all | solution.py:533
  8.8 0.0 copy-start
  8.8 1.1 %copy-done = f32[3,8,64,128]{3,2,1,0:T(8,128)S(1)} copy-done((f32[3,8,64,128]{3,2,1,0:T(8,128)S(1)}, f32[3,8,64,128]{3,2,1,0:T(8,128)}, u32[]{:S(2)}) %copy-start) | copy-done | bytes 786456
  9.9 0.8 %shard_map.37 = (f32[3,64,8,128]{3,2,1,0:T(8,128)S(1)}, f32[3,18,8,128]{3,2,1,0:T(8,128)S(1)}, f32[3,18,8,128]{3,2,1,0:T(8,128)S(1)}, f32[3,10,8,128]{3,2,1,0:T(8,128)S(1)}, f32[3,10,8,128]{3,2,1,0:T(8,128)S(1)}) custom-call(f32[1536,128]{1,0:T(8,128)S(1)} %bitcast.5), custom_call_target="tpu_custom_call" | custom-call | bytes 3000000 | tf_op jit(solution)/shard_map/pallas_call | solution.py:498
  10.7 0.2 collective-permute-start.1
  10.9 1.7 %collective-permute-start.2 = (f32[3,10,8,128]{3,2,1,0:T(8,128)S(1)}, f32[3,10,8,128]{3,2,1,0:T(8,128)S(1)}, u32[]{:S(2)}, u32[]{:S(2)}) collective-permute-start(f32[3,10,8,128]{3,2,1,0:T(8,128)S(1)} %get-tuple-element.20), channel_id=1, source_target_pairs={{0,15},{1,2},{2,1},{3,4},{4,3},{5,6},{6,5},{7,8},{8,7},{9,10},{10,... | collective-permute-start | bytes 368648 | tf_op jit(solution)/shard_map/ppermute | solution.py:53
  12.6 2.6 %collective-permute-start.4 = (f32[3,18,8,128]{3,2,1,0:T(8,128)S(1)}, f32[3,18,8,128]{3,2,1,0:T(8,128)S(1)}, u32[]{:S(2)}, u32[]{:S(2)}) collective-permute-start(f32[3,18,8,128]{3,2,1,0:T(8,128)S(1)} %get-tuple-element.29), channel_id=1, source_target_pairs={{0,16},{16,0},{32,48},{48,32},{64,80},{80,64},{96,112},{112,96},{1... | collective-permute-start | bytes 663560 | tf_op jit(solution)/shard_map/ppermute | solution.py:48
  15.2 3.8 %collective-permute-start = (f32[3,18,8,128]{3,2,1,0:T(8,128)S(1)}, f32[3,18,8,128]{3,2,1,0:T(8,128)S(1)}, u32[]{:S(2)}, u32[]{:S(2)}) collective-permute-start(f32[3,18,8,128]{3,2,1,0:T(8,128)S(1)} %get-tuple-element.18), channel_id=1, source_target_pairs={{0,112},{16,32},{32,16},{48,64},{64,48},{80,96},{96,80},{112,0},{1... | collective-permute-start | bytes 663560 | tf_op jit(solution)/shard_map/ppermute | solution.py:53
  19.0 0.0 collective-permute-done.1.y_near_ref
  19.1 0.0 collective-permute-done.2.y_far_ref
  19.1 0.0 all-to-all-done
  19.1 0.3 shard_map.39
  19.4 2.4 %collective-permute-start.5 = (f32[27,8,128]{2,1,0:T(8,128)S(1)}, f32[27,8,128]{2,1,0:T(8,128)S(1)}, u32[]{:S(2)}, u32[]{:S(2)}) collective-permute-start(f32[27,8,128]{2,1,0:T(8,128)S(1)} %get-tuple-element.30), channel_id=1, source_target_pairs={{0,16},{16,0},{32,48},{48,32},{64,80},{80,64},{96,112},{112,96},{1... | collective-permute-start | bytes 331784 | tf_op jit(solution)/shard_map/ppermute | solution.py:48
  21.8 3.7 %collective-permute-start.3 = (f32[27,8,128]{2,1,0:T(8,128)S(1)}, f32[27,8,128]{2,1,0:T(8,128)S(1)}, u32[]{:S(2)}, u32[]{:S(2)}) collective-permute-start(f32[27,8,128]{2,1,0:T(8,128)S(1)} %get-tuple-element.21), channel_id=1, source_target_pairs={{0,112},{16,32},{32,16},{48,64},{64,48},{80,96},{96,80},{112,0},{1... | collective-permute-start | bytes 331784 | tf_op jit(solution)/shard_map/ppermute | solution.py:53
  25.5 5.9 %shard_map.40 = (f32[9,2,3,12,8,128]{5,4,3,2,1,0:T(8,128)S(1)}, f32[3,28,8,128]{3,2,1,0:T(8,128)S(1)}, f32[2,3,32,8,128]{4,3,2,1,0:T(8,128)S(1)}, bf16[128,512]{...) custom-call(f32[32,2,8,128]{3,2,1,0:T(8,128)S(1)} %bitcast.4, ...), custom_call_target="tpu_custom_call" | custom-call | bytes 18000000 | tf_op jit(solution)/shard_map/pallas_call | solution.py:498
  31.4 0.0 collective-permute-done.4.main_ref
  31.4 0.9 %collective-permute-done.5.message_ref = f32[27,8,128]{2,1,0:T(8,128)S(1)} collective-permute-done((f32[27,8,128]{2,1,0:T(8,128)S(1)}, f32[27,8,128]{2,1,0:T(8,128)S(1)}, u32[]{:S(2)}, u32[]{:S(2)}) %collective-permute-start.5) | collective-permute-done | bytes 110624 | tf_op jit(solution)/shard_map/ppermute | solution.py:48
  32.3 4.9 %shard_map.41.before_ref = f32[24,64,128]{2,1,0:T(8,128)} custom-call(f32[3,18,8,128]{3,2,1,0:T(8,128)S(1)} %collective-permute-done.4.main_ref, f32[27,8,128]{2,1,0:T(8,128)S(1)} %collective-permute-done.5.message_ref, f32[9,2,3,12,8,128]{5,4,3,2,1,0:T(8,128)S(1)} %get-tuple-element.23.edges_ref, f32[2,3,32,8,128]{4,3,2,1,0:T(8,128)S(1)} %get-tuple-element.24.refined_ref, ...), custom_call_target="tpu_custom_call" | custom-call | bytes 9000000 | tf_op jit(solution)/shard_map/pallas_call | solution.py:498
  37.2 0.0 collective-permute-done.main_ref
  37.2 0.3 collective-permute-done.3.message_ref
  37.5 4.6 %shard_map.42 = f32[24,64,128]{2,1,0:T(8,128)} custom-call(f32[3,18,8,128]{3,2,1,0:T(8,128)S(1)} %collective-permute-done.main_ref, f32[27,8,128]{2,1,0:T(8,128)S(1)} %collective-permute-done.3.message_ref, f32[9,2,3,12,8,128]{5,4,3,2,1,0:T(8,128)S(1)} %get-tuple-element.23.edges_ref, ...), custom_call_target="tpu_custom_call", output_to_operand_aliasing={{}: (8, {})} | custom-call | bytes 9000000 | tf_op jit(solution)/shard_map/pallas_call | solution.py:498
Async XLA Ops:
  1.9 17.1 %all-to-all-start = ((f32[16,2,2,8,128]{4,3,2,1,0:T(8,128)}), f32[16,2,2,8,128]{4,3,2,1,0:T(8,128)S(1)}, u32[]{:S(2)}, u32[]{:S(2)}) async-start(f32[16,2,2,8,128]{4,3,2,1,0:T(8,128)} %shard_map.38), calls=%async_computation | async-start | bytes 524288 | tf_op jit(solution)/shard_map/all_to_all | solution.py:533
  8.8 1.1 %copy-start = (f32[3,8,64,128]{3,2,1,0:T(8,128)S(1)}, f32[3,8,64,128]{3,2,1,0:T(8,128)}, u32[]{:S(2)}) copy-start(f32[3,8,64,128]{3,2,1,0:T(8,128)} %param.5) | copy-start | bytes 2359300
  10.7 8.3 %collective-permute-start.1 = (f32[3,10,8,128]{3,2,1,0:T(8,128)S(1)}, f32[3,10,8,128]{3,2,1,0:T(8,128)S(1)}, u32[]{:S(2)}, u32[]{:S(2)}) collective-permute-start(f32[3,10,8,128]{3,2,1,0:T(8,128)S(1)} %get-tuple-element.19), channel_id=1, source_target_pairs={{0,1},{1,0},{2,3},{3,2},{4,5},{5,4},{6,7},{7,6},{8,9},{9,8},{10,11... | collective-permute-start | bytes 368648 | tf_op jit(solution)/shard_map/ppermute | solution.py:48
  10.9 8.1 %collective-permute-start.2 = (f32[3,10,8,128]{3,2,1,0:T(8,128)S(1)}, f32[3,10,8,128]{3,2,1,0:T(8,128)S(1)}, u32[]{:S(2)}, u32[]{:S(2)}) collective-permute-start(f32[3,10,8,128]{3,2,1,0:T(8,128)S(1)} %get-tuple-element.20), channel_id=1, source_target_pairs={{0,15},{1,2},{2,1},{3,4},{4,3},{5,6},{6,5},{7,8},{8,7},{9,10},{10,... | collective-permute-start | bytes 368648 | tf_op jit(solution)/shard_map/ppermute | solution.py:53
  12.6 18.8 %collective-permute-start.4 = (f32[3,18,8,128]{3,2,1,0:T(8,128)S(1)}, f32[3,18,8,128]{3,2,1,0:T(8,128)S(1)}, u32[]{:S(2)}, u32[]{:S(2)}) collective-permute-start(f32[3,18,8,128]{3,2,1,0:T(8,128)S(1)} %get-tuple-element.29), channel_id=1, source_target_pairs={{0,16},{16,0},{32,48},{48,32},{64,80},{80,64},{96,112},{112,96},{1... | collective-permute-start | bytes 663560 | tf_op jit(solution)/shard_map/ppermute | solution.py:48
  15.2 22.0 %collective-permute-start = (f32[3,18,8,128]{3,2,1,0:T(8,128)S(1)}, f32[3,18,8,128]{3,2,1,0:T(8,128)S(1)}, u32[]{:S(2)}, u32[]{:S(2)}) collective-permute-start(f32[3,18,8,128]{3,2,1,0:T(8,128)S(1)} %get-tuple-element.18), channel_id=1, source_target_pairs={{0,112},{16,32},{32,16},{48,64},{64,48},{80,96},{96,80},{112,0},{1... | collective-permute-start | bytes 663560 | tf_op jit(solution)/shard_map/ppermute | solution.py:53
  19.4 12.9 %collective-permute-start.5 = (f32[27,8,128]{2,1,0:T(8,128)S(1)}, f32[27,8,128]{2,1,0:T(8,128)S(1)}, u32[]{:S(2)}, u32[]{:S(2)}) collective-permute-start(f32[27,8,128]{2,1,0:T(8,128)S(1)} %get-tuple-element.30), channel_id=1, source_target_pairs={{0,16},{16,0},{32,48},{48,32},{64,80},{80,64},{96,112},{112,96},{1... | collective-permute-start | bytes 331784 | tf_op jit(solution)/shard_map/ppermute | solution.py:48
  21.8 15.8 %collective-permute-start.3 = (f32[27,8,128]{2,1,0:T(8,128)S(1)}, f32[27,8,128]{2,1,0:T(8,128)S(1)}, u32[]{:S(2)}, u32[]{:S(2)}) collective-permute-start(f32[27,8,128]{2,1,0:T(8,128)S(1)} %get-tuple-element.21), channel_id=1, source_target_pairs={{0,112},{16,32},{32,16},{48,64},{64,48},{80,96},{96,80},{112,0},{1... | collective-permute-start | bytes 331784 | tf_op jit(solution)/shard_map/ppermute | solution.py:53

commit v7 on v5

--- a/solution.py
+++ b/solution.py
@@ -342,23 +342,6 @@
     side, main_ref, message_ref, edges_ref, refined_ref, refined, background, state, first, second
 ):
     lane = lanes()
-    east_table, north_table, table = refine_table(0), refine_table(1), difference_table()
-    own = MARGIN + HROWS
-    for k in range(2):
-        for f in range(3):
-            refined[k, f, pl.ds((1 - side) * HROWS, MARGIN)] = refined_ref[
-                k, f, pl.ds(side * (CROWS - MARGIN), MARGIN)
-            ]
-
-    def keep(k, f, values):
-        refined[k, f, pl.ds(side * MARGIN, HROWS)] = values[:HROWS]
-
-    values = message_ref[: 2 * HROWS + 2].reshape(HROWS + 1, 2, LEVELS, COLS)
-    refine_columns(values, east_table, north_table, keep)
-    for k in range(2):
-        for f in range(3):
-            refine_rows(refined, k, f, 0, own, background, 0)
-
     halo = side * (REACH + HAND)
     for f in range(3):
         state[0, f, pl.ds(halo, REACH)] = main_ref[f]
@@ -370,6 +353,23 @@
                 corner = message_ref[2 * HROWS + CREGS * f + register]
                 sides.append(roll(corner, (RIM - REACH) * right - start - offset))
             state[1, f, halo + row] = rim_of(main_ref[f, row], sides[0], sides[1], lane)
+
+    east_table, north_table, table = refine_table(0), refine_table(1), difference_table()
+    own = MARGIN + HROWS
+    for k in range(2):
+        for f in range(3):
+            refined[k, f, pl.ds((1 - side) * HROWS, MARGIN)] = refined_ref[
+                k, f, pl.ds(side * (CROWS - MARGIN), MARGIN)
+            ]
+
+    def keep(k, f, values):
+        refined[k, f, pl.ds(side * MARGIN, HROWS)] = values[:HROWS]
+
+    values = message_ref[: 2 * HROWS + 2].reshape(HROWS + 1, 2, LEVELS, COLS)
+    refine_columns(values, east_table, north_table, keep)
+    for k in range(2):
+        for f in range(3):
+            refine_rows(refined, k, f, 0, own, background, 0)
 
     buffers = (state, first, second, state)
 

time: 42.5 us -> 42.5 us (level)
  no operation moved by 1% of the time
where the time goes in v7:
time: 42.5 us; the launch traced here: 42.3 us
  starting transfers between devices  21.3 us (50%)
  Pallas kernels  18.5 us (44%)
  local copies, waits for them, and re-layouts  1.13 us (3%)
  waiting for transfers between devices  1.11 us (3%)
    pallas_call x6, Pallas kernels, run(): pl.pallas_call(kernel, out_shape=[jax.ShapeDtypeStruct(shape, F32) for sh...  18.5 us
    ppermute x3, starting transfers between devices, swap_far(): lax.ppermute(values, axis, [(i, (i + 1) % count if i % 2 else (i - 1) % c...  9.25 us
    all_to_all x1, starting transfers between devices, local(): lax.all_to_all(packed, 'gy', split_axis=0, concat_axis=0, tiled=True)  6.84 us
    ppermute x3, starting transfers between devices, swap_near(): lax.ppermute(values, axis, [(i, i ^ 1) for i in range(lax.axis_size(axis))])  5.18 us
    unnamed x2, local copies, waits for them, and re-layouts  1.13 us
  transfers between devices with their start and end apart: 7, of which 2 were waited for; matrix products, arithmetic and copies ran while one was open for 0% of the time, Pallas kernels for 28%

profile of v7, /device:TPU:1, one launch (start us, length us, event | category | flops | bytes accessed | tf_op | source)
XLA Modules:
  0.0 42.3 jit_solution(17532119999735591754)
XLA Ops:
  0.0 1.9 %shard_map.38 = f32[16,2,2,8,128]{4,3,2,1,0:T(8,128)} custom-call(f32[2,8,2,1024]{3,2,1,0:T(2,128)} %wind_hbm.1, f32[8,2,1024]{2,1,0:T(2,128)} %temp_hbm.1), custom_call_target="tpu_custom_call" | custom-call | bytes 3000000 | tf_op jit(solution)/shard_map/pallas_call | solution.py:494
  1.9 6.8 %all-to-all-start = ((f32[16,2,2,8,128]{4,3,2,1,0:T(8,128)}), f32[16,2,2,8,128]{4,3,2,1,0:T(8,128)S(1)}, u32[]{:S(2)}, u32[]{:S(2)}) async-start(f32[16,2,2,8,128]{4,3,2,1,0:T(8,128)} %shard_map.38), calls=%async_computation | async-start | bytes 524288 | tf_op jit(solution)/shard_map/all_to_all | solution.py:526
  8.8 0.0 copy-start
  8.8 1.1 %copy-done = f32[3,8,64,128]{3,2,1,0:T(8,128)S(1)} copy-done((f32[3,8,64,128]{3,2,1,0:T(8,128)S(1)}, f32[3,8,64,128]{3,2,1,0:T(8,128)}, u32[]{:S(2)}) %copy-start) | copy-done | bytes 786456
  9.9 0.8 %shard_map.37 = (f32[3,64,8,128]{3,2,1,0:T(8,128)S(1)}, f32[3,18,8,128]{3,2,1,0:T(8,128)S(1)}, f32[3,18,8,128]{3,2,1,0:T(8,128)S(1)}, f32[3,10,8,128]{3,2,1,0:T(8,128)S(1)}, f32[3,10,8,128]{3,2,1,0:T(8,128)S(1)}) custom-call(f32[1536,128]{1,0:T(8,128)S(1)} %bitcast.5), custom_call_target="tpu_custom_call" | custom-call | bytes 3000000 | tf_op jit(solution)/shard_map/pallas_call | solution.py:494
  10.7 0.2 collective-permute-start.1
  10.9 1.7 %collective-permute-start.2 = (f32[3,10,8,128]{3,2,1,0:T(8,128)S(1)}, f32[3,10,8,128]{3,2,1,0:T(8,128)S(1)}, u32[]{:S(2)}, u32[]{:S(2)}) collective-permute-start(f32[3,10,8,128]{3,2,1,0:T(8,128)S(1)} %get-tuple-element.17), channel_id=1, source_target_pairs={{0,15},{1,2},{2,1},{3,4},{4,3},{5,6},{6,5},{7,8},{8,7},{9,10},{10,... | collective-permute-start | bytes 368648 | tf_op jit(solution)/shard_map/ppermute | solution.py:53
  12.6 2.6 %collective-permute-start.4 = (f32[3,18,8,128]{3,2,1,0:T(8,128)S(1)}, f32[3,18,8,128]{3,2,1,0:T(8,128)S(1)}, u32[]{:S(2)}, u32[]{:S(2)}) collective-permute-start(f32[3,18,8,128]{3,2,1,0:T(8,128)S(1)} %get-tuple-element.23), channel_id=1, source_target_pairs={{0,16},{16,0},{32,48},{48,32},{64,80},{80,64},{96,112},{112,96},{1... | collective-permute-start | bytes 663560 | tf_op jit(solution)/shard_map/ppermute | solution.py:48
  15.2 3.8 %collective-permute-start = (f32[3,18,8,128]{3,2,1,0:T(8,128)S(1)}, f32[3,18,8,128]{3,2,1,0:T(8,128)S(1)}, u32[]{:S(2)}, u32[]{:S(2)}) collective-permute-start(f32[3,18,8,128]{3,2,1,0:T(8,128)S(1)} %get-tuple-element.15), channel_id=1, source_target_pairs={{0,112},{16,32},{32,16},{48,64},{64,48},{80,96},{96,80},{112,0},{1... | collective-permute-start | bytes 663560 | tf_op jit(solution)/shard_map/ppermute | solution.py:53
  19.1 0.0 collective-permute-done.1.y_near_ref
  19.1 0.0 collective-permute-done.2.y_far_ref
  19.1 0.0 all-to-all-done
  19.1 0.3 shard_map.39
  19.4 2.4 %collective-permute-start.5 = (f32[27,8,128]{2,1,0:T(8,128)S(1)}, f32[27,8,128]{2,1,0:T(8,128)S(1)}, u32[]{:S(2)}, u32[]{:S(2)}) collective-permute-start(f32[27,8,128]{2,1,0:T(8,128)S(1)} %get-tuple-element.24), channel_id=1, source_target_pairs={{0,16},{16,0},{32,48},{48,32},{64,80},{80,64},{96,112},{112,96},{1... | collective-permute-start | bytes 331784 | tf_op jit(solution)/shard_map/ppermute | solution.py:48
  21.8 3.7 %collective-permute-start.3 = (f32[27,8,128]{2,1,0:T(8,128)S(1)}, f32[27,8,128]{2,1,0:T(8,128)S(1)}, u32[]{:S(2)}, u32[]{:S(2)}) collective-permute-start(f32[27,8,128]{2,1,0:T(8,128)S(1)} %get-tuple-element.18), channel_id=1, source_target_pairs={{0,112},{16,32},{32,16},{48,64},{64,48},{80,96},{96,80},{112,0},{1... | collective-permute-start | bytes 331784 | tf_op jit(solution)/shard_map/ppermute | solution.py:53
  25.5 6.0 %shard_map.40 = (f32[9,2,3,12,8,128]{5,4,3,2,1,0:T(8,128)S(1)}, f32[3,28,8,128]{3,2,1,0:T(8,128)S(1)}, f32[2,3,32,8,128]{4,3,2,1,0:T(8,128)S(1)}) custom-call(f32[32,2,8,128]{3,2,1,0:T(8,128)S(1)} %bitcast.4, f32[3,64,8,128]{3,2,1,0:T(8,128)S(1)} %get-tuple-element.19.tile_ref, f32[3,10,8,128]{3,2,1,0:T(8,128)S(1)} %collective-permute-done.1.y_near_ref, ...), custom_call_target="tpu_custom_call" | custom-call | bytes 18000000 | tf_op jit(solution)/shard_map/pallas_call | solution.py:494
  31.5 0.0 collective-permute-done.4.main_ref
  31.5 0.8 %collective-permute-done.5.message_ref = f32[27,8,128]{2,1,0:T(8,128)S(1)} collective-permute-done((f32[27,8,128]{2,1,0:T(8,128)S(1)}, f32[27,8,128]{2,1,0:T(8,128)S(1)}, u32[]{:S(2)}, u32[]{:S(2)}) %collective-permute-start.5) | collective-permute-done | bytes 110624 | tf_op jit(solution)/shard_map/ppermute | solution.py:48
  32.3 4.9 %shard_map.41.before_ref = f32[24,64,128]{2,1,0:T(8,128)} custom-call(f32[3,18,8,128]{3,2,1,0:T(8,128)S(1)} %collective-permute-done.4.main_ref, f32[27,8,128]{2,1,0:T(8,128)S(1)} %collective-permute-done.5.message_ref, f32[9,2,3,12,8,128]{5,4,3,2,1,0:T(8,128)S(1)} %get-tuple-element.20.edges_ref, f32[2,3,32,8,128]{4,3,2,1,0:T(8,128)S(1)} %get-tuple-element.21.refined_ref, ...), custom_call_target="tpu_custom_call" | custom-call | bytes 9000000 | tf_op jit(solution)/shard_map/pallas_call | solution.py:494
  37.2 0.0 collective-permute-done.main_ref
  37.2 0.3 collective-permute-done.3.message_ref
  37.5 4.5 %shard_map.42 = f32[24,64,128]{2,1,0:T(8,128)} custom-call(f32[3,18,8,128]{3,2,1,0:T(8,128)S(1)} %collective-permute-done.main_ref, f32[27,8,128]{2,1,0:T(8,128)S(1)} %collective-permute-done.3.message_ref, f32[9,2,3,12,8,128]{5,4,3,2,1,0:T(8,128)S(1)} %get-tuple-element.20.edges_ref, ...), custom_call_target="tpu_custom_call", output_to_operand_aliasing={{}: (5, {})} | custom-call | bytes 9000000 | tf_op jit(solution)/shard_map/pallas_call | solution.py:494
Async XLA Ops:
  1.9 17.1 %all-to-all-start = ((f32[16,2,2,8,128]{4,3,2,1,0:T(8,128)}), f32[16,2,2,8,128]{4,3,2,1,0:T(8,128)S(1)}, u32[]{:S(2)}, u32[]{:S(2)}) async-start(f32[16,2,2,8,128]{4,3,2,1,0:T(8,128)} %shard_map.38), calls=%async_computation | async-start | bytes 524288 | tf_op jit(solution)/shard_map/all_to_all | solution.py:526
  8.8 1.1 %copy-start = (f32[3,8,64,128]{3,2,1,0:T(8,128)S(1)}, f32[3,8,64,128]{3,2,1,0:T(8,128)}, u32[]{:S(2)}) copy-start(f32[3,8,64,128]{3,2,1,0:T(8,128)} %param.5) | copy-start | bytes 2359300
  10.7 8.3 %collective-permute-start.1 = (f32[3,10,8,128]{3,2,1,0:T(8,128)S(1)}, f32[3,10,8,128]{3,2,1,0:T(8,128)S(1)}, u32[]{:S(2)}, u32[]{:S(2)}) collective-permute-start(f32[3,10,8,128]{3,2,1,0:T(8,128)S(1)} %get-tuple-element.16), channel_id=1, source_target_pairs={{0,1},{1,0},{2,3},{3,2},{4,5},{5,4},{6,7},{7,6},{8,9},{9,8},{10,11... | collective-permute-start | bytes 368648 | tf_op jit(solution)/shard_map/ppermute | solution.py:48
  10.9 8.1 %collective-permute-start.2 = (f32[3,10,8,128]{3,2,1,0:T(8,128)S(1)}, f32[3,10,8,128]{3,2,1,0:T(8,128)S(1)}, u32[]{:S(2)}, u32[]{:S(2)}) collective-permute-start(f32[3,10,8,128]{3,2,1,0:T(8,128)S(1)} %get-tuple-element.17), channel_id=1, source_target_pairs={{0,15},{1,2},{2,1},{3,4},{4,3},{5,6},{6,5},{7,8},{8,7},{9,10},{10,... | collective-permute-start | bytes 368648 | tf_op jit(solution)/shard_map/ppermute | solution.py:53
  12.6 18.9 %collective-permute-start.4 = (f32[3,18,8,128]{3,2,1,0:T(8,128)S(1)}, f32[3,18,8,128]{3,2,1,0:T(8,128)S(1)}, u32[]{:S(2)}, u32[]{:S(2)}) collective-permute-start(f32[3,18,8,128]{3,2,1,0:T(8,128)S(1)} %get-tuple-element.23), channel_id=1, source_target_pairs={{0,16},{16,0},{32,48},{48,32},{64,80},{80,64},{96,112},{112,96},{1... | collective-permute-start | bytes 663560 | tf_op jit(solution)/shard_map/ppermute | solution.py:48
  15.2 22.0 %collective-permute-start = (f32[3,18,8,128]{3,2,1,0:T(8,128)S(1)}, f32[3,18,8,128]{3,2,1,0:T(8,128)S(1)}, u32[]{:S(2)}, u32[]{:S(2)}) collective-permute-start(f32[3,18,8,128]{3,2,1,0:T(8,128)S(1)} %get-tuple-element.15), channel_id=1, source_target_pairs={{0,112},{16,32},{32,16},{48,64},{64,48},{80,96},{96,80},{112,0},{1... | collective-permute-start | bytes 663560 | tf_op jit(solution)/shard_map/ppermute | solution.py:53
  19.4 12.9 %collective-permute-start.5 = (f32[27,8,128]{2,1,0:T(8,128)S(1)}, f32[27,8,128]{2,1,0:T(8,128)S(1)}, u32[]{:S(2)}, u32[]{:S(2)}) collective-permute-start(f32[27,8,128]{2,1,0:T(8,128)S(1)} %get-tuple-element.24), channel_id=1, source_target_pairs={{0,16},{16,0},{32,48},{48,32},{64,80},{80,64},{96,112},{112,96},{1... | collective-permute-start | bytes 331784 | tf_op jit(solution)/shard_map/ppermute | solution.py:48
  21.8 15.8 %collective-permute-start.3 = (f32[27,8,128]{2,1,0:T(8,128)S(1)}, f32[27,8,128]{2,1,0:T(8,128)S(1)}, u32[]{:S(2)}, u32[]{:S(2)}) collective-permute-start(f32[27,8,128]{2,1,0:T(8,128)S(1)} %get-tuple-element.18), channel_id=1, source_target_pairs={{0,112},{16,32},{32,16},{48,64},{64,48},{80,96},{96,80},{112,0},{1... | collective-permute-start | bytes 331784 | tf_op jit(solution)/shard_map/ppermute | solution.py:53

commit v8 on v5

--- a/solution.py
+++ b/solution.py
@@ -26,7 +26,7 @@
 CREGS = -(-2 * PAIRS // PER)
 OWN = -(-REACH // 8) * 8
 HAND = 6
-CHUNK = 16
+CHUNK = 8
 PACK_LIMIT = 57
 SIDE = EDGE + MIDDLE
 

time: 42.5 us -> 42.5 us (level)
  transfers between devices with their start and end apart: 7 -> 7, of which waited for: 2 -> 2; matrix products, arithmetic and copies ran while one was open for 0% -> 0% of each run, Pallas kernels for 28% -> 29%
where the time goes in v8:
time: 42.5 us; the launch traced here: 42.3 us
  starting transfers between devices  21.3 us (50%)
  Pallas kernels  18.6 us (44%)
  local copies, waits for them, and re-layouts  1.13 us (3%)
  waiting for transfers between devices  1.01 us (2%)
    pallas_call x6, Pallas kernels, run(): pl.pallas_call(kernel, out_shape=[jax.ShapeDtypeStruct(shape, F32) for sh...  18.6 us
    ppermute x3, starting transfers between devices, swap_far(): lax.ppermute(values, axis, [(i, (i + 1) % count if i % 2 else (i - 1) % c...  9.25 us
    all_to_all x1, starting transfers between devices, local(): lax.all_to_all(packed, 'gy', split_axis=0, concat_axis=0, tiled=True)  6.84 us
    ppermute x3, starting transfers between devices, swap_near(): lax.ppermute(values, axis, [(i, i ^ 1) for i in range(lax.axis_size(axis))])  5.18 us
    unnamed x2, local copies, waits for them, and re-layouts  1.13 us
  transfers between devices with their start and end apart: 7, of which 2 were waited for; matrix products, arithmetic and copies ran while one was open for 0% of the time, Pallas kernels for 29%

profile of v8, /device:TPU:1, one launch (start us, length us, event | category | flops | bytes accessed | tf_op | source)
XLA Modules:
  0.0 42.3 jit_solution(333860969271921577)
XLA Ops:
  0.0 1.9 %shard_map.38 = f32[16,2,2,8,128]{4,3,2,1,0:T(8,128)} custom-call(f32[2,8,2,1024]{3,2,1,0:T(2,128)} %wind_hbm.1, f32[8,2,1024]{2,1,0:T(2,128)} %temp_hbm.1), custom_call_target="tpu_custom_call" | custom-call | bytes 3000000 | tf_op jit(solution)/shard_map/pallas_call | solution.py:494
  1.9 6.8 %all-to-all-start = ((f32[16,2,2,8,128]{4,3,2,1,0:T(8,128)}), f32[16,2,2,8,128]{4,3,2,1,0:T(8,128)S(1)}, u32[]{:S(2)}, u32[]{:S(2)}) async-start(f32[16,2,2,8,128]{4,3,2,1,0:T(8,128)} %shard_map.38), calls=%async_computation | async-start | bytes 524288 | tf_op jit(solution)/shard_map/all_to_all | solution.py:526
  8.8 0.0 copy-start
  8.8 1.1 %copy-done = f32[3,8,64,128]{3,2,1,0:T(8,128)S(1)} copy-done((f32[3,8,64,128]{3,2,1,0:T(8,128)S(1)}, f32[3,8,64,128]{3,2,1,0:T(8,128)}, u32[]{:S(2)}) %copy-start) | copy-done | bytes 786456
  9.9 0.8 %shard_map.37 = (f32[3,64,8,128]{3,2,1,0:T(8,128)S(1)}, f32[3,18,8,128]{3,2,1,0:T(8,128)S(1)}, f32[3,18,8,128]{3,2,1,0:T(8,128)S(1)}, f32[3,10,8,128]{3,2,1,0:T(8,128)S(1)}, f32[3,10,8,128]{3,2,1,0:T(8,128)S(1)}) custom-call(f32[1536,128]{1,0:T(8,128)S(1)} %bitcast.5), custom_call_target="tpu_custom_call" | custom-call | bytes 3000000 | tf_op jit(solution)/shard_map/pallas_call | solution.py:494
  10.7 0.2 collective-permute-start.1
  10.9 1.7 %collective-permute-start.2 = (f32[3,10,8,128]{3,2,1,0:T(8,128)S(1)}, f32[3,10,8,128]{3,2,1,0:T(8,128)S(1)}, u32[]{:S(2)}, u32[]{:S(2)}) collective-permute-start(f32[3,10,8,128]{3,2,1,0:T(8,128)S(1)} %get-tuple-element.17), channel_id=1, source_target_pairs={{0,15},{1,2},{2,1},{3,4},{4,3},{5,6},{6,5},{7,8},{8,7},{9,10},{10,... | collective-permute-start | bytes 368648 | tf_op jit(solution)/shard_map/ppermute | solution.py:53
  12.6 2.6 %collective-permute-start.4 = (f32[3,18,8,128]{3,2,1,0:T(8,128)S(1)}, f32[3,18,8,128]{3,2,1,0:T(8,128)S(1)}, u32[]{:S(2)}, u32[]{:S(2)}) collective-permute-start(f32[3,18,8,128]{3,2,1,0:T(8,128)S(1)} %get-tuple-element.23), channel_id=1, source_target_pairs={{0,16},{16,0},{32,48},{48,32},{64,80},{80,64},{96,112},{112,96},{1... | collective-permute-start | bytes 663560 | tf_op jit(solution)/shard_map/ppermute | solution.py:48
  15.2 3.8 %collective-permute-start = (f32[3,18,8,128]{3,2,1,0:T(8,128)S(1)}, f32[3,18,8,128]{3,2,1,0:T(8,128)S(1)}, u32[]{:S(2)}, u32[]{:S(2)}) collective-permute-start(f32[3,18,8,128]{3,2,1,0:T(8,128)S(1)} %get-tuple-element.15), channel_id=1, source_target_pairs={{0,112},{16,32},{32,16},{48,64},{64,48},{80,96},{96,80},{112,0},{1... | collective-permute-start | bytes 663560 | tf_op jit(solution)/shard_map/ppermute | solution.py:53
  19.1 0.0 collective-permute-done.1.y_near_ref
  19.1 0.0 collective-permute-done.2.y_far_ref
  19.1 0.0 all-to-all-done
  19.1 0.3 shard_map.39
  19.4 2.4 %collective-permute-start.5 = (f32[27,8,128]{2,1,0:T(8,128)S(1)}, f32[27,8,128]{2,1,0:T(8,128)S(1)}, u32[]{:S(2)}, u32[]{:S(2)}) collective-permute-start(f32[27,8,128]{2,1,0:T(8,128)S(1)} %get-tuple-element.24), channel_id=1, source_target_pairs={{0,16},{16,0},{32,48},{48,32},{64,80},{80,64},{96,112},{112,96},{1... | collective-permute-start | bytes 331784 | tf_op jit(solution)/shard_map/ppermute | solution.py:48
  21.8 3.7 %collective-permute-start.3 = (f32[27,8,128]{2,1,0:T(8,128)S(1)}, f32[27,8,128]{2,1,0:T(8,128)S(1)}, u32[]{:S(2)}, u32[]{:S(2)}) collective-permute-start(f32[27,8,128]{2,1,0:T(8,128)S(1)} %get-tuple-element.18), channel_id=1, source_target_pairs={{0,112},{16,32},{32,16},{48,64},{64,48},{80,96},{96,80},{112,0},{1... | collective-permute-start | bytes 331784 | tf_op jit(solution)/shard_map/ppermute | solution.py:53
  25.5 6.1 %shard_map.40 = (f32[9,2,3,12,8,128]{5,4,3,2,1,0:T(8,128)S(1)}, f32[3,28,8,128]{3,2,1,0:T(8,128)S(1)}, f32[2,3,32,8,128]{4,3,2,1,0:T(8,128)S(1)}) custom-call(f32[32,2,8,128]{3,2,1,0:T(8,128)S(1)} %bitcast.4, f32[3,64,8,128]{3,2,1,0:T(8,128)S(1)} %get-tuple-element.19.tile_ref, f32[3,10,8,128]{3,2,1,0:T(8,128)S(1)} %collective-permute-done.1.y_near_ref, ...), custom_call_target="tpu_custom_call" | custom-call | bytes 18000000 | tf_op jit(solution)/shard_map/pallas_call | solution.py:494
  31.6 0.0 collective-permute-done.4.main_ref
  31.6 0.7 %collective-permute-done.5.message_ref = f32[27,8,128]{2,1,0:T(8,128)S(1)} collective-permute-done((f32[27,8,128]{2,1,0:T(8,128)S(1)}, f32[27,8,128]{2,1,0:T(8,128)S(1)}, u32[]{:S(2)}, u32[]{:S(2)}) %collective-permute-start.5) | collective-permute-done | bytes 110624 | tf_op jit(solution)/shard_map/ppermute | solution.py:48
  32.3 4.9 %shard_map.41.before_ref = f32[24,64,128]{2,1,0:T(8,128)} custom-call(f32[3,18,8,128]{3,2,1,0:T(8,128)S(1)} %collective-permute-done.4.main_ref, f32[27,8,128]{2,1,0:T(8,128)S(1)} %collective-permute-done.5.message_ref, f32[9,2,3,12,8,128]{5,4,3,2,1,0:T(8,128)S(1)} %get-tuple-element.20.edges_ref, f32[2,3,32,8,128]{4,3,2,1,0:T(8,128)S(1)} %get-tuple-element.21.refined_ref, ...), custom_call_target="tpu_custom_call" | custom-call | bytes 9000000 | tf_op jit(solution)/shard_map/pallas_call | solution.py:494
  37.2 0.0 collective-permute-done.main_ref
  37.2 0.3 collective-permute-done.3.message_ref
  37.5 4.5 %shard_map.42 = f32[24,64,128]{2,1,0:T(8,128)} custom-call(f32[3,18,8,128]{3,2,1,0:T(8,128)S(1)} %collective-permute-done.main_ref, f32[27,8,128]{2,1,0:T(8,128)S(1)} %collective-permute-done.3.message_ref, f32[9,2,3,12,8,128]{5,4,3,2,1,0:T(8,128)S(1)} %get-tuple-element.20.edges_ref, ...), custom_call_target="tpu_custom_call", output_to_operand_aliasing={{}: (5, {})} | custom-call | bytes 9000000 | tf_op jit(solution)/shard_map/pallas_call | solution.py:494
Async XLA Ops:
  1.9 17.1 %all-to-all-start = ((f32[16,2,2,8,128]{4,3,2,1,0:T(8,128)}), f32[16,2,2,8,128]{4,3,2,1,0:T(8,128)S(1)}, u32[]{:S(2)}, u32[]{:S(2)}) async-start(f32[16,2,2,8,128]{4,3,2,1,0:T(8,128)} %shard_map.38), calls=%async_computation | async-start | bytes 524288 | tf_op jit(solution)/shard_map/all_to_all | solution.py:526
  8.8 1.1 %copy-start = (f32[3,8,64,128]{3,2,1,0:T(8,128)S(1)}, f32[3,8,64,128]{3,2,1,0:T(8,128)}, u32[]{:S(2)}) copy-start(f32[3,8,64,128]{3,2,1,0:T(8,128)} %param.5) | copy-start | bytes 2359300
  10.7 8.3 %collective-permute-start.1 = (f32[3,10,8,128]{3,2,1,0:T(8,128)S(1)}, f32[3,10,8,128]{3,2,1,0:T(8,128)S(1)}, u32[]{:S(2)}, u32[]{:S(2)}) collective-permute-start(f32[3,10,8,128]{3,2,1,0:T(8,128)S(1)} %get-tuple-element.16), channel_id=1, source_target_pairs={{0,1},{1,0},{2,3},{3,2},{4,5},{5,4},{6,7},{7,6},{8,9},{9,8},{10,11... | collective-permute-start | bytes 368648 | tf_op jit(solution)/shard_map/ppermute | solution.py:48
  10.9 8.1 %collective-permute-start.2 = (f32[3,10,8,128]{3,2,1,0:T(8,128)S(1)}, f32[3,10,8,128]{3,2,1,0:T(8,128)S(1)}, u32[]{:S(2)}, u32[]{:S(2)}) collective-permute-start(f32[3,10,8,128]{3,2,1,0:T(8,128)S(1)} %get-tuple-element.17), channel_id=1, source_target_pairs={{0,15},{1,2},{2,1},{3,4},{4,3},{5,6},{6,5},{7,8},{8,7},{9,10},{10,... | collective-permute-start | bytes 368648 | tf_op jit(solution)/shard_map/ppermute | solution.py:53
  12.6 19.0 %collective-permute-start.4 = (f32[3,18,8,128]{3,2,1,0:T(8,128)S(1)}, f32[3,18,8,128]{3,2,1,0:T(8,128)S(1)}, u32[]{:S(2)}, u32[]{:S(2)}) collective-permute-start(f32[3,18,8,128]{3,2,1,0:T(8,128)S(1)} %get-tuple-element.23), channel_id=1, source_target_pairs={{0,16},{16,0},{32,48},{48,32},{64,80},{80,64},{96,112},{112,96},{1... | collective-permute-start | bytes 663560 | tf_op jit(solution)/shard_map/ppermute | solution.py:48
  15.2 22.0 %collective-permute-start = (f32[3,18,8,128]{3,2,1,0:T(8,128)S(1)}, f32[3,18,8,128]{3,2,1,0:T(8,128)S(1)}, u32[]{:S(2)}, u32[]{:S(2)}) collective-permute-start(f32[3,18,8,128]{3,2,1,0:T(8,128)S(1)} %get-tuple-element.15), channel_id=1, source_target_pairs={{0,112},{16,32},{32,16},{48,64},{64,48},{80,96},{96,80},{112,0},{1... | collective-permute-start | bytes 663560 | tf_op jit(solution)/shard_map/ppermute | solution.py:53
  19.4 12.9 %collective-permute-start.5 = (f32[27,8,128]{2,1,0:T(8,128)S(1)}, f32[27,8,128]{2,1,0:T(8,128)S(1)}, u32[]{:S(2)}, u32[]{:S(2)}) collective-permute-start(f32[27,8,128]{2,1,0:T(8,128)S(1)} %get-tuple-element.24), channel_id=1, source_target_pairs={{0,16},{16,0},{32,48},{48,32},{64,80},{80,64},{96,112},{112,96},{1... | collective-permute-start | bytes 331784 | tf_op jit(solution)/shard_map/ppermute | solution.py:48
  21.8 15.8 %collective-permute-start.3 = (f32[27,8,128]{2,1,0:T(8,128)S(1)}, f32[27,8,128]{2,1,0:T(8,128)S(1)}, u32[]{:S(2)}, u32[]{:S(2)}) collective-permute-start(f32[27,8,128]{2,1,0:T(8,128)S(1)} %get-tuple-element.18), channel_id=1, source_target_pairs={{0,112},{16,32},{32,16},{48,64},{64,48},{80,96},{96,80},{112,0},{1... | collective-permute-start | bytes 331784 | tf_op jit(solution)/shard_map/ppermute | solution.py:53
